TPU v7x, 256 devices: a whole 4x4x8 slice. The times are simulated.
256 devices in a mesh: grp: 64 (over y, x, z_lo), tp: 4 (over z_hi, core).
Axes of the slice: x: 4, y: 4, z: 8 (z_hi: 2, z_lo: 4; z = z_hi * 4 + z_lo), core: 2. Of those that a mesh axis runs over, the one named last changes fastest.
Arguments:
- x_rows: bfloat16 [1024, 7168], P('grp'), may hold values from -6 to 6
- route_ids: int32 [1024, 2], P('grp'), may hold values from 0 to 7, all different within a row; in each aligned block of 16 rows (0 to 15, 16 to 31, ...) at most 5 rows name the same one
- router: float32 [7168, 8], replicated, may hold values from -0.0625 to 0.0625
- w_gate: bfloat16 [7168, 40960], P(None, ('grp', 'tp')), may hold values from -0.0625 to 0.0625
- w_up: bfloat16 [7168, 40960], P(None, ('grp', 'tp')), may hold values from -0.0625 to 0.0625
- w_down: bfloat16 [40960, 7168], P(('grp', 'tp')), may hold values from -0.078125 to 0.078125
- queries: bfloat16 [1024, 16384], P(('grp', 'tp')), may hold values from -90 to 90
- cache: bfloat16 [1024, 1024, 512], P(('grp', 'tp')), may hold values from -5 to 5
- lengths: int32 [1024], P(('grp', 'tp')), may hold values from 2 to 1024, as said below
Outputs:
- moe_out: bfloat16 [1024, 7168], P('grp', 'tp')
- attn_out: bfloat16 [1024, 16384], P(('grp', 'tp'))
Inputs may be any that keep to these rules, and one draw needn't show every extreme that they name: `route_ids`: in each aligned block of 16 rows (the rows of one index of grp) no expert is named by more than 5 rows, and some block has an expert named by exactly 5 rows; the ids of a row differ. `lengths`: some request has all 1024 positions live.
All inputs are finite; a program needn't handle non-finite values.
Results may differ from a plain program's by a relative error of at most 0.005.
Values may be sent and summed in bfloat16 or wider, within the bound.
No kernel may reach another device: no remote copies, remote signals or barrier semaphores. Data moves between devices by JAX's collectives and lax.ppermute only.
A program may use at most 128 MiB of HBM per device.

v0:
```python
import math

import jax
import jax.numpy as jnp
from jax import lax
from jax.sharding import PartitionSpec as P

CAP = 5


def attention_block(queries, cache, lengths):
    head_dim = cache.shape[2] // 2
    head_count = queries.shape[1] // head_dim
    requests = queries.shape[0]
    position_count = cache.shape[1]
    query_heads = queries.reshape(requests, head_count, head_dim)
    key_block = cache[:, :, :head_dim]
    value_block = cache[:, :, head_dim:]
    scores = jnp.einsum(
        "bhd,bpd->bhp", query_heads, key_block, preferred_element_type=jnp.float32
    ) / math.sqrt(head_dim)
    live = jnp.arange(position_count)[None, :] < lengths[:, None]
    scores = jnp.where(live[:, None, :], scores, -1e30)
    largest = jnp.max(scores, axis=2, keepdims=True)
    weights = jnp.where(live[:, None, :], jnp.exp(scores - largest), 0.0)
    denominator = jnp.sum(weights, axis=2, keepdims=True)
    mixed = jnp.einsum(
        "bhp,bpd->bhd",
        weights.astype(jnp.bfloat16),
        value_block,
        preferred_element_type=jnp.float32,
    )
    return (mixed / denominator).astype(jnp.bfloat16).reshape(requests, head_count * head_dim)


def shards(x_rows, route_ids, router, w_gate, w_up, w_down, queries, cache, lengths):
    group_count = lax.axis_size("grp")
    tensor_count = lax.axis_size("tp")
    local_rows, model_width = x_rows.shape
    expert_count = router.shape[1]
    picks_per_row = route_ids.shape[1]
    spread = group_count // expert_count
    quarter = model_width // tensor_count
    flat_ids = route_ids.reshape(-1)
    onehot = (flat_ids[:, None] == jnp.arange(expert_count)[None, :]).astype(jnp.int32)
    before = jnp.cumsum(onehot, axis=0) - onehot
    slot_of = jnp.sum(before * onehot, axis=1)
    placed = onehot[:, :, None] * (slot_of[:, None, None] == jnp.arange(CAP)[None, None, :]).astype(
        jnp.int32
    )
    placed = placed.reshape(local_rows, picks_per_row, expert_count, CAP)
    logits = jnp.dot(x_rows.astype(jnp.float32), router, precision=lax.Precision.HIGHEST)
    chosen = jnp.sum(
        onehot.reshape(local_rows, picks_per_row, expert_count).astype(jnp.float32)
        * logits[:, None, :],
        axis=2,
    )
    squashed = jax.nn.sigmoid(chosen)
    gate_share = squashed / jnp.sum(squashed, axis=1, keepdims=True)
    selector = jnp.sum(placed, axis=1).astype(jnp.bfloat16)
    weighting = jnp.sum(placed.astype(jnp.float32) * gate_share[:, :, None, None], axis=1)
    attn_out = attention_block(queries, cache, lengths)
    packed = jnp.einsum("rec,rd->ecd", selector, x_rows, preferred_element_type=jnp.float32).astype(
        jnp.bfloat16
    )
    outgoing = jnp.repeat(packed, spread, axis=0)
    arrived = lax.all_to_all(outgoing, "grp", split_axis=0, concat_axis=0, tiled=True)
    rows_in = arrived.reshape(group_count * CAP, model_width)
    gate_part = jnp.dot(rows_in, w_gate, preferred_element_type=jnp.float32)
    up_part = jnp.dot(rows_in, w_up, preferred_element_type=jnp.float32)
    hidden = (jax.nn.silu(gate_part) * up_part).astype(jnp.bfloat16)
    partial_value = jnp.dot(hidden, w_down, preferred_element_type=jnp.float32).reshape(
        group_count, CAP, model_width
    )
    summed = lax.psum_scatter(partial_value, "tp", scatter_dimension=2, tiled=True)
    returned = lax.all_to_all(summed, "grp", split_axis=0, concat_axis=0, tiled=True)
    per_expert = jnp.sum(returned.reshape(expert_count, spread, CAP, quarter), axis=1)
    moe_out = jnp.einsum("rec,ecd->rd", weighting, per_expert, precision=lax.Precision.HIGHEST)
    return (moe_out.astype(jnp.bfloat16), attn_out)


def solution(mesh):
    placed = (
        P("grp", None),
        P("grp", None),
        P(),
        P(None, ("grp", "tp")),
        P(None, ("grp", "tp")),
        P(("grp", "tp"), None),
        P(("grp", "tp"), None),
        P(("grp", "tp"), None, None),
        P(("grp", "tp")),
    )
    return jax.shard_map(
        shards,
        mesh=mesh,
        in_specs=placed,
        out_specs=(P("grp", "tp"), P(("grp", "tp"), None)),
        check_vma=False,
    )
```

profile of v0, /device:TPU:32, one launch (start us, length us, event | category | flops | bytes accessed | tf_op | source)
XLA Modules:
  0.0 528.7 jit_solution(3248157326172135552)
XLA Ops:
  7.2 0.0 copy-start
  7.2 0.0 reduce-scatter.2.cloned.1.call-start
  7.2 0.9 copy.24
  8.1 0.7 fusion.41
  8.8 0.1 eq.49
  8.9 0.1 fusion.39
  9.0 0.1 reduce_window_sum.11
  9.0 0.2 select_reduce_fusion
  9.2 0.1 eq.53
  9.3 0.1 copy.25
  9.4 1.2 convolution_convert_fusion
  10.7 0.3 copy.26
  11.0 0.9 broadcast_in_dim.20
  11.9 175.0 %all_to_all.10 = bf16[64,5,7168]{2,1,0:T(8,128)(2,1)} all-to-all(bf16[64,5,7168]{2,1,0:T(8,128)(2,1)S(1)} %bitcast.28), channel_id=1, replica_groups=mesh['grp'=64,'tp'=4] {'grp'}, dimensions={0} | all-to-all | bytes 9175040 | tf_op jit(solution)/shard_map/all_to_all | solution.py:67
  186.9 8.2 %reshape.125 = bf16[320,7168]{1,0:T(8,128)(2,1)} reshape(bf16[64,5,7168]{2,1,0:T(8,128)(2,1)} %all_to_all.10) | data formatting | bytes 9175040 | tf_op jit(solution)/shard_map/reshape | solution.py:68
  195.1 4.9 fusion.50
  200.0 0.0 copy-done
  200.0 10.5 %fusion.22 = f32[320,7168]{1,0:T(8,128)} fusion(bf16[160,7168]{1,0:T(8,128)(2,1)S(1)} %copy-done, bf16[320,7168]{1,0:T(8,128)(2,1)} %reshape.125, bf16[7168,160]{0,1:T(8,128)(2,1)} %param.13, f32[320,160]{0,1:T(8,128)S(1)} %fusion.50), kind=kOutput, calls=%fused_computation.18 | convolution fusion | flops 1468313600 | bytes 18554880 | tf_op jit(solution)/shard_map/dot_general | solution.py:72
  210.5 10.6 %reshape.126 = f32[64,5,7168]{2,1,0:T(8,128)} reshape(f32[320,7168]{1,0:T(8,128)} %fusion.22) | data formatting | bytes 18350080 | tf_op jit(solution)/shard_map/reshape | solution.py:72
  221.1 0.0 reduce-scatter.2.cloned.1.call-update
  221.1 0.0 copy-start.4
  221.1 0.0 copy-start.5
  221.1 202.5 %reduce-scatter.2.cloned.1.call-done = f32[64,5,1792]{2,1,0:T(8,128)} async-done(((f32[64,5,7168]{2,1,0:T(8,128)}), f32[64,5,1792]{2,1,0:T(8,128)}) %reduce-scatter.2.cloned.1.call-update) | async-done | bytes 2293776 | tf_op jit(solution)/shard_map/reduce_scatter | solution.py:75
  423.6 10.3 %all-to-all-start.1 = ((f32[64,5,1792]{2,1,0:T(8,128)}), f32[64,5,1792]{2,1,0:T(8,128)}, u32[]{:S(2)}, u32[]{:S(2)}) async-start(f32[64,5,1792]{2,1,0:T(8,128)} %reduce-scatter.2.cloned.1.call-done), calls=%async_computation.2 | async-start | bytes 7340032 | tf_op jit(solution)/shard_map/all_to_all | solution.py:76
  433.9 0.0 copy-done.4
  433.9 0.1 iota_compare_fusion
  433.9 0.0 copy-done.5
  433.9 0.0 copy-start.1
  434.0 0.0 copy-start.2
  434.0 0.0 copy-start.3
  434.0 2.6 fusion.44
  436.6 2.1 fusion.23
  438.7 0.8 copy.29
  439.4 0.0 copy-done.1
  439.4 0.0 copy-done.2
  439.4 0.3 fusion.49
  439.8 0.0 copy-done.3
  439.9 78.7 %all-to-all-done.1 = f32[64,5,1792]{2,1,0:T(8,128)} async-done(((f32[64,5,1792]{2,1,0:T(8,128)}), f32[64,5,1792]{2,1,0:T(8,128)}, u32[]{:S(2)}, u32[]{:S(2)}) %all-to-all-start.1) | async-done | bytes 2293792 | tf_op jit(solution)/shard_map/all_to_all | solution.py:76
  518.6 2.3 bitcast_reduce_fusion
  520.9 1.0 fusion.1
  (6 shorter events, 0.1 us)
Async XLA Ops:
  7.2 192.9 %copy-start = (bf16[160,7168]{1,0:T(8,128)(2,1)S(1)}, bf16[160,7168]{1,0:T(8,128)(2,1)}, u32[]{:S(2)}) copy-start(bf16[160,7168]{1,0:T(8,128)(2,1)} %param.14) | copy-start | bytes 6881284
  7.2 416.4 %reduce-scatter.2.cloned.1.call-start = ((), (), s32[]{:S(2)}) async-start(), calls=%async_computation.3 | async-start | bytes 18350080 | tf_op jit(solution)/shard_map/reduce_scatter | solution.py:75
  221.1 212.8 %copy-start.4 = (s32[4]{0:T(128)S(1)}, s32[4]{0:T(128)}, u32[]{:S(2)}) copy-start(s32[4]{0:T(128)} %param.17) | copy-start | bytes 52
  221.1 212.8 %copy-start.5 = (bf16[4,16384]{1,0:T(4,128)(2,1)S(1)}, bf16[4,16384]{1,0:T(4,128)(2,1)}, u32[]{:S(2)}) copy-start(bf16[4,16384]{1,0:T(4,128)(2,1)} %param.15) | copy-start | bytes 393220
  423.6 95.0 %all-to-all-start.1 = ((f32[64,5,1792]{2,1,0:T(8,128)}), f32[64,5,1792]{2,1,0:T(8,128)}, u32[]{:S(2)}, u32[]{:S(2)}) async-start(f32[64,5,1792]{2,1,0:T(8,128)} %reduce-scatter.2.cloned.1.call-done), calls=%async_computation.2 | async-start | bytes 7340032 | tf_op jit(solution)/shard_map/all_to_all | solution.py:76
  433.9 5.5 %copy-start.1 = (bf16[16,7168]{1,0:T(8,128)(2,1)S(1)}, bf16[16,7168]{1,0:T(8,128)(2,1)}, u32[]{:S(2)}) copy-start(bf16[16,7168]{1,0:T(8,128)(2,1)} %param.9) | copy-start | bytes 688132
  434.0 5.5 %copy-start.2 = (f32[7168,8]{0,1:T(8,128)S(1)}, f32[7168,8]{0,1:T(8,128)}, u32[]{:S(2)}) copy-start(f32[7168,8]{0,1:T(8,128)} %param.11) | copy-start | bytes 688132
  434.0 5.8 %copy-start.3 = (s32[16,2]{0,1:T(2,128)S(1)}, s32[16,2]{0,1:T(2,128)}, u32[]{:S(2)}) copy-start(s32[16,2]{0,1:T(2,128)} %param.10) | copy-start | bytes 388
Sparse Core Ops, SparseCore 0:
  221.2 202.3 reduce-scatter.1
where the time goes:
time: 529 us
  waiting for transfers between devices  281 us (53%)
  blocking collectives  175 us (33%)
  matrix products  22.6 us (4%)
  local copies, waits for them, and re-layouts  22 us (4%)
  between operations  14.2 us (3%)
  starting transfers between devices  10.3 us (2%)
    reduce_scatter x1, waiting for transfers between devices, shards(): lax.psum_scatter(partial_value, 'tp', scatter_dimension=2, tiled=True)  202 us
    all_to_all x1, blocking collectives, shards(): lax.all_to_all(outgoing, 'grp', split_axis=0, concat_axis=0, tiled=True)  175 us
    all_to_all x1, waiting for transfers between devices, shards(): lax.all_to_all(summed, 'grp', split_axis=0, concat_axis=0, tiled=True)  78.7 us
  transfers between devices with their start and end apart: 2, of which 2 were waited for; matrix products, arithmetic and copies ran while one was open for 1% of the time, Pallas kernels for 0%

commit v1 on v0

v1 whole, which is shorter than its diff:
```python
import math

import jax
import jax.numpy as jnp
from jax import lax
from jax.sharding import Mesh
from jax.sharding import PartitionSpec as P

CAP = 5
SLOT = 8
ZLO = 4
ZALL = 8


def attention_block(queries, cache, lengths):
    head_dim = cache.shape[2] // 2
    head_count = queries.shape[1] // head_dim
    requests = queries.shape[0]
    position_count = cache.shape[1]
    query_heads = queries.reshape(requests, head_count, head_dim)
    key_block = cache[:, :, :head_dim]
    value_block = cache[:, :, head_dim:]
    scores = jnp.einsum(
        "bhd,bpd->bhp", query_heads, key_block, preferred_element_type=jnp.float32
    ) / math.sqrt(head_dim)
    live = jnp.arange(position_count)[None, :] < lengths[:, None]
    scores = jnp.where(live[:, None, :], scores, -1e30)
    largest = jnp.max(scores, axis=2, keepdims=True)
    weights = jnp.where(live[:, None, :], jnp.exp(scores - largest), 0.0)
    denominator = jnp.sum(weights, axis=2, keepdims=True)
    mixed = jnp.einsum(
        "bhp,bpd->bhd",
        weights.astype(jnp.bfloat16),
        value_block,
        preferred_element_type=jnp.float32,
    )
    return (mixed / denominator).astype(jnp.bfloat16).reshape(requests, head_count * head_dim)


def place(z):
    return (z % ZLO) * 2 + z // ZLO


UP = [(place(z), place((z + 1) % ZALL)) for z in range(ZALL)]
DOWN = [(place(z), place((z - 1) % ZALL)) for z in range(ZALL)]
SWAP = [(0, 1), (1, 0)]


def to_next(value):
    return lax.ppermute(value, ("zl", "zh"), UP)


def to_last(value):
    return lax.ppermute(value, ("zl", "zh"), DOWN)


def shards(x_rows, route_ids, router, w_gate, w_up, w_down, queries, cache, lengths):
    local_rows, model_width = x_rows.shape
    expert_count = router.shape[1]
    picks = route_ids.shape[1]
    quarter = model_width // 4
    half = model_width // 2
    piece = quarter // 2
    bf16, f32 = jnp.bfloat16, jnp.float32
    x_pos, z_lo, z_hi, core = (lax.axis_index(a) for a in ("xl", "zl", "zh", "c"))
    z_pos = z_hi * ZLO + z_lo

    flat_ids = route_ids.reshape(-1)
    onehot = (flat_ids[:, None] == jnp.arange(expert_count)[None, :]).astype(jnp.int32)
    before = jnp.cumsum(onehot, axis=0) - onehot
    slot_of = jnp.sum(before * onehot, axis=1)
    placed = onehot[:, :, None] * (
        slot_of[:, None, None] == jnp.arange(SLOT)[None, None, :]
    ).astype(jnp.int32)
    placed = placed.reshape(local_rows, picks, expert_count * SLOT)
    selector = jnp.sum(placed, axis=1).astype(bf16)

    x_quarter = lax.dynamic_slice_in_dim(x_rows, (z_hi * 2 + core) * quarter, quarter, 1)
    packed = jnp.einsum("rs,rd->sd", selector, x_quarter, preferred_element_type=f32).astype(bf16)
    arrived = lax.all_to_all(
        packed.reshape(expert_count, SLOT, quarter), ("y", "xh"), 0, 0, tiled=True
    )
    mine = arrived[:, :CAP].reshape(expert_count * CAP, quarter)
    theirs = lax.ppermute(mine, "xl", SWAP)
    first = x_pos == 0
    own = jnp.concatenate(
        [jnp.where(first, mine, theirs), jnp.where(first, theirs, mine)], axis=0
    )
    rows = own.shape[0]

    held = [None] * ZALL
    held[0] = own
    held[1], held[7] = to_last(own), to_next(own)
    held[2], held[6] = to_last(held[1]), to_next(held[7])
    held[3], held[5] = to_last(held[2]), to_next(held[6])
    held[4] = jnp.concatenate(
        [to_last(held[3][:, :piece]), to_next(held[5][:, piece:])], axis=1
    )
    other = [lax.ppermute(block, "c", SWAP) for block in held]
    is_zero = core == 0
    low_first = [(z_pos + k) % ZALL < ZLO for k in range(ZLO)]
    lines = []
    for k in range(ZLO):
        parts = []
        for at in (
            jnp.where(low_first[k], 0, 1),
            jnp.where(low_first[k], 1, 0),
        ):
            a = jnp.where(at == 0, held[k], held[k + ZLO])
            b = jnp.where(at == 0, other[k], other[k + ZLO])
            parts += [jnp.where(is_zero, a, b), jnp.where(is_zero, b, a)]
        lines.append(jnp.concatenate(parts, axis=1))
    rows_in = jnp.concatenate(lines, axis=0)

    gate_part = jnp.dot(rows_in, w_gate, preferred_element_type=f32)
    up_part = jnp.dot(rows_in, w_up, preferred_element_type=f32)
    hidden = (jax.nn.silu(gate_part) * up_part).astype(bf16)

    def columns(which):
        return jnp.concatenate(
            [
                lax.dynamic_slice_in_dim(w_down, which * quarter, quarter, 1),
                lax.dynamic_slice_in_dim(w_down, half + which * quarter, quarter, 1),
            ],
            axis=1,
        )

    away = jnp.dot(hidden, columns(1 - core), preferred_element_type=f32).astype(bf16)
    got = lax.ppermute(away, "c", SWAP)
    kept = jnp.dot(hidden, columns(core), preferred_element_type=f32) + got.astype(f32)

    def share(k):
        side = (z_pos + k) % ZALL // ZLO
        return lax.dynamic_slice(kept, ((k % ZLO) * rows, side * quarter), (rows, quarter))

    far = share(4).astype(bf16)
    from_last = to_next(far[:, :piece]).astype(f32)
    from_next = to_last(far[:, piece:]).astype(f32)
    from_last = jnp.pad(from_last, ((0, 0), (0, piece)))
    from_next = jnp.pad(from_next, ((0, 0), (piece, 0)))
    for k in (3, 2, 1):
        from_last = to_next((share(k) + from_last).astype(bf16)).astype(f32)
        from_next = to_last((share(ZALL - k) + from_next).astype(bf16)).astype(f32)
    total = share(0) + from_last + from_next
    top, bottom = total[: rows // 2], total[rows // 2 :]
    sent = jnp.where(first, bottom, top).astype(bf16)
    final = jnp.where(first, top, bottom) + lax.ppermute(sent, "xl", SWAP).astype(f32)
    final = jnp.pad(
        final.reshape(expert_count, CAP, quarter), ((0, 0), (0, SLOT - CAP), (0, 0))
    )
    returned = lax.all_to_all(final, ("y", "xh"), 0, 0, tiled=True)

    logits = jnp.dot(x_rows.astype(f32), router, precision=lax.Precision.HIGHEST)
    chosen = jnp.sum(
        onehot.reshape(local_rows, picks, expert_count).astype(f32) * logits[:, None, :], axis=2
    )
    squashed = jax.nn.sigmoid(chosen)
    gate_share = squashed / jnp.sum(squashed, axis=1, keepdims=True)
    weighting = jnp.sum(placed.astype(f32) * gate_share[:, :, None], axis=1)
    moe_out = jnp.dot(
        weighting, returned.reshape(expert_count * SLOT, quarter), precision=lax.Precision.HIGHEST
    )
    attn_out = attention_block(queries, cache, lengths)
    return (moe_out.astype(bf16), attn_out)


def solution(mesh):
    fine = Mesh(mesh.devices.reshape(4, 2, 2, 4, 2, 2), ("y", "xh", "xl", "zl", "zh", "c"))
    grp, tp = ("y", "xh", "xl", "zl"), ("zh", "c")
    every = grp + tp
    return jax.shard_map(
        shards,
        mesh=fine,
        in_specs=(
            P(grp, None),
            P(grp, None),
            P(),
            P(None, every),
            P(None, every),
            P(every, None),
            P(every, None),
            P(every, None, None),
            P(every),
        ),
        out_specs=(P(grp, tp), P(every, None)),
        check_vma=False,
    )
```

time: 529 us -> 228 us (0.43)
  waiting for transfers between devices: 281 us -> 72.9 us
  blocking collectives: 175 us -> 15.3 us
  other arithmetic: 3.48 us -> 78.7 us
  starting transfers between devices: 10.3 us -> 30 us
  local copies, waits for them, and re-layouts: 22 us -> 8.89 us
  between operations: 14.2 us -> 1.15 us
    reduce_scatter x1 -> x0, waiting for transfers between devices: 202 us -> none  [shards(): lax.psum_scatter(partial_value, 'tp', scatter_dimension=2, tiled=True)]
    all_to_all x1, blocking collectives: 175 us -> 15.3 us  [shards(): lax.all_to_all(packed.reshape(expert_count, SLOT, quarter), ('y', 'xh'),...]
    all_to_all x1, waiting for transfers between devices: 78.7 us -> 6.57 us  [shards(): returned = lax.all_to_all(final, ('y', 'xh'), 0, 0, tiled=True)]
    concatenate x0 -> x2, other arithmetic: none -> 68.5 us  [the longest x1 68.5 us: shards(): rows_in = jnp.concatenate(lines, axis=0)]
    ppermute x0 -> x27, waiting for transfers between devices: none -> 66.3 us  [the longest x8 26.8 us: to_next(): return lax.ppermute(value, ('zl', 'zh'), UP)]
    ppermute x0 -> x27, starting transfers between devices: none -> 26.6 us  [the longest x8 20.8 us: to_last(): return lax.ppermute(value, ('zl', 'zh'), DOWN)]
    reshape x2, local copies, waits for them, and re-layouts: 18.8 us -> 0.11 us  [the longest x1 0.07 us: shards(): mine = arrived[:, :CAP].reshape(expert_count * CAP, quarter)]
    all_to_all x1, starting transfers between devices: 10.3 us -> 3.47 us  [shards(): returned = lax.all_to_all(final, ('y', 'xh'), 0, 0, tiled=True)]
  transfers between devices with their start and end apart: 2 -> 28, of which waited for: 2 -> 20; matrix products, arithmetic and copies ran while one was open for 1% -> 6% of each run, Pallas kernels for 0% -> 0%
where the time goes in v1:
time: 228 us; the launch traced here: 224 us
  other arithmetic  78.7 us (35%)
  waiting for transfers between devices  72.9 us (32%)
  starting transfers between devices  30 us (13%)
  matrix products  17.4 us (8%)
  blocking collectives  15.3 us (7%)
  local copies, waits for them, and re-layouts  8.89 us (4%)
    concatenate x1, other arithmetic, shards(): rows_in = jnp.concatenate(lines, axis=0)  68.5 us
    ppermute x8, waiting for transfers between devices, to_next(): return lax.ppermute(value, ('zl', 'zh'), UP)  26.8 us
    ppermute x8, waiting for transfers between devices, to_last(): return lax.ppermute(value, ('zl', 'zh'), DOWN)  24.4 us
    ppermute x8, starting transfers between devices, to_last(): return lax.ppermute(value, ('zl', 'zh'), DOWN)  20.8 us
    all_to_all x1, blocking collectives, shards(): lax.all_to_all(packed.reshape(expert_count, SLOT, quarter), ('y', 'xh'),...  15.3 us
    all_to_all x1, waiting for transfers between devices, shards(): returned = lax.all_to_all(final, ('y', 'xh'), 0, 0, tiled=True)  6.57 us
    ppermute x1, waiting for transfers between devices, shards(): lax.ppermute(sent, 'xl', SWAP).astype(f32)  5.28 us
    unnamed x39, local copies, waits for them, and re-layouts  5.15 us
  transfers between devices with their start and end apart: 28, of which 20 were waited for; matrix products, arithmetic and copies ran while one was open for 6% of the time, Pallas kernels for 0%

profile of v1, /device:TPU:32, one launch (start us, length us, event | category | flops | bytes accessed | tf_op | source)
XLA Modules:
  0.0 224.4 jit_solution(6512475414603473509)
XLA Ops:
  0.6 0.9 copy.17
  2.3 1.1 fusion.1
  3.4 15.3 %all_to_all.10 = bf16[8,8,1792]{2,1,0:T(8,128)(2,1)S(1)} all-to-all(bf16[8,8,1792]{2,1,0:T(8,128)(2,1)S(1)} %fusion.1), channel_id=1, replica_groups=mesh['y'=4,'xh'=2,'xl'=2,'zl'=4,'zh'=2,'c'=2] {'y','xh'}, dimensions={0} | all-to-all | bytes 458752 | tf_op jit(solution)/shard_map/all_to_all | solution.py:80
  19.5 4.5 %collective-permute-done = bf16[40,1792]{1,0:T(8,128)(2,1)S(1)} collective-permute-done((bf16[40,1792]{1,0:T(8,128)(2,1)S(1)}, bf16[40,1792]{1,0:T(8,128)(2,1)S(1)}, u32[]{:S(2)}, u32[]{:S(2)}) %collective-permute-start) | collective-permute-done | bytes 143392 | tf_op jit(solution)/shard_map/ppermute | solution.py:84
  24.9 1.9 collective-permute-start.5
  26.8 5.5 %collective-permute-done.1 = bf16[80,1792]{1,0:T(8,128)(2,1)S(1)} collective-permute-done((bf16[80,1792]{1,0:T(8,128)(2,1)S(1)}, bf16[80,1792]{1,0:T(8,128)(2,1)S(1)}, u32[]{:S(2)}, u32[]{:S(2)}) %collective-permute-start.1) | collective-permute-done | bytes 286752 | tf_op jit(solution)/shard_map/ppermute | solution.py:54
  32.3 2.6 %collective-permute-start.2 = (bf16[80,1792]{1,0:T(8,128)(2,1)S(1)}, bf16[80,1792]{1,0:T(8,128)(2,1)}, u32[]{:S(2)}, u32[]{:S(2)}) collective-permute-start(bf16[80,1792]{1,0:T(8,128)(2,1)S(1)} %collective-permute-done.1), channel_id=1, source_target_pairs={{0,14},{4,0},{8,4},{12,8},{2,12},{6,2},{10,6},{14,10},{1,15},{5,1}... | collective-permute-start | bytes 860168 | tf_op jit(solution)/shard_map/ppermute | solution.py:54
  35.5 4.8 %collective-permute-done.2 = bf16[80,1792]{1,0:T(8,128)(2,1)} collective-permute-done((bf16[80,1792]{1,0:T(8,128)(2,1)S(1)}, bf16[80,1792]{1,0:T(8,128)(2,1)}, u32[]{:S(2)}, u32[]{:S(2)}) %collective-permute-start.2) | collective-permute-done | bytes 286752 | tf_op jit(solution)/shard_map/ppermute | solution.py:54
  40.2 3.3 %collective-permute-start.3 = (bf16[80,1792]{1,0:T(8,128)(2,1)}, bf16[80,1792]{1,0:T(8,128)(2,1)S(1)}, u32[]{:S(2)}, u32[]{:S(2)}) collective-permute-start(bf16[80,1792]{1,0:T(8,128)(2,1)} %collective-permute-done.2), channel_id=1, source_target_pairs={{0,14},{4,0},{8,4},{12,8},{2,12},{6,2},{10,6},{14,10},{1,15},{5,1}... | collective-permute-start | bytes 860168 | tf_op jit(solution)/shard_map/ppermute | solution.py:54
  44.1 1.8 constant_dynamic-slice_fusion.3
  46.1 1.9 collective-permute-done.3
  48.0 7.1 %collective-permute-done.7 = bf16[80,1792]{1,0:T(8,128)(2,1)S(1)} collective-permute-done((bf16[80,1792]{1,0:T(8,128)(2,1)}, bf16[80,1792]{1,0:T(8,128)(2,1)S(1)}, u32[]{:S(2)}, u32[]{:S(2)}) %collective-permute-start.7) | collective-permute-done | bytes 286752 | tf_op jit(solution)/shard_map/ppermute | solution.py:50
  55.2 3.0 %collective-permute-start.4 = (bf16[80,896]{1,0:T(8,128)(2,1)S(1)}, bf16[80,896]{1,0:T(8,128)(2,1)S(1)}, u32[]{:S(2)}, u32[]{:S(2)}) collective-permute-start(bf16[80,896]{1,0:T(8,128)(2,1)S(1)} %slice.37), channel_id=1, source_target_pairs={{0,14},{4,0},{8,4},{12,8},{2,12},{6,2},{10,6},{14,10},{1,15},{5,1}... | collective-permute-start | bytes 430088 | tf_op jit(solution)/shard_map/ppermute | solution.py:54
  58.3 1.2 broadcast_select_fusion.23
  59.5 1.2 collective-permute-done.4
  60.8 2.5 %collective-permute-done.8 = bf16[80,896]{1,0:T(8,128)(2,1)S(1)} collective-permute-done((bf16[80,896]{1,0:T(8,128)(2,1)S(1)}, bf16[80,896]{1,0:T(8,128)(2,1)S(1)}, u32[]{:S(2)}, u32[]{:S(2)}) %collective-permute-start.8) | collective-permute-done | bytes 143392 | tf_op jit(solution)/shard_map/ppermute | solution.py:50
  65.6 68.5 %maximum_maximum_fusion = bf16[320,7168]{1,0:T(8,128)(2,1)S(1)} fusion(bf16[80,1792]{1,0:T(8,128)(2,1)S(1)} %get-tuple-element.23, bf16[80,1792]{1,0:T(8,128)(2,1)S(1)} %get-tuple-element.22, bf16[80,1792]{1,0:T(8,128)(2,1)S(1)} %get-tuple-element.21, bf16[80,1792]{1,0:T(8,128)(2,1)S(1)} %get-tuple-element.20, bf16[80,1792]{1,0:T(8,128)(2,1)S(1)} %get-tuple-element.19, ...), kind=kLoop, calls=%fused_computation.2 | loop fusion | flops 73400320 | bytes 9175040 | tf_op jit(solution)/shard_map/concatenate | solution.py:113
  134.1 1.9 fusion.51
  136.0 1.9 multiply_convert_fusion
  137.9 2.2 convolution_convert_fusion
  140.5 4.4 %collective-permute-done.17 = bf16[320,3584]{1,0:T(8,128)(2,1)} collective-permute-done((bf16[320,3584]{1,0:T(8,128)(2,1)}, bf16[320,3584]{1,0:T(8,128)(2,1)}, u32[]{:S(2)}, u32[]{:S(2)}) %collective-permute-start.17) | collective-permute-done | bytes 2293792 | tf_op jit(solution)/shard_map/ppermute | solution.py:129
  144.9 2.5 %convert_add_fusion = f32[320,3584]{1,0:T(8,128)S(1)} fusion(bf16[320,3584]{1,0:T(8,128)(2,1)} %collective-permute-done.17, bf16[320,160]{0,1:T(8,128)(2,1)} %copy-done.6, bf16[160,1792]{1,0:T(8,128)(2,1)S(1)} %get-tuple-element.5, bf16[160,1792]{1,0:T(8,128)(2,1)S(1)} %get-tuple-element.4), kind=kOutput, calls=%fused_computation.3 | convolution fusion | flops 371589120 | bytes 8130560 | tf_op jit(solution)/shard_map/dot_general | solution.py:130
  147.4 2.1 copy-done.1
  150.2 6.0 %collective-permute-done.18 = bf16[80,896]{1,0:T(8,128)(2,1)S(1)} collective-permute-done((bf16[80,896]{1,0:T(8,128)(2,1)S(1)}, bf16[80,896]{1,0:T(8,128)(2,1)S(1)}, u32[]{:S(2)}, u32[]{:S(2)}) %collective-permute-start.18) | collective-permute-done | bytes 143392 | tf_op jit(solution)/shard_map/ppermute | solution.py:50
  156.3 1.1 add_convert_fusion.5
  157.7 8.7 %collective-permute-done.19 = bf16[80,1792]{1,0:T(8,128)(2,1)S(1)} collective-permute-done((bf16[80,1792]{1,0:T(8,128)(2,1)S(1)}, bf16[80,1792]{1,0:T(8,128)(2,1)S(1)}, u32[]{:S(2)}, u32[]{:S(2)}) %collective-permute-start.19) | collective-permute-done | bytes 286752 | tf_op jit(solution)/shard_map/ppermute | solution.py:50
  166.4 1.1 add_convert_fusion.4
  167.6 3.0 %collective-permute-start.22 = (bf16[80,896]{1,0:T(8,128)(2,1)}, bf16[80,896]{1,0:T(8,128)(2,1)S(1)}, u32[]{:S(2)}, u32[]{:S(2)}) collective-permute-start(bf16[80,896]{1,0:T(8,128)(2,1)} %get-tuple-element.25), channel_id=1, source_target_pairs={{0,14},{4,0},{8,4},{12,8},{2,12},{6,2},{10,6},{14,10},{1,15},{5,1}... | collective-permute-start | bytes 430088 | tf_op jit(solution)/shard_map/ppermute | solution.py:54
  170.7 3.0 %collective-permute-done.22 = bf16[80,896]{1,0:T(8,128)(2,1)S(1)} collective-permute-done((bf16[80,896]{1,0:T(8,128)(2,1)}, bf16[80,896]{1,0:T(8,128)(2,1)S(1)}, u32[]{:S(2)}, u32[]{:S(2)}) %collective-permute-start.22) | collective-permute-done | bytes 143392 | tf_op jit(solution)/shard_map/ppermute | solution.py:54
  174.3 1.9 collective-permute-done.20
  176.2 1.3 add_convert_fusion.3
  177.5 3.0 %collective-permute-start.23 = (bf16[80,1792]{1,0:T(8,128)(2,1)S(1)}, bf16[80,1792]{1,0:T(8,128)(2,1)}, u32[]{:S(2)}, u32[]{:S(2)}) collective-permute-start(bf16[80,1792]{1,0:T(8,128)(2,1)S(1)} %get-tuple-element.3), channel_id=1, source_target_pairs={{0,14},{4,0},{8,4},{12,8},{2,12},{6,2},{10,6},{14,10},{1,15},{5,1}... | collective-permute-start | bytes 860168 | tf_op jit(solution)/shard_map/ppermute | solution.py:54
  180.6 4.2 %collective-permute-done.23 = bf16[80,1792]{1,0:T(8,128)(2,1)} collective-permute-done((bf16[80,1792]{1,0:T(8,128)(2,1)S(1)}, bf16[80,1792]{1,0:T(8,128)(2,1)}, u32[]{:S(2)}, u32[]{:S(2)}) %collective-permute-start.23) | collective-permute-done | bytes 286752 | tf_op jit(solution)/shard_map/ppermute | solution.py:54
  184.7 1.2 add_convert_fusion.1
  185.9 2.7 %collective-permute-start.24 = (bf16[80,1792]{1,0:T(8,128)(2,1)S(1)}, bf16[80,1792]{1,0:T(8,128)(2,1)S(1)}, u32[]{:S(2)}, u32[]{:S(2)}) collective-permute-start(bf16[80,1792]{1,0:T(8,128)(2,1)S(1)} %add_convert_fusion.1), channel_id=1, source_target_pairs={{0,14},{4,0},{8,4},{12,8},{2,12},{6,2},{10,6},{14,10},{1,15},{5,1}... | collective-permute-start | bytes 860168 | tf_op jit(solution)/shard_map/ppermute | solution.py:54
  188.7 1.3 fusion.50
  190.0 2.8 %collective-permute-done.24 = bf16[80,1792]{1,0:T(8,128)(2,1)S(1)} collective-permute-done((bf16[80,1792]{1,0:T(8,128)(2,1)S(1)}, bf16[80,1792]{1,0:T(8,128)(2,1)S(1)}, u32[]{:S(2)}, u32[]{:S(2)}) %collective-permute-start.24) | collective-permute-done | bytes 286752 | tf_op jit(solution)/shard_map/ppermute | solution.py:54
  192.8 1.8 add_convert_fusion
  194.6 3.0 %collective-permute-start.25 = (bf16[80,1792]{1,0:T(8,128)(2,1)}, bf16[80,1792]{1,0:T(8,128)(2,1)S(1)}, u32[]{:S(2)}, u32[]{:S(2)}) collective-permute-start(bf16[80,1792]{1,0:T(8,128)(2,1)} %add_convert_fusion), channel_id=1, source_target_pairs={{0,14},{4,0},{8,4},{12,8},{2,12},{6,2},{10,6},{14,10},{1,15},{5,1}... | collective-permute-start | bytes 860168 | tf_op jit(solution)/shard_map/ppermute | solution.py:54
  197.6 3.4 %fusion.45 = (f32[4,64]{1,0:T(4,128)S(1)}, bf16[4,64,1024]{2,1,0:T(8,128)(2,1)}) fusion(pred[4,1024]{1,0:T(4,128)(4,1)S(1)} %iota_compare_fusion, bf16[4,1024,512]{2,1,0:T(8,128)(2,1)} %param.16, bf16[1,4,64,256]{3,1,2,0:T(4,128)(2,1)} %bitcast.27), kind=kOutput, calls=%fused_computation.101 | convolution fusion | flops 135791616 | bytes 2761728 | tf_op jit(solution)/shard_map/sub | solution.py:29
  201.0 1.1 collective-permute-done.25
  202.1 1.1 convert_add_fusion.1
  204.0 5.3 %collective-permute-done.26 = bf16[40,1792]{1,0:T(8,128)(2,1)S(1)} collective-permute-done((bf16[40,1792]{1,0:T(8,128)(2,1)S(1)}, bf16[40,1792]{1,0:T(8,128)(2,1)S(1)}, u32[]{:S(2)}, u32[]{:S(2)}) %collective-permute-start.26) | collective-permute-done | bytes 143392 | tf_op jit(solution)/shard_map/ppermute | solution.py:147
  209.4 0.8 pad.22
  210.2 3.5 %all-to-all-start.1 = ((f32[8,8,1792]{2,1,0:T(8,128)}), f32[8,8,1792]{2,1,0:T(8,128)S(1)}, u32[]{:S(2)}, u32[]{:S(2)}) async-start(f32[8,8,1792]{2,1,0:T(8,128)} %pad.22), calls=%async_computation.1 | async-start | bytes 917504 | tf_op jit(solution)/shard_map/all_to_all | solution.py:151
  213.8 2.2 fusion.30
  216.9 6.6 %all-to-all-done.1 = f32[8,8,1792]{2,1,0:T(8,128)S(1)} async-done(((f32[8,8,1792]{2,1,0:T(8,128)}), f32[8,8,1792]{2,1,0:T(8,128)S(1)}, u32[]{:S(2)}, u32[]{:S(2)}) %all-to-all-start.1) | async-done | bytes 458784 | tf_op jit(solution)/shard_map/all_to_all | solution.py:151
  223.5 1.0 convolution_convert_fusion.2
  (95 shorter events, 10.1 us)
Async XLA Ops:
  0.6 133.4 %copy-start = (bf16[7168,160]{0,1:T(8,128)(2,1)S(1)}, bf16[7168,160]{0,1:T(8,128)(2,1)}, u32[]{:S(2)}) copy-start(bf16[7168,160]{0,1:T(8,128)(2,1)} %param.12) | copy-start | bytes 6881284
  18.8 5.2 %collective-permute-start = (bf16[40,1792]{1,0:T(8,128)(2,1)S(1)}, bf16[40,1792]{1,0:T(8,128)(2,1)S(1)}, u32[]{:S(2)}, u32[]{:S(2)}) collective-permute-start(bf16[40,1792]{1,0:T(8,128)(2,1)S(1)} %reshape.126), channel_id=1, source_target_pairs={{0,16},{16,0},{1,17},{17,1},{2,18},{18,2},{3,19},{19,3},{4,20},{20... | collective-permute-start | bytes 430088 | tf_op jit(solution)/shard_map/ppermute | solution.py:84
  24.0 0.7 copy-start.2
  24.0 0.7 copy-start.4
  24.7 10.7 %copy-start.12 = (bf16[80,1792]{1,0:T(8,128)(2,1)}, bf16[80,1792]{1,0:T(8,128)(2,1)S(1)}, u32[]{:S(2)}) copy-start(bf16[80,1792]{1,0:T(8,128)(2,1)S(1)} %pad_maximum_fusion) | copy-start | bytes 860164
  24.7 7.6 %collective-permute-start.1 = (bf16[80,1792]{1,0:T(8,128)(2,1)S(1)}, bf16[80,1792]{1,0:T(8,128)(2,1)S(1)}, u32[]{:S(2)}, u32[]{:S(2)}) collective-permute-start(bf16[80,1792]{1,0:T(8,128)(2,1)S(1)} %pad_maximum_fusion), channel_id=1, source_target_pairs={{0,14},{4,0},{8,4},{12,8},{2,12},{6,2},{10,6},{14,10},{1,15},{5,1}... | collective-permute-start | bytes 860168 | tf_op jit(solution)/shard_map/ppermute | solution.py:54
  24.9 10.5 %collective-permute-start.5 = (bf16[80,1792]{1,0:T(8,128)(2,1)S(1)}, bf16[80,1792]{1,0:T(8,128)(2,1)S(1)}, u32[]{:S(2)}, u32[]{:S(2)}) collective-permute-start(bf16[80,1792]{1,0:T(8,128)(2,1)S(1)} %pad_maximum_fusion), channel_id=1, source_target_pairs={{0,4},{4,8},{8,12},{12,2},{2,6},{6,10},{10,14},{14,0},{1,5},{5,9},... | collective-permute-start | bytes 860168 | tf_op jit(solution)/shard_map/ppermute | solution.py:50
  32.3 11.8 %copy-start.8 = (bf16[80,1792]{1,0:T(8,128)(2,1)}, bf16[80,1792]{1,0:T(8,128)(2,1)S(1)}, u32[]{:S(2)}) copy-start(bf16[80,1792]{1,0:T(8,128)(2,1)S(1)} %collective-permute-done.1) | copy-start | bytes 860164
  32.3 7.9 %collective-permute-start.2 = (bf16[80,1792]{1,0:T(8,128)(2,1)S(1)}, bf16[80,1792]{1,0:T(8,128)(2,1)}, u32[]{:S(2)}, u32[]{:S(2)}) collective-permute-start(bf16[80,1792]{1,0:T(8,128)(2,1)S(1)} %collective-permute-done.1), channel_id=1, source_target_pairs={{0,14},{4,0},{8,4},{12,8},{2,12},{6,2},{10,6},{14,10},{1,15},{5,1}... | collective-permute-start | bytes 860168 | tf_op jit(solution)/shard_map/ppermute | solution.py:54
  35.3 8.7 %copy-start.10 = (bf16[80,1792]{1,0:T(8,128)(2,1)}, bf16[80,1792]{1,0:T(8,128)(2,1)S(1)}, u32[]{:S(2)}) copy-start(bf16[80,1792]{1,0:T(8,128)(2,1)S(1)} %collective-permute-done.5) | copy-start | bytes 860164
  35.4 8.2 %collective-permute-start.6 = (bf16[80,1792]{1,0:T(8,128)(2,1)S(1)}, bf16[80,1792]{1,0:T(8,128)(2,1)}, u32[]{:S(2)}, u32[]{:S(2)}) collective-permute-start(bf16[80,1792]{1,0:T(8,128)(2,1)S(1)} %collective-permute-done.5), channel_id=1, source_target_pairs={{0,4},{4,8},{8,12},{12,2},{2,6},{6,10},{10,14},{14,0},{1,5},{5,9},... | collective-permute-start | bytes 860168 | tf_op jit(solution)/shard_map/ppermute | solution.py:50
  35.4 10.4 %copy-start.13 = (bf16[80,1792]{1,0:T(8,128)(2,1)S(1)}, bf16[80,1792]{1,0:T(8,128)(2,1)}, u32[]{:S(2)}) copy-start(bf16[80,1792]{1,0:T(8,128)(2,1)} %copy-done.12) | copy-start | bytes 860164
  40.2 7.8 %collective-permute-start.3 = (bf16[80,1792]{1,0:T(8,128)(2,1)}, bf16[80,1792]{1,0:T(8,128)(2,1)S(1)}, u32[]{:S(2)}, u32[]{:S(2)}) collective-permute-start(bf16[80,1792]{1,0:T(8,128)(2,1)} %collective-permute-done.2), channel_id=1, source_target_pairs={{0,14},{4,0},{8,4},{12,8},{2,12},{6,2},{10,6},{14,10},{1,15},{5,1}... | collective-permute-start | bytes 860168 | tf_op jit(solution)/shard_map/ppermute | solution.py:54
  43.5 14.6 %collective-permute-start.13 = (bf16[80,1792]{1,0:T(8,128)(2,1)}, bf16[80,1792]{1,0:T(8,128)(2,1)S(1)}, u32[]{:S(2)}, u32[]{:S(2)}) collective-permute-start(bf16[80,1792]{1,0:T(8,128)(2,1)} %collective-permute-done.2), channel_id=1, source_target_pairs={{0,1},{1,0},{2,3},{3,2},{4,5},{5,4},{6,7},{7,6},{8,9},{9,8},{10,11... | collective-permute-start | bytes 860168 | tf_op jit(solution)/shard_map/ppermute | solution.py:99
  43.5 14.7 %collective-permute-start.14 = (bf16[80,1792]{1,0:T(8,128)(2,1)}, bf16[80,1792]{1,0:T(8,128)(2,1)S(1)}, u32[]{:S(2)}, u32[]{:S(2)}) collective-permute-start(bf16[80,1792]{1,0:T(8,128)(2,1)} %collective-permute-done.6), channel_id=1, source_target_pairs={{0,1},{1,0},{2,3},{3,2},{4,5},{5,4},{6,7},{7,6},{8,9},{9,8},{10,11... | collective-permute-start | bytes 860168 | tf_op jit(solution)/shard_map/ppermute | solution.py:99
  44.1 11.1 %collective-permute-start.7 = (bf16[80,1792]{1,0:T(8,128)(2,1)}, bf16[80,1792]{1,0:T(8,128)(2,1)S(1)}, u32[]{:S(2)}, u32[]{:S(2)}) collective-permute-start(bf16[80,1792]{1,0:T(8,128)(2,1)} %collective-permute-done.6), channel_id=1, source_target_pairs={{0,4},{4,8},{8,12},{12,2},{2,6},{6,10},{10,14},{14,0},{1,5},{5,9},... | collective-permute-start | bytes 860168 | tf_op jit(solution)/shard_map/ppermute | solution.py:50
  44.1 3.9 %copy-start.11 = (bf16[80,1792]{1,0:T(8,128)(2,1)S(1)}, bf16[80,1792]{1,0:T(8,128)(2,1)}, u32[]{:S(2)}) copy-start(bf16[80,1792]{1,0:T(8,128)(2,1)} %copy-done.10) | copy-start | bytes 860164
  44.1 16.7 %copy-start.9 = (bf16[80,1792]{1,0:T(8,128)(2,1)S(1)}, bf16[80,1792]{1,0:T(8,128)(2,1)}, u32[]{:S(2)}) copy-start(bf16[80,1792]{1,0:T(8,128)(2,1)} %copy-done.8) | copy-start | bytes 860164
  45.9 19.4 %copy-start.3 = (bf16[40,1792]{1,0:T(8,128)(2,1)S(1)}, bf16[40,1792]{1,0:T(8,128)(2,1)}, u32[]{:S(2)}) copy-start(bf16[40,1792]{1,0:T(8,128)(2,1)} %copy-done.2) | copy-start | bytes 430084
  45.9 19.4 %copy-start.5 = (bf16[40,1792]{1,0:T(8,128)(2,1)S(1)}, bf16[40,1792]{1,0:T(8,128)(2,1)}, u32[]{:S(2)}) copy-start(bf16[40,1792]{1,0:T(8,128)(2,1)} %copy-done.4) | copy-start | bytes 430084
  45.9 19.1 %collective-permute-start.9 = (bf16[80,1792]{1,0:T(8,128)(2,1)S(1)}, bf16[80,1792]{1,0:T(8,128)(2,1)S(1)}, u32[]{:S(2)}, u32[]{:S(2)}) collective-permute-start(bf16[80,1792]{1,0:T(8,128)(2,1)S(1)} %copy-done.13), channel_id=1, source_target_pairs={{0,1},{1,0},{2,3},{3,2},{4,5},{5,4},{6,7},{7,6},{8,9},{9,8},{10,11... | collective-permute-start | bytes 860168 | tf_op jit(solution)/shard_map/ppermute | solution.py:99
  48.0 15.3 %collective-permute-start.16 = (bf16[80,1792]{1,0:T(8,128)(2,1)S(1)}, bf16[80,1792]{1,0:T(8,128)(2,1)S(1)}, u32[]{:S(2)}, u32[]{:S(2)}) collective-permute-start(bf16[80,1792]{1,0:T(8,128)(2,1)S(1)} %copy-done.11), channel_id=1, source_target_pairs={{0,1},{1,0},{2,3},{3,2},{4,5},{5,4},{6,7},{7,6},{8,9},{9,8},{10,11... | collective-permute-start | bytes 860168 | tf_op jit(solution)/shard_map/ppermute | solution.py:99
  55.2 5.6 %collective-permute-start.4 = (bf16[80,896]{1,0:T(8,128)(2,1)S(1)}, bf16[80,896]{1,0:T(8,128)(2,1)S(1)}, u32[]{:S(2)}, u32[]{:S(2)}) collective-permute-start(bf16[80,896]{1,0:T(8,128)(2,1)S(1)} %slice.37), channel_id=1, source_target_pairs={{0,14},{4,0},{8,4},{12,8},{2,12},{6,2},{10,6},{14,10},{1,15},{5,1}... | collective-permute-start | bytes 430088 | tf_op jit(solution)/shard_map/ppermute | solution.py:54
  58.1 5.2 %collective-permute-start.8 = (bf16[80,896]{1,0:T(8,128)(2,1)S(1)}, bf16[80,896]{1,0:T(8,128)(2,1)S(1)}, u32[]{:S(2)}, u32[]{:S(2)}) collective-permute-start(bf16[80,896]{1,0:T(8,128)(2,1)S(1)} %slice.38), channel_id=1, source_target_pairs={{0,4},{4,8},{8,12},{12,2},{2,6},{6,10},{10,14},{14,0},{1,5},{5,9},... | collective-permute-start | bytes 430088 | tf_op jit(solution)/shard_map/ppermute | solution.py:50
  58.2 5.9 %collective-permute-start.15 = (bf16[80,1792]{1,0:T(8,128)(2,1)S(1)}, bf16[80,1792]{1,0:T(8,128)(2,1)S(1)}, u32[]{:S(2)}, u32[]{:S(2)}) collective-permute-start(bf16[80,1792]{1,0:T(8,128)(2,1)S(1)} %collective-permute-done.3), channel_id=1, source_target_pairs={{0,1},{1,0},{2,3},{3,2},{4,5},{5,4},{6,7},{7,6},{8,9},{9,8},{10,11... | collective-permute-start | bytes 860168 | tf_op jit(solution)/shard_map/ppermute | solution.py:99
  60.7 3.5 %collective-permute-start.11 = (bf16[80,1792]{1,0:T(8,128)(2,1)S(1)}, bf16[80,1792]{1,0:T(8,128)(2,1)S(1)}, u32[]{:S(2)}, u32[]{:S(2)}) collective-permute-start(bf16[80,1792]{1,0:T(8,128)(2,1)S(1)} %copy-done.9), channel_id=1, source_target_pairs={{0,1},{1,0},{2,3},{3,2},{4,5},{5,4},{6,7},{7,6},{8,9},{9,8},{10,11... | collective-permute-start | bytes 860168 | tf_op jit(solution)/shard_map/ppermute | solution.py:99
  63.3 1.6 collective-permute-start.12
  63.3 2.0 collective-permute-start.10
  134.1 1.9 copy-start.17
  137.9 2.2 copy-start.6
  140.1 4.8 %collective-permute-start.17 = (bf16[320,3584]{1,0:T(8,128)(2,1)}, bf16[320,3584]{1,0:T(8,128)(2,1)}, u32[]{:S(2)}, u32[]{:S(2)}) collective-permute-start(bf16[320,3584]{1,0:T(8,128)(2,1)} %convolution_convert_fusion), channel_id=1, source_target_pairs={{0,1},{1,0},{2,3},{3,2},{4,5},{5,4},{6,7},{7,6},{8,9},{9,8},{10,11... | collective-permute-start | bytes 6881288 | tf_op jit(solution)/shard_map/ppermute | solution.py:129
  147.4 2.1 copy-start.1
  149.5 39.1 %copy-start.16 = (s32[4]{0:T(128)S(1)}, s32[4]{0:T(128)}, u32[]{:S(2)}) copy-start(s32[4]{0:T(128)} %param.17) | copy-start | bytes 52
  149.5 39.2 %copy-start.7 = (bf16[16,7168]{1,0:T(8,128)(2,1)S(1)}, bf16[16,7168]{1,0:T(8,128)(2,1)}, u32[]{:S(2)}) copy-start(bf16[16,7168]{1,0:T(8,128)(2,1)} %param.9) | copy-start | bytes 688132
  150.2 6.0 %collective-permute-start.18 = (bf16[80,896]{1,0:T(8,128)(2,1)S(1)}, bf16[80,896]{1,0:T(8,128)(2,1)S(1)}, u32[]{:S(2)}, u32[]{:S(2)}) collective-permute-start(bf16[80,896]{1,0:T(8,128)(2,1)S(1)} %get-tuple-element.24), channel_id=1, source_target_pairs={{0,4},{4,8},{8,12},{12,2},{2,6},{6,10},{10,14},{14,0},{1,5},{5,9},... | collective-permute-start | bytes 430088 | tf_op jit(solution)/shard_map/ppermute | solution.py:50
  157.4 9.1 %collective-permute-start.19 = (bf16[80,1792]{1,0:T(8,128)(2,1)S(1)}, bf16[80,1792]{1,0:T(8,128)(2,1)S(1)}, u32[]{:S(2)}, u32[]{:S(2)}) collective-permute-start(bf16[80,1792]{1,0:T(8,128)(2,1)S(1)} %add_convert_fusion.5), channel_id=1, source_target_pairs={{0,4},{4,8},{8,12},{12,2},{2,6},{6,10},{10,14},{14,0},{1,5},{5,9},... | collective-permute-start | bytes 860168 | tf_op jit(solution)/shard_map/ppermute | solution.py:50
  167.5 8.7 %collective-permute-start.20 = (bf16[80,1792]{1,0:T(8,128)(2,1)S(1)}, bf16[80,1792]{1,0:T(8,128)(2,1)S(1)}, u32[]{:S(2)}, u32[]{:S(2)}) collective-permute-start(bf16[80,1792]{1,0:T(8,128)(2,1)S(1)} %add_convert_fusion.4), channel_id=1, source_target_pairs={{0,4},{4,8},{8,12},{12,2},{2,6},{6,10},{10,14},{14,0},{1,5},{5,9},... | collective-permute-start | bytes 860168 | tf_op jit(solution)/shard_map/ppermute | solution.py:50
  167.6 6.0 %collective-permute-start.22 = (bf16[80,896]{1,0:T(8,128)(2,1)}, bf16[80,896]{1,0:T(8,128)(2,1)S(1)}, u32[]{:S(2)}, u32[]{:S(2)}) collective-permute-start(bf16[80,896]{1,0:T(8,128)(2,1)} %get-tuple-element.25), channel_id=1, source_target_pairs={{0,14},{4,0},{8,4},{12,8},{2,12},{6,2},{10,6},{14,10},{1,15},{5,1}... | collective-permute-start | bytes 430088 | tf_op jit(solution)/shard_map/ppermute | solution.py:54
  173.6 0.7 copy-start.14
  177.5 7.2 %collective-permute-start.23 = (bf16[80,1792]{1,0:T(8,128)(2,1)S(1)}, bf16[80,1792]{1,0:T(8,128)(2,1)}, u32[]{:S(2)}, u32[]{:S(2)}) collective-permute-start(bf16[80,1792]{1,0:T(8,128)(2,1)S(1)} %get-tuple-element.3), channel_id=1, source_target_pairs={{0,14},{4,0},{8,4},{12,8},{2,12},{6,2},{10,6},{14,10},{1,15},{5,1}... | collective-permute-start | bytes 860168 | tf_op jit(solution)/shard_map/ppermute | solution.py:54
  185.9 18.1 %copy-start.15 = (s32[16,2]{0,1:T(2,128)S(1)}, s32[16,2]{0,1:T(2,128)}, u32[]{:S(2)}) copy-start(s32[16,2]{0,1:T(2,128)} %param.10) | copy-start | bytes 388
  185.9 6.8 %collective-permute-start.24 = (bf16[80,1792]{1,0:T(8,128)(2,1)S(1)}, bf16[80,1792]{1,0:T(8,128)(2,1)S(1)}, u32[]{:S(2)}, u32[]{:S(2)}) collective-permute-start(bf16[80,1792]{1,0:T(8,128)(2,1)S(1)} %add_convert_fusion.1), channel_id=1, source_target_pairs={{0,14},{4,0},{8,4},{12,8},{2,12},{6,2},{10,6},{14,10},{1,15},{5,1}... | collective-permute-start | bytes 860168 | tf_op jit(solution)/shard_map/ppermute | solution.py:54
  190.0 11.0 %collective-permute-start.21 = (bf16[80,1792]{1,0:T(8,128)(2,1)S(1)}, bf16[80,1792]{1,0:T(8,128)(2,1)S(1)}, u32[]{:S(2)}, u32[]{:S(2)}) collective-permute-start(bf16[80,1792]{1,0:T(8,128)(2,1)S(1)} %get-tuple-element.2), channel_id=1, source_target_pairs={{0,4},{4,8},{8,12},{12,2},{2,6},{6,10},{10,14},{14,0},{1,5},{5,9},... | collective-permute-start | bytes 860168 | tf_op jit(solution)/shard_map/ppermute | solution.py:50
  194.6 7.5 %collective-permute-start.25 = (bf16[80,1792]{1,0:T(8,128)(2,1)}, bf16[80,1792]{1,0:T(8,128)(2,1)S(1)}, u32[]{:S(2)}, u32[]{:S(2)}) collective-permute-start(bf16[80,1792]{1,0:T(8,128)(2,1)} %add_convert_fusion), channel_id=1, source_target_pairs={{0,14},{4,0},{8,4},{12,8},{2,12},{6,2},{10,6},{14,10},{1,15},{5,1}... | collective-permute-start | bytes 860168 | tf_op jit(solution)/shard_map/ppermute | solution.py:54
  203.3 6.0 %collective-permute-start.26 = (bf16[40,1792]{1,0:T(8,128)(2,1)S(1)}, bf16[40,1792]{1,0:T(8,128)(2,1)S(1)}, u32[]{:S(2)}, u32[]{:S(2)}) collective-permute-start(bf16[40,1792]{1,0:T(8,128)(2,1)S(1)} %select_convert_fusion), channel_id=1, source_target_pairs={{0,16},{16,0},{1,17},{17,1},{2,18},{18,2},{3,19},{19,3},{4,20},{20... | collective-permute-start | bytes 430088 | tf_op jit(solution)/shard_map/ppermute | solution.py:147
  210.2 13.3 %all-to-all-start.1 = ((f32[8,8,1792]{2,1,0:T(8,128)}), f32[8,8,1792]{2,1,0:T(8,128)S(1)}, u32[]{:S(2)}, u32[]{:S(2)}) async-start(f32[8,8,1792]{2,1,0:T(8,128)} %pad.22), calls=%async_computation.1 | async-start | bytes 917504 | tf_op jit(solution)/shard_map/all_to_all | solution.py:151

commit v2 on v0

v2 whole, which is shorter than its diff:
```python
import functools
import math

import jax
import jax.numpy as jnp
import numpy as np
from jax import lax
from jax.experimental import pallas as pl
from jax.experimental.pallas import tpu as pltpu
from jax.sharding import Mesh
from jax.sharding import PartitionSpec as P

CAP = 5
ZLO = 4
ZALL = 8
EXPERTS = 8
BLOCK = 16
PLANE = 16
LANES = 128
REACH = (0, 1, 2, -1)
BF16, F32 = jnp.bfloat16, jnp.float32
VMEM_BYTES = 40 * 1024 * 1024


def place(z):
    return (z % ZLO) * 2 + z // ZLO


def z_pairs(step):
    return [(place(z), place((z + step) % ZALL)) for z in range(ZALL)]


SWAP = [(0, 1), (1, 0)]


def z_send(value, step):
    return lax.ppermute(value, ("zl", "zh"), z_pairs(step))


def as_bf16(array):
    return jnp.asarray(np.asarray(array, np.float32), BF16)


def tables():
    lane = np.arange(LANES)
    lane_e = np.where(lane < EXPERTS * CAP, lane // CAP, -1)
    lane_s = lane % CAP
    e, u = np.divmod(np.arange(EXPERTS * BLOCK), BLOCK)
    k64 = np.arange(ZLO * BLOCK) // BLOCK
    pick_main = (lane_e[None] == e[:, None]) & (lane_s[None] == (u % CAP)[:, None])
    mask_main = (u // CAP)[:, None] == k64[None]
    g, s = np.divmod(u, 4)
    pick_rest = (lane_e[None] == e[:, None]) & (lane_s[None] == ((16 + s) % CAP)[:, None])
    g256 = np.arange(4 * 64) // 64
    k256 = np.tile(k64, 4)
    mask_rest = (g[:, None] == g256[None]) & (((16 + s) // CAP)[:, None] == k256[None])
    row = np.arange(PLANE * BLOCK)
    src, gs = np.divmod(row, BLOCK)
    spot = (gs // 4) * 64 + src * 4 + gs % 4
    shuffle = np.zeros((PLANE * BLOCK, PLANE * BLOCK))
    shuffle[spot, row] = 1
    e2, u2 = row // (2 * BLOCK), row % BLOCK
    back_main = (lane_e[:, None] == e2[None]) & (lane_s[:, None] == (u2 % CAP)[None])
    back_mask = k64[:, None] == (u2 // CAP)[None]
    g2, s2 = np.divmod(u2, 4)
    back_rest = (lane_e[:, None] == e2[None]) & (lane_s[:, None] == ((16 + s2) % CAP)[None])
    back_rest_mask = np.stack(
        [(g2[None] == i) & (k64[:, None] == ((16 + s2) // CAP)[None]) for i in range(4)]
    )
    spread = lane[:, None] == e2[None]
    return dict(
        pack=[as_bf16(a) for a in (pick_main, mask_main, pick_rest, mask_rest)],
        shuffle=as_bf16(shuffle),
        unshuffle=as_bf16(shuffle.T),
        back=[as_bf16(a) for a in (back_main, back_mask, back_rest, back_rest_mask, spread)],
    )


def dot(a, b):
    return jnp.dot(a, b, preferred_element_type=F32)


def dot_t(a, b):
    return lax.dot_general(a, b, (((1,), (1,)), ((), ())), preferred_element_type=F32)


def call(kernel, out_shape, *args):
    at = [pl.BlockSpec(memory_space=pltpu.SMEM if a.dtype == jnp.int32 else pltpu.VMEM) for a in args]
    return pl.pallas_call(
        kernel,
        out_shape=out_shape,
        in_specs=at,
        out_specs=jax.tree.map(lambda _: pl.BlockSpec(memory_space=pltpu.VMEM), out_shape),
        compiler_params=pltpu.CompilerParams(vmem_limit_bytes=VMEM_BYTES),
    )(*args)


def pack_kernel(quarter, *refs):
    blocks, (pick_main, mask_main, pick_rest, mask_rest), (out, marks) = refs[:4], refs[4:8], refs[8:]
    half = 2 * quarter
    eighth = quarter // 2
    rows = jnp.concatenate([b[:, :half] for b in blocks], axis=0)
    chosen = jnp.concatenate([b[:, half:] for b in blocks], axis=0)
    marks[...] = chosen
    select = (dot_t(pick_main[...], chosen) * mask_main[...].astype(F32)).astype(BF16)
    main = dot(select, rows).astype(BF16).reshape(EXPERTS, BLOCK, half)
    chosen4 = jnp.concatenate([chosen] * 4, axis=0)
    rows4 = jnp.concatenate([rows[:, i * eighth : (i + 1) * eighth] for i in range(4)], axis=0)
    select = (dot_t(pick_rest[...], chosen4) * mask_rest[...].astype(F32)).astype(BF16)
    rest = dot(select, rows4).astype(BF16).reshape(EXPERTS, BLOCK, eighth)
    for x in range(2):
        out[:, x, :, :half] = main
        out[:, x, :, half:] = rest


def experts_in(quarter, core, block, shuffle, w_gate, w_up):
    half, eighth = 2 * quarter, quarter // 2
    rest = dot(shuffle[...], block[:, half:]).astype(BF16)
    gate, up = 0.0, 0.0
    for f in range(2):
        top = block[:, f * quarter : (f + 1) * quarter]
        tail = jnp.concatenate(
            [rest[(2 * f + i) * 64 : (2 * f + i + 1) * 64] for i in range(2)], axis=1
        )
        rows = jnp.concatenate([top, tail], axis=0)
        at = pl.ds(pl.multiple_of(f * half + core * quarter, LANES), quarter)
        gate = gate + dot(rows, w_gate[at, :])
        up = up + dot(rows, w_up[at, :])
    return gate, up


def experts_out(quarter, core, hidden, w_down):
    half, eighth = 2 * quarter, quarter // 2
    mains, rests = [], []
    for f in range(2):
        at = pl.ds(pl.multiple_of(f * half + core * quarter, LANES), quarter)
        y = dot(hidden, w_down[:, at])
        mains.append(y[: PLANE * BLOCK])
        tail = y[PLANE * BLOCK :]
        rests += [tail[:, :eighth], tail[:, eighth:]]
    return mains, jnp.concatenate(rests, axis=0)


def own_kernel(quarter, core, block, shuffle, w_gate, w_up, gate_out, up_out):
    gate, up = experts_in(quarter, core[0], block, shuffle, w_gate, w_up)
    gate_out[...] = gate
    up_out[...] = up


def other_kernel(
    quarter, core, block, shuffle, unshuffle, w_gate, w_up, w_down, gate_in, up_in, hidden_out, away
):
    half = 2 * quarter
    there = 1 - core[0]
    gate, up = experts_in(quarter, there, block, shuffle, w_gate, w_up)
    gate, up = gate + gate_in[...], up + up_in[...]
    hidden = (gate * jax.nn.sigmoid(gate) * up).astype(BF16)
    hidden_out[...] = hidden
    mains, rest = experts_out(quarter, there, hidden, w_down)
    for f in range(2):
        away[:, f * quarter : (f + 1) * quarter] = mains[f].astype(BF16)
    away[:, half:] = dot(unshuffle[...], rest.astype(BF16)).astype(BF16)


def sum_kernel(quarter, core, hidden, unshuffle, w_down, got, out):
    half = 2 * quarter
    mains, rest = experts_out(quarter, core[0], hidden[...], w_down)
    for f in range(2):
        at = slice(f * quarter, (f + 1) * quarter)
        out[:, at] = (mains[f] + got[:, at].astype(F32)).astype(BF16)
    high = rest.astype(BF16)
    low = (rest - high.astype(F32)).astype(BF16)
    rest = dot(unshuffle[...], high) + dot(unshuffle[...], low)
    out[:, half:] = (rest + got[:, half:].astype(F32)).astype(BF16)


def combine_kernel(quarter, *refs):
    back, marks = refs[0], refs[1]
    shares = refs[2:6]
    back_main, back_mask, back_rest, back_rest_mask, spread = refs[6:11]
    outs = refs[11:]
    half, eighth = 2 * quarter, quarter // 2
    share = jnp.concatenate([s[...] for s in shares], axis=0)
    high = share.astype(BF16)
    low = (share - high.astype(F32)).astype(BF16)
    chosen = marks[...]
    main = dot(chosen, back_main[...]) * back_mask[...].astype(F32)
    rest = dot(chosen, back_rest[...])
    wide_high, wide_low = dot(high, spread[...]), dot(low, spread[...])
    total = dot((main * wide_high).astype(BF16), back[:, :half]) + dot(
        (main * wide_low).astype(BF16), back[:, :half]
    )
    tail = back[:, half:]
    pieces = []
    for i in range(4):
        mask = rest * back_rest_mask[i].astype(F32)
        pieces.append(
            dot((mask * wide_high).astype(BF16), tail) + dot((mask * wide_low).astype(BF16), tail)
        )
    total = total + jnp.concatenate(pieces, axis=1)
    outs[0][...] = total[:BLOCK]
    for k in range(1, ZLO):
        outs[k][...] = total[k * BLOCK : (k + 1) * BLOCK].astype(BF16)


def attention_block(queries, cache, lengths):
    head_dim = cache.shape[2] // 2
    head_count = queries.shape[1] // head_dim
    requests = queries.shape[0]
    position_count = cache.shape[1]
    query_heads = queries.reshape(requests, head_count, head_dim)
    key_block = cache[:, :, :head_dim]
    value_block = cache[:, :, head_dim:]
    scores = jnp.einsum(
        "bhd,bpd->bhp", query_heads, key_block, preferred_element_type=F32
    ) / math.sqrt(head_dim)
    live = jnp.arange(position_count)[None, :] < lengths[:, None]
    scores = jnp.where(live[:, None, :], scores, -1e30)
    largest = jnp.max(scores, axis=2, keepdims=True)
    weights = jnp.where(live[:, None, :], jnp.exp(scores - largest), 0.0)
    denominator = jnp.sum(weights, axis=2, keepdims=True)
    mixed = jnp.einsum("bhp,bpd->bhd", weights.astype(BF16), value_block, preferred_element_type=F32)
    return (mixed / denominator).astype(BF16).reshape(requests, head_count * head_dim)


def shards(x_rows, route_ids, router, w_gate, w_up, w_down, queries, cache, lengths):
    model_width = x_rows.shape[1]
    hidden_count = w_gate.shape[1]
    quarter = model_width // 4
    half, eighth = 2 * quarter, quarter // 2
    width = half + eighth
    table = tables()
    z_hi, core = lax.axis_index("zh"), lax.axis_index("c")
    core_ref = core.astype(jnp.int32).reshape(1)

    lane = jnp.arange(LANES)
    named = jnp.any(
        (route_ids[:, :, None] == (lane // CAP)[None, None, :]) & (lane < EXPERTS * CAP), axis=1
    )
    earlier = jnp.arange(BLOCK)[:, None] > jnp.arange(BLOCK)[None, :]
    rank = jnp.sum(jnp.where(earlier[:, :, None], named[None].astype(jnp.int32), 0), axis=1)
    marks = (named & (rank == (lane % CAP)[None, :])).astype(BF16)
    payload = jnp.concatenate(
        [
            lax.dynamic_slice_in_dim(x_rows, core * quarter, quarter, 1),
            lax.dynamic_slice_in_dim(x_rows, half + core * quarter, quarter, 1),
            marks,
        ],
        axis=1,
    )
    blocks = [payload] + [z_send(payload, -k) for k in REACH[1:]]

    packed, marks = call(
        functools.partial(pack_kernel, quarter),
        (
            jax.ShapeDtypeStruct((EXPERTS, 2, BLOCK, width), BF16),
            jax.ShapeDtypeStruct((ZLO * BLOCK, LANES), BF16),
        ),
        *blocks,
        *table["pack"],
    )
    arrived = lax.all_to_all(
        packed.reshape(PLANE, BLOCK, width), ("y", "xh", "xl"), 0, 0, tiled=True
    ).reshape(PLANE * BLOCK, width)
    beside = lax.ppermute(arrived, "c", SWAP)
    rows = PLANE * (BLOCK + ZLO)
    partial = jax.ShapeDtypeStruct((rows, hidden_count), F32)
    gate, up = call(
        functools.partial(own_kernel, quarter),
        (partial, partial),
        core_ref, arrived, table["shuffle"], w_gate, w_up,
    )
    pieces = jax.ShapeDtypeStruct((PLANE * BLOCK, width), BF16)
    hidden, away = call(
        functools.partial(other_kernel, quarter),
        (jax.ShapeDtypeStruct((rows, hidden_count), BF16), pieces),
        core_ref, beside, table["shuffle"], table["unshuffle"], w_gate, w_up, w_down, gate, up,
    )
    got = lax.ppermute(away, "c", SWAP)
    summed = call(
        functools.partial(sum_kernel, quarter),
        pieces,
        core_ref, hidden, table["unshuffle"], w_down, got,
    )
    returned = lax.all_to_all(
        summed.reshape(PLANE, BLOCK, width), ("y", "xh", "xl"), 0, 0, tiled=True
    ).reshape(PLANE * BLOCK, width)

    logits = jnp.dot(x_rows.astype(F32), router, precision=lax.Precision.HIGHEST)
    squashed = jax.nn.sigmoid(logits)
    picked = jnp.any(route_ids[:, :, None] == jnp.arange(EXPERTS)[None, None, :], axis=1)
    share = squashed / jnp.sum(jnp.where(picked, squashed, 0.0), axis=1, keepdims=True)
    share = jnp.pad(jnp.where(picked, share, 0.0), ((0, 0), (0, LANES - EXPERTS)))
    shares = [share] + [z_send(share, -k) for k in REACH[1:]]

    parts = call(
        functools.partial(combine_kernel, quarter),
        tuple(jax.ShapeDtypeStruct((BLOCK, half), F32 if k == 0 else BF16) for k in range(ZLO)),
        returned, marks, *shares, *table["back"],
    )
    total = parts[0]
    for k in range(1, ZLO):
        total = total + z_send(parts[k], REACH[k]).astype(F32)
    low, high = total[:, :quarter], total[:, quarter:]
    lower = z_hi == 0
    sent = jnp.where(lower, high, low).astype(BF16)
    moe_out = jnp.where(lower, low, high) + lax.ppermute(sent, "zh", SWAP).astype(F32)
    attn_out = attention_block(queries, cache, lengths)
    return (moe_out.astype(BF16), attn_out)


def solution(mesh):
    fine = Mesh(mesh.devices.reshape(4, 2, 2, 4, 2, 2), ("y", "xh", "xl", "zl", "zh", "c"))
    grp, tp = ("y", "xh", "xl", "zl"), ("zh", "c")
    every = grp + tp
    return jax.shard_map(
        shards,
        mesh=fine,
        in_specs=(
            P(grp, None),
            P(grp, None),
            P(),
            P(None, every),
            P(None, every),
            P(every, None),
            P(every, None),
            P(every, None, None),
            P(every),
        ),
        out_specs=(P(grp, tp), P(every, None)),
        check_vma=False,
    )
```

time: 529 us -> 150 us (0.28)
  waiting for transfers between devices: 281 us -> 42.6 us
  blocking collectives: 175 us -> 36.8 us
  starting transfers between devices: 10.3 us -> 29.8 us
  matrix products: 22.6 us -> 5.26 us
  between operations: 14.2 us -> 0.87 us
  Pallas kernels: 0 us -> 11.4 us
    reduce_scatter x1 -> x0, waiting for transfers between devices: 202 us -> none  [shards(): lax.psum_scatter(partial_value, 'tp', scatter_dimension=2, tiled=True)]
    all_to_all x1, blocking collectives: 175 us -> 36.8 us  [shards(): lax.all_to_all(packed.reshape(PLANE, BLOCK, width), ('y', 'xh', 'xl'), 0,...]
    all_to_all x1, waiting for transfers between devices: 78.7 us -> 25.4 us  [shards(): lax.all_to_all(summed.reshape(PLANE, BLOCK, width), ('y', 'xh', 'xl'), 0,...]
    ppermute x0 -> x12, starting transfers between devices: none -> 25.8 us  [the longest x9 21 us: z_send(): return lax.ppermute(value, ('zl', 'zh'), z_pairs(step))]
    reshape x2 -> x0, local copies, waits for them, and re-layouts: 18.8 us -> none  [the longest x1 10.6 us: shards(): jnp.dot(hidden, w_down, preferred_element_type=jnp.float32)]
    dot_general x6 -> x2, matrix products: 20 us -> 2.62 us  [the longest x1 2.06 us: attention_block(): jnp.einsum('bhp,bpd->bhd', weights.astype(BF16), value_block, preferred_e...]
    ppermute x0 -> x12, waiting for transfers between devices: none -> 17.2 us  [the longest x9 11.8 us: z_send(): return lax.ppermute(value, ('zl', 'zh'), z_pairs(step))]
    unnamed x14 -> x41, local copies, waits for them, and re-layouts: 1.71 us -> 18.6 us
  transfers between devices with their start and end apart: 2 -> 13, of which waited for: 2 -> 7; matrix products, arithmetic and copies ran while one was open for 1% -> 11% of each run, Pallas kernels for 0% -> 1%
where the time goes in v2:
time: 150 us; the launch traced here: 148 us
  waiting for transfers between devices  42.6 us (28%)
  blocking collectives  36.8 us (25%)
  starting transfers between devices  29.8 us (20%)
  local copies, waits for them, and re-layouts  19.5 us (13%)
  Pallas kernels  11.4 us (8%)
  matrix products  5.26 us (4%)
  other arithmetic  1.83 us (1%)
    all_to_all x1, blocking collectives, shards(): lax.all_to_all(packed.reshape(PLANE, BLOCK, width), ('y', 'xh', 'xl'), 0,...  36.8 us
    all_to_all x1, waiting for transfers between devices, shards(): lax.all_to_all(summed.reshape(PLANE, BLOCK, width), ('y', 'xh', 'xl'), 0,...  25.4 us
    ppermute x9, starting transfers between devices, z_send(): return lax.ppermute(value, ('zl', 'zh'), z_pairs(step))  21 us
    unnamed x41, local copies, waits for them, and re-layouts  18.6 us
    ppermute x9, waiting for transfers between devices, z_send(): return lax.ppermute(value, ('zl', 'zh'), z_pairs(step))  11.8 us
    pallas_call x5, Pallas kernels, call(): pl.pallas_call(kernel, out_shape=out_shape, in_specs=at, out_specs=jax.tr...  11.4 us
    ppermute x1, starting transfers between devices, shards(): lax.ppermute(sent, 'zh', SWAP).astype(F32)  4.29 us
    ppermute x1, waiting for transfers between devices, shards(): got = lax.ppermute(away, 'c', SWAP)  4.07 us
  transfers between devices with their start and end apart: 13, of which 7 were waited for; matrix products, arithmetic and copies ran while one was open for 11% of the time, Pallas kernels for 1%

profile of v2, /device:TPU:32, one launch (start us, length us, event | category | flops | bytes accessed | tf_op | source)
XLA Modules:
  0.0 148.1 jit_solution(3339320801988240826)
XLA Ops:
  0.6 0.0 copy-start
  0.7 0.8 and_reduce_fusion
  1.5 0.1 select_reduce_fusion
  1.6 0.9 constant_dynamic-slice_fusion.1
  2.5 1.9 %collective-permute-start = (bf16[16,3712]{1,0:T(8,128)(2,1)S(1)}, bf16[16,3712]{1,0:T(8,128)(2,1)S(1)}, u32[]{:S(2)}, u32[]{:S(2)}) collective-permute-start(bf16[16,3712]{1,0:T(8,128)(2,1)S(1)} %pad_maximum_fusion.refs_0_), channel_id=1, source_target_pairs={{0,14},{4,0},{8,4},{12,8},{2,12},{6,2},{10,6},{14,10},{1,15},{5,1}... | collective-permute-start | bytes 356360 | tf_op jit(solution)/shard_map/ppermute | solution.py:37
  4.4 4.6 %collective-permute-start.1 = (bf16[16,3712]{1,0:T(8,128)(2,1)S(1)}, bf16[16,3712]{1,0:T(8,128)(2,1)S(1)}, u32[]{:S(2)}, u32[]{:S(2)}) collective-permute-start(bf16[16,3712]{1,0:T(8,128)(2,1)S(1)} %pad_maximum_fusion.refs_0_), channel_id=1, source_target_pairs={{0,10},{4,14},{8,0},{12,4},{2,8},{6,12},{10,2},{14,6},{1,11},{5,15... | collective-permute-start | bytes 356360 | tf_op jit(solution)/shard_map/ppermute | solution.py:37
  9.0 1.0 collective-permute-start.2
  10.0 3.8 %collective-permute-done.1.refs_2_ = bf16[16,3712]{1,0:T(8,128)(2,1)S(1)} collective-permute-done((bf16[16,3712]{1,0:T(8,128)(2,1)S(1)}, bf16[16,3712]{1,0:T(8,128)(2,1)S(1)}, u32[]{:S(2)}, u32[]{:S(2)}) %collective-permute-start.1) | collective-permute-done | bytes 118816 | tf_op jit(solution)/shard_map/ppermute | solution.py:37
  13.8 0.0 collective-permute-done.2.refs_3_
  13.8 0.8 copy-done.8
  14.7 0.8 copy-done.13
  15.4 0.8 copy-done.14
  16.2 0.8 copy-done.15
  17.0 0.7 shard_map.203
  17.7 36.8 %all_to_all.10 = bf16[16,16,4480]{2,1,0:T(8,128)(2,1)S(1)} all-to-all(bf16[16,16,4480]{2,1,0:T(8,128)(2,1)S(1)} %bitcast.20), channel_id=1, replica_groups=mesh['y'=4,'xh'=2,'xl'=2,'zl'=4,'zh'=2,'c'=2] {'y','xh','xl'}, dimensions={0} | all-to-all | bytes 4587520 | tf_op jit(solution)/shard_map/all_to_all | solution.py:262
  54.5 4.6 %copy.31.w_gate = bf16[7168,160]{1,0:T(8,128)(2,1)} copy(bf16[7168,160]{0,1:T(8,128)(2,1)} %param.23) | data formatting | bytes 4587520 | tf_op args[3]
  59.2 4.7 %copy.32.w_up = bf16[7168,160]{1,0:T(8,128)(2,1)} copy(bf16[7168,160]{0,1:T(8,128)(2,1)} %param.24) | data formatting | bytes 4587520 | tf_op args[4]
  63.8 2.0 %copy-done.1 = bf16[7168,160]{1,0:T(8,128)(2,1)S(1)} copy-done((bf16[7168,160]{1,0:T(8,128)(2,1)S(1)}, bf16[7168,160]{1,0:T(8,128)(2,1)}, u32[]{:S(2)}) %copy-start.1) | copy-done | bytes 2293784
  65.9 2.0 %copy-done.3 = bf16[7168,160]{1,0:T(8,128)(2,1)S(1)} copy-done((bf16[7168,160]{1,0:T(8,128)(2,1)S(1)}, bf16[7168,160]{1,0:T(8,128)(2,1)}, u32[]{:S(2)}) %copy-start.3) | copy-done | bytes 2293784
  67.9 1.5 shard_map.204
  69.4 0.5 copy-done.2
  69.9 0.7 copy-done.4
  70.7 5.2 %shard_map.205 = (bf16[320,160]{1,0:T(8,128)(2,1)S(1)}, bf16[256,4480]{1,0:T(8,128)(2,1)S(1)}) custom-call(s32[1]{0:T(128)} %bitcast.core, bf16[256,4480]{1,0:T(8,128)(2,1)} %collective-permute-done.3.block, bf16[256,256]{1,0:T(8,128)(2,1)S(1)} %copy-done.6, bf16[256,256]{1,0:T(8,128)(2,1)S(1)} %copy-done.5, bf16[7168,160]{1,0:T(8,128)(2,1)S(1)} %copy-done.2, ...), custom_call_target="tpu_custom_call" | custom-call | tf_op jit(solution)/shard_map/pallas_call | solution.py:89
  75.8 0.6 collective-permute-start.4
  76.4 4.1 %collective-permute-done.4.got = bf16[256,4480]{1,0:T(8,128)(2,1)S(1)} collective-permute-done((bf16[256,4480]{1,0:T(8,128)(2,1)S(1)}, bf16[256,4480]{1,0:T(8,128)(2,1)S(1)}, u32[]{:S(2)}, u32[]{:S(2)}) %collective-permute-start.4) | collective-permute-done | bytes 2293792 | tf_op jit(solution)/shard_map/ppermute | solution.py:279
  80.5 2.6 %shard_map.206 = bf16[256,4480]{1,0:T(8,128)(2,1)} custom-call(s32[1]{0:T(128)} %bitcast.core, bf16[320,160]{1,0:T(8,128)(2,1)S(1)} %get-tuple-element.15.hidden, bf16[256,256]{1,0:T(8,128)(2,1)S(1)} %copy-done.5, bf16[160,7168]{1,0:T(8,128)(2,1)S(1)} %copy-done.4, bf16[256,4480]{1,0:T(8,128)(2,1)S(1)} %collective-permute-done.4.got), custom_call_target="tpu_custom_call" | custom-call | tf_op jit(solution)/shard_map/pallas_call | solution.py:89
  83.1 0.0 copy-start.9
  83.1 0.0 copy-start.10
  83.1 3.9 %all-to-all-start.1 = ((bf16[16,16,4480]{2,1,0:T(8,128)(2,1)}), bf16[16,16,4480]{2,1,0:T(8,128)(2,1)S(1)}, u32[]{:S(2)}, u32[]{:S(2)}) async-start(bf16[16,16,4480]{2,1,0:T(8,128)(2,1)} %bitcast.3), calls=%async_computation.1 | async-start | bytes 4587520 | tf_op jit(solution)/shard_map/all_to_all | solution.py:285
  87.1 0.1 copy.35
  87.2 0.6 select_reduce_fusion.1
  87.7 0.1 divide_select_fusion
  87.8 2.3 %collective-permute-start.5 = (f32[16,128]{1,0:T(8,128)S(1)}, f32[16,128]{1,0:T(8,128)S(1)}, u32[]{:S(2)}, u32[]{:S(2)}) collective-permute-start(f32[16,128]{1,0:T(8,128)S(1)} %pad.4.refs_2_), channel_id=1, source_target_pairs={{0,14},{4,0},{8,4},{12,8},{2,12},{6,2},{10,6},{14,10},{1,15},{5,1}... | collective-permute-start | bytes 24584 | tf_op jit(solution)/shard_map/ppermute | solution.py:37
  90.2 4.8 %collective-permute-start.6 = (f32[16,128]{1,0:T(8,128)S(1)}, f32[16,128]{1,0:T(8,128)S(1)}, u32[]{:S(2)}, u32[]{:S(2)}) collective-permute-start(f32[16,128]{1,0:T(8,128)S(1)} %pad.4.refs_2_), channel_id=1, source_target_pairs={{0,10},{4,14},{8,0},{12,4},{2,8},{6,12},{10,2},{14,6},{1,11},{5,15... | collective-permute-start | bytes 24584 | tf_op jit(solution)/shard_map/ppermute | solution.py:37
  95.0 0.1 iota_compare_fusion
  95.1 1.3 collective-permute-done.6.refs_4_
  96.3 2.3 %collective-permute-done.7.refs_5_ = f32[16,128]{1,0:T(8,128)S(1)} collective-permute-done((f32[16,128]{1,0:T(8,128)S(1)}, f32[16,128]{1,0:T(8,128)S(1)}, u32[]{:S(2)}, u32[]{:S(2)}) %collective-permute-start.7) | collective-permute-done | bytes 8224 | tf_op jit(solution)/shard_map/ppermute | solution.py:37
  98.6 25.4 %all-to-all-done.1 = bf16[16,16,4480]{2,1,0:T(8,128)(2,1)S(1)} async-done(((bf16[16,16,4480]{2,1,0:T(8,128)(2,1)}), bf16[16,16,4480]{2,1,0:T(8,128)(2,1)S(1)}, u32[]{:S(2)}, u32[]{:S(2)}) %all-to-all-start.1) | async-done | bytes 2293792 | tf_op jit(solution)/shard_map/all_to_all | solution.py:285
  124.0 1.5 %shard_map.207 = (f32[16,3584]{1,0:T(8,128)S(1)}, bf16[16,3584]{1,0:T(8,128)(2,1)S(1)}, bf16[16,3584]{1,0:T(8,128)(2,1)S(1)}, bf16[16,3584]{1,0:T(8,128)(2,1)S(1)}) custom-call(bf16[256,4480]{1,0:T(8,128)(2,1)S(1)} %bitcast.19, bf16[64,128]{1,0:T(8,128)(2,1)S(1)} %get-tuple-element.17.refs_1_, f32[16,128]{1,0:T(8,128)S(1)} %pad.4.refs_2_, ...), custom_call_target="tpu_custom_call" | custom-call | tf_op jit(solution)/shard_map/pallas_call | solution.py:89
  125.6 2.6 %collective-permute-start.10 = (bf16[16,3584]{1,0:T(8,128)(2,1)S(1)}, bf16[16,3584]{1,0:T(8,128)(2,1)S(1)}, u32[]{:S(2)}, u32[]{:S(2)}) collective-permute-start(bf16[16,3584]{1,0:T(8,128)(2,1)S(1)} %get-tuple-element.21), channel_id=1, source_target_pairs={{0,14},{4,0},{8,4},{12,8},{2,12},{6,2},{10,6},{14,10},{1,15},{5,1}... | collective-permute-start | bytes 344072 | tf_op jit(solution)/shard_map/ppermute | solution.py:37
  128.1 3.8 %collective-permute-start.9 = (bf16[16,3584]{1,0:T(8,128)(2,1)S(1)}, bf16[16,3584]{1,0:T(8,128)(2,1)S(1)}, u32[]{:S(2)}, u32[]{:S(2)}) collective-permute-start(bf16[16,3584]{1,0:T(8,128)(2,1)S(1)} %get-tuple-element.20), channel_id=1, source_target_pairs={{0,8},{4,12},{8,2},{12,6},{2,10},{6,14},{10,0},{14,4},{1,9},{5,13}... | collective-permute-start | bytes 344072 | tf_op jit(solution)/shard_map/ppermute | solution.py:37
  131.9 2.6 %fusion.29 = (f32[4,64]{1,0:T(4,128)S(1)}, bf16[4,64,1024]{2,1,0:T(8,128)(2,1)S(1)}) fusion(pred[4,1024]{1,0:T(4,128)(4,1)S(1)} %iota_compare_fusion, bf16[4,1024,512]{2,1,0:T(8,128)(2,1)} %param.27, bf16[1,4,64,256]{3,1,2,0:T(4,128)(2,1)} %bitcast.22), kind=kOutput, calls=%fused_computation.40 | convolution fusion | flops 135791616 | bytes 2761728 | tf_op jit(solution)/shard_map/sub | solution.py:220
  134.6 4.4 %collective-permute-done.9 = bf16[16,3584]{1,0:T(8,128)(2,1)S(1)} collective-permute-done((bf16[16,3584]{1,0:T(8,128)(2,1)S(1)}, bf16[16,3584]{1,0:T(8,128)(2,1)S(1)}, u32[]{:S(2)}, u32[]{:S(2)}) %collective-permute-start.9) | collective-permute-done | bytes 114720 | tf_op jit(solution)/shard_map/ppermute | solution.py:37
  139.0 4.3 %collective-permute-start.11 = (bf16[16,1792]{1,0:T(8,128)(2,1)S(1)}, bf16[16,1792]{1,0:T(8,128)(2,1)S(1)}, u32[]{:S(2)}, u32[]{:S(2)}) collective-permute-start(bf16[16,1792]{1,0:T(8,128)(2,1)S(1)} %select_convert_fusion), channel_id=1, source_target_pairs={{0,2},{2,0},{1,3},{3,1},{4,6},{6,4},{5,7},{7,5},{8,10},{10,8},{9,1... | collective-permute-start | bytes 172040 | tf_op jit(solution)/shard_map/ppermute | solution.py:307
  143.3 2.1 %fusion.20 = bf16[1,4,64,256]{3,2,1,0:T(8,128)(2,1)S(1)} fusion(bf16[4,1024,512]{2,1,0:T(8,128)(2,1)} %param.27, bf16[4,64,1024]{2,1,0:T(8,128)(2,1)S(1)} %get-tuple-element.27, f32[4,64]{1,0:T(4,128)S(1)} %get-tuple-element.26), kind=kOutput, calls=%fused_computation.12 | convolution fusion | flops 134348800 | bytes 2753536 | tf_op jit(solution)/shard_map/bhp,bpd->bhd/dot_general | solution.py:222
  145.4 0.8 copy.38
  146.1 1.3 collective-permute-done.11
  147.5 0.6 add_convert_fusion
  (45 shorter events, 0.2 us)
Async XLA Ops:
  0.6 86.5 %copy-start = (f32[7168,8]{0,1:T(8,128)S(1)}, f32[7168,8]{0,1:T(8,128)}, u32[]{:S(2)}) copy-start(f32[7168,8]{0,1:T(8,128)} %param.22) | copy-start | bytes 688132
  2.5 7.5 %collective-permute-start = (bf16[16,3712]{1,0:T(8,128)(2,1)S(1)}, bf16[16,3712]{1,0:T(8,128)(2,1)S(1)}, u32[]{:S(2)}, u32[]{:S(2)}) collective-permute-start(bf16[16,3712]{1,0:T(8,128)(2,1)S(1)} %pad_maximum_fusion.refs_0_), channel_id=1, source_target_pairs={{0,14},{4,0},{8,4},{12,8},{2,12},{6,2},{10,6},{14,10},{1,15},{5,1}... | collective-permute-start | bytes 356360 | tf_op jit(solution)/shard_map/ppermute | solution.py:37
  4.4 9.4 %collective-permute-start.1 = (bf16[16,3712]{1,0:T(8,128)(2,1)S(1)}, bf16[16,3712]{1,0:T(8,128)(2,1)S(1)}, u32[]{:S(2)}, u32[]{:S(2)}) collective-permute-start(bf16[16,3712]{1,0:T(8,128)(2,1)S(1)} %pad_maximum_fusion.refs_0_), channel_id=1, source_target_pairs={{0,10},{4,14},{8,0},{12,4},{2,8},{6,12},{10,2},{14,6},{1,11},{5,15... | collective-permute-start | bytes 356360 | tf_op jit(solution)/shard_map/ppermute | solution.py:37
  9.0 4.8 %collective-permute-start.2 = (bf16[16,3712]{1,0:T(8,128)(2,1)S(1)}, bf16[16,3712]{1,0:T(8,128)(2,1)S(1)}, u32[]{:S(2)}, u32[]{:S(2)}) collective-permute-start(bf16[16,3712]{1,0:T(8,128)(2,1)S(1)} %pad_maximum_fusion.refs_0_), channel_id=1, source_target_pairs={{0,4},{4,8},{8,12},{12,2},{2,6},{6,10},{10,14},{14,0},{1,5},{5,9},... | collective-permute-start | bytes 356360 | tf_op jit(solution)/shard_map/ppermute | solution.py:37
  13.8 0.8 copy-start.8
  14.7 0.8 copy-start.13
  15.4 0.8 copy-start.14
  16.2 0.8 copy-start.15
  54.5 14.9 %collective-permute-start.3 = (bf16[256,4480]{1,0:T(8,128)(2,1)S(1)}, bf16[256,4480]{1,0:T(8,128)(2,1)}, u32[]{:S(2)}, u32[]{:S(2)}) collective-permute-start(bf16[256,4480]{1,0:T(8,128)(2,1)S(1)} %bitcast.17), channel_id=1, source_target_pairs={{0,1},{1,0},{2,3},{3,2},{4,5},{5,4},{6,7},{7,6},{8,9},{9,8},{10,11... | collective-permute-start | bytes 6881288 | tf_op jit(solution)/shard_map/ppermute | solution.py:265
  59.2 4.7 %copy-start.6 = (bf16[256,256]{1,0:T(8,128)(2,1)S(1)}, bf16[256,256]{1,0:T(8,128)(2,1)}, u32[]{:S(2)}) copy-start(bf16[256,256]{1,0:T(8,128)(2,1)} %constant.77.clone.shuffle) | copy-start | bytes 393220
  63.8 2.0 %copy-start.1 = (bf16[7168,160]{1,0:T(8,128)(2,1)S(1)}, bf16[7168,160]{1,0:T(8,128)(2,1)}, u32[]{:S(2)}) copy-start(bf16[7168,160]{1,0:T(8,128)(2,1)} %copy.31.w_gate) | copy-start | bytes 6881284
  65.9 2.0 %copy-start.3 = (bf16[7168,160]{1,0:T(8,128)(2,1)S(1)}, bf16[7168,160]{1,0:T(8,128)(2,1)}, u32[]{:S(2)}) copy-start(bf16[7168,160]{1,0:T(8,128)(2,1)} %copy.32.w_up) | copy-start | bytes 6881284
  67.9 2.0 %copy-start.2 = (bf16[7168,160]{1,0:T(8,128)(2,1)S(1)}, bf16[7168,160]{1,0:T(8,128)(2,1)}, u32[]{:S(2)}) copy-start(bf16[7168,160]{1,0:T(8,128)(2,1)} %copy.31.w_gate) | copy-start | bytes 6881284
  67.9 2.8 %copy-start.4 = (bf16[160,7168]{1,0:T(8,128)(2,1)S(1)}, bf16[160,7168]{1,0:T(8,128)(2,1)}, u32[]{:S(2)}) copy-start(bf16[160,7168]{1,0:T(8,128)(2,1)} %w_down.3) | copy-start | bytes 6881284
  67.9 2.8 %copy-start.5 = (bf16[256,256]{1,0:T(8,128)(2,1)S(1)}, bf16[256,256]{1,0:T(8,128)(2,1)}, u32[]{:S(2)}) copy-start(bf16[256,256]{1,0:T(8,128)(2,1)} %constant.78.clone.unshuffle) | copy-start | bytes 393220
  75.8 4.7 %collective-permute-start.4 = (bf16[256,4480]{1,0:T(8,128)(2,1)S(1)}, bf16[256,4480]{1,0:T(8,128)(2,1)S(1)}, u32[]{:S(2)}, u32[]{:S(2)}) collective-permute-start(bf16[256,4480]{1,0:T(8,128)(2,1)S(1)} %get-tuple-element.16), channel_id=1, source_target_pairs={{0,1},{1,0},{2,3},{3,2},{4,5},{5,4},{6,7},{7,6},{8,9},{9,8},{10,11... | collective-permute-start | bytes 6881288 | tf_op jit(solution)/shard_map/ppermute | solution.py:279
  83.1 4.0 %copy-start.17 = (s32[16,2]{0,1:T(2,128)S(1)}, s32[16,2]{0,1:T(2,128)}, u32[]{:S(2)}) copy-start(s32[16,2]{0,1:T(2,128)} %param.21) | copy-start | bytes 388
  83.1 4.1 %copy-start.16 = (bf16[16,7168]{1,0:T(8,128)(2,1)S(1)}, bf16[16,7168]{1,0:T(8,128)(2,1)}, u32[]{:S(2)}) copy-start(bf16[16,7168]{1,0:T(8,128)(2,1)} %param.20) | copy-start | bytes 688132
  83.1 11.9 %copy-start.18 = (s32[4]{0:T(128)S(1)}, s32[4]{0:T(128)}, u32[]{:S(2)}) copy-start(s32[4]{0:T(128)} %param.28) | copy-start | bytes 52
  83.1 41.0 %copy-start.7 = (bf16[4,64,256]{2,1,0:T(8,128)(2,1)S(1)}, bf16[4,64,256]{2,1,0:T(8,128)(2,1)}, u32[]{:S(2)}) copy-start(bf16[4,64,256]{2,1,0:T(8,128)(2,1)} %constant.82.clone.refs_9_) | copy-start | bytes 393220
  83.1 41.0 %copy-start.9 = (bf16[128,256]{1,0:T(8,128)(2,1)S(1)}, bf16[128,256]{1,0:T(8,128)(2,1)}, u32[]{:S(2)}) copy-start(bf16[128,256]{1,0:T(8,128)(2,1)} %constant.79.clone.refs_6_) | copy-start | bytes 196612
  83.1 40.9 %copy-start.10 = (bf16[128,256]{1,0:T(8,128)(2,1)S(1)}, bf16[128,256]{1,0:T(8,128)(2,1)}, u32[]{:S(2)}) copy-start(bf16[128,256]{1,0:T(8,128)(2,1)} %constant.81.clone.refs_8_) | copy-start | bytes 196612
  83.1 40.9 %copy-start.11 = (bf16[128,256]{1,0:T(8,128)(2,1)S(1)}, bf16[128,256]{1,0:T(8,128)(2,1)}, u32[]{:S(2)}) copy-start(bf16[128,256]{1,0:T(8,128)(2,1)} %constant.83.clone.refs_10_) | copy-start | bytes 196612
  83.1 40.9 %copy-start.12 = (bf16[64,256]{1,0:T(8,128)(2,1)S(1)}, bf16[64,256]{1,0:T(8,128)(2,1)}, u32[]{:S(2)}) copy-start(bf16[64,256]{1,0:T(8,128)(2,1)} %constant.80.clone.refs_7_) | copy-start | bytes 98308
  83.1 40.9 %all-to-all-start.1 = ((bf16[16,16,4480]{2,1,0:T(8,128)(2,1)}), bf16[16,16,4480]{2,1,0:T(8,128)(2,1)S(1)}, u32[]{:S(2)}, u32[]{:S(2)}) async-start(bf16[16,16,4480]{2,1,0:T(8,128)(2,1)} %bitcast.3), calls=%async_computation.1 | async-start | bytes 4587520 | tf_op jit(solution)/shard_map/all_to_all | solution.py:285
  87.8 7.2 %collective-permute-start.5 = (f32[16,128]{1,0:T(8,128)S(1)}, f32[16,128]{1,0:T(8,128)S(1)}, u32[]{:S(2)}, u32[]{:S(2)}) collective-permute-start(f32[16,128]{1,0:T(8,128)S(1)} %pad.4.refs_2_), channel_id=1, source_target_pairs={{0,14},{4,0},{8,4},{12,8},{2,12},{6,2},{10,6},{14,10},{1,15},{5,1}... | collective-permute-start | bytes 24584 | tf_op jit(solution)/shard_map/ppermute | solution.py:37
  90.2 6.2 %collective-permute-start.6 = (f32[16,128]{1,0:T(8,128)S(1)}, f32[16,128]{1,0:T(8,128)S(1)}, u32[]{:S(2)}, u32[]{:S(2)}) collective-permute-start(f32[16,128]{1,0:T(8,128)S(1)} %pad.4.refs_2_), channel_id=1, source_target_pairs={{0,10},{4,14},{8,0},{12,4},{2,8},{6,12},{10,2},{14,6},{1,11},{5,15... | collective-permute-start | bytes 24584 | tf_op jit(solution)/shard_map/ppermute | solution.py:37
  95.0 3.7 %collective-permute-start.7 = (f32[16,128]{1,0:T(8,128)S(1)}, f32[16,128]{1,0:T(8,128)S(1)}, u32[]{:S(2)}, u32[]{:S(2)}) collective-permute-start(f32[16,128]{1,0:T(8,128)S(1)} %pad.4.refs_2_), channel_id=1, source_target_pairs={{0,4},{4,8},{8,12},{12,2},{2,6},{6,10},{10,14},{14,0},{1,5},{5,9},... | collective-permute-start | bytes 24584 | tf_op jit(solution)/shard_map/ppermute | solution.py:37
  125.6 9.0 %collective-permute-start.10 = (bf16[16,3584]{1,0:T(8,128)(2,1)S(1)}, bf16[16,3584]{1,0:T(8,128)(2,1)S(1)}, u32[]{:S(2)}, u32[]{:S(2)}) collective-permute-start(bf16[16,3584]{1,0:T(8,128)(2,1)S(1)} %get-tuple-element.21), channel_id=1, source_target_pairs={{0,14},{4,0},{8,4},{12,8},{2,12},{6,2},{10,6},{14,10},{1,15},{5,1}... | collective-permute-start | bytes 344072 | tf_op jit(solution)/shard_map/ppermute | solution.py:37
  128.1 6.4 %collective-permute-start.8 = (bf16[16,3584]{1,0:T(8,128)(2,1)S(1)}, bf16[16,3584]{1,0:T(8,128)(2,1)S(1)}, u32[]{:S(2)}, u32[]{:S(2)}) collective-permute-start(bf16[16,3584]{1,0:T(8,128)(2,1)S(1)} %get-tuple-element.19), channel_id=1, source_target_pairs={{0,4},{4,8},{8,12},{12,2},{2,6},{6,10},{10,14},{14,0},{1,5},{5,9},... | collective-permute-start | bytes 344072 | tf_op jit(solution)/shard_map/ppermute | solution.py:37
  128.1 10.8 %collective-permute-start.9 = (bf16[16,3584]{1,0:T(8,128)(2,1)S(1)}, bf16[16,3584]{1,0:T(8,128)(2,1)S(1)}, u32[]{:S(2)}, u32[]{:S(2)}) collective-permute-start(bf16[16,3584]{1,0:T(8,128)(2,1)S(1)} %get-tuple-element.20), channel_id=1, source_target_pairs={{0,8},{4,12},{8,2},{12,6},{2,10},{6,14},{10,0},{14,4},{1,9},{5,13}... | collective-permute-start | bytes 344072 | tf_op jit(solution)/shard_map/ppermute | solution.py:37
  139.0 8.4 %collective-permute-start.11 = (bf16[16,1792]{1,0:T(8,128)(2,1)S(1)}, bf16[16,1792]{1,0:T(8,128)(2,1)S(1)}, u32[]{:S(2)}, u32[]{:S(2)}) collective-permute-start(bf16[16,1792]{1,0:T(8,128)(2,1)S(1)} %select_convert_fusion), channel_id=1, source_target_pairs={{0,2},{2,0},{1,3},{3,1},{4,6},{6,4},{5,7},{7,5},{8,10},{10,8},{9,1... | collective-permute-start | bytes 172040 | tf_op jit(solution)/shard_map/ppermute | solution.py:307

commit v3 on v2

--- a/solution.py
+++ b/solution.py
@@ -3,7 +3,6 @@
 
 import jax
 import jax.numpy as jnp
-import numpy as np
 from jax import lax
 from jax.experimental import pallas as pl
 from jax.experimental.pallas import tpu as pltpu
@@ -37,43 +36,31 @@
     return lax.ppermute(value, ("zl", "zh"), z_pairs(step))
 
 
-def as_bf16(array):
-    return jnp.asarray(np.asarray(array, np.float32), BF16)
-
-
-def tables():
-    lane = np.arange(LANES)
-    lane_e = np.where(lane < EXPERTS * CAP, lane // CAP, -1)
-    lane_s = lane % CAP
-    e, u = np.divmod(np.arange(EXPERTS * BLOCK), BLOCK)
-    k64 = np.arange(ZLO * BLOCK) // BLOCK
-    pick_main = (lane_e[None] == e[:, None]) & (lane_s[None] == (u % CAP)[:, None])
-    mask_main = (u // CAP)[:, None] == k64[None]
-    g, s = np.divmod(u, 4)
-    pick_rest = (lane_e[None] == e[:, None]) & (lane_s[None] == ((16 + s) % CAP)[:, None])
-    g256 = np.arange(4 * 64) // 64
-    k256 = np.tile(k64, 4)
-    mask_rest = (g[:, None] == g256[None]) & (((16 + s) // CAP)[:, None] == k256[None])
-    row = np.arange(PLANE * BLOCK)
-    src, gs = np.divmod(row, BLOCK)
-    spot = (gs // 4) * 64 + src * 4 + gs % 4
-    shuffle = np.zeros((PLANE * BLOCK, PLANE * BLOCK))
-    shuffle[spot, row] = 1
-    e2, u2 = row // (2 * BLOCK), row % BLOCK
-    back_main = (lane_e[:, None] == e2[None]) & (lane_s[:, None] == (u2 % CAP)[None])
-    back_mask = k64[:, None] == (u2 // CAP)[None]
-    g2, s2 = np.divmod(u2, 4)
-    back_rest = (lane_e[:, None] == e2[None]) & (lane_s[:, None] == ((16 + s2) % CAP)[None])
-    back_rest_mask = np.stack(
-        [(g2[None] == i) & (k64[:, None] == ((16 + s2) // CAP)[None]) for i in range(4)]
-    )
-    spread = lane[:, None] == e2[None]
-    return dict(
-        pack=[as_bf16(a) for a in (pick_main, mask_main, pick_rest, mask_rest)],
-        shuffle=as_bf16(shuffle),
-        unshuffle=as_bf16(shuffle.T),
-        back=[as_bf16(a) for a in (back_main, back_mask, back_rest, back_rest_mask, spread)],
-    )
+def grid(rows, columns):
+    return (
+        lax.broadcasted_iota(jnp.int32, (rows, columns), 0),
+        lax.broadcasted_iota(jnp.int32, (rows, columns), 1),
+    )
+
+
+def fifth(value):
+    return (value * 205) >> 10
+
+
+def fifth_rest(value):
+    return value - CAP * fifth(value)
+
+
+def ones(condition):
+    return jnp.where(condition, 1.0, 0.0)
+
+
+def shuffle_table(back):
+    new, old = grid(PLANE * BLOCK, PLANE * BLOCK)
+    if back:
+        new, old = old, new
+    spot = ((old >> 2) & 3) * 64 + (old >> 4) * 4 + (old & 3)
+    return ones(new == spot).astype(BF16)
 
 
 def dot(a, b):
@@ -96,26 +83,34 @@
 
 
 def pack_kernel(quarter, *refs):
-    blocks, (pick_main, mask_main, pick_rest, mask_rest), (out, marks) = refs[:4], refs[4:8], refs[8:]
+    blocks, (out, marks) = refs[:4], refs[4:]
     half = 2 * quarter
     eighth = quarter // 2
     rows = jnp.concatenate([b[:, :half] for b in blocks], axis=0)
     chosen = jnp.concatenate([b[:, half:] for b in blocks], axis=0)
     marks[...] = chosen
-    select = (dot_t(pick_main[...], chosen) * mask_main[...].astype(F32)).astype(BF16)
-    main = dot(select, rows).astype(BF16).reshape(EXPERTS, BLOCK, half)
+    slot, lane = grid(EXPERTS * BLOCK, LANES)
+    same = fifth(lane) == slot >> 4
+    pick_main = ones(same & (fifth_rest(lane) == fifth_rest(slot & 15))).astype(BF16)
+    pick_rest = ones(same & (fifth_rest(lane) == 1 + (slot & 3))).astype(BF16)
+    slot, row = grid(EXPERTS * BLOCK, ZLO * BLOCK)
+    mask = ones(fifth(slot & 15) == row >> 4)
+    main = dot((dot_t(pick_main, chosen) * mask).astype(BF16), rows)
+    main = main.astype(BF16).reshape(EXPERTS, BLOCK, half)
     chosen4 = jnp.concatenate([chosen] * 4, axis=0)
     rows4 = jnp.concatenate([rows[:, i * eighth : (i + 1) * eighth] for i in range(4)], axis=0)
-    select = (dot_t(pick_rest[...], chosen4) * mask_rest[...].astype(F32)).astype(BF16)
-    rest = dot(select, rows4).astype(BF16).reshape(EXPERTS, BLOCK, eighth)
+    slot, row = grid(EXPERTS * BLOCK, 4 * ZLO * BLOCK)
+    mask = ones(((slot >> 2) & 3 == row >> 6) & ((row >> 4) & 3 == 3))
+    rest = dot((dot_t(pick_rest, chosen4) * mask).astype(BF16), rows4)
+    rest = rest.astype(BF16).reshape(EXPERTS, BLOCK, eighth)
     for x in range(2):
         out[:, x, :, :half] = main
         out[:, x, :, half:] = rest
 
 
-def experts_in(quarter, core, block, shuffle, w_gate, w_up):
-    half, eighth = 2 * quarter, quarter // 2
-    rest = dot(shuffle[...], block[:, half:]).astype(BF16)
+def experts_in(quarter, core, block, w_gate, w_up):
+    half = 2 * quarter
+    rest = dot(shuffle_table(False), block[:, half:]).astype(BF16)
     gate, up = 0.0, 0.0
     for f in range(2):
         top = block[:, f * quarter : (f + 1) * quarter]
@@ -124,8 +119,8 @@
         )
         rows = jnp.concatenate([top, tail], axis=0)
         at = pl.ds(pl.multiple_of(f * half + core * quarter, LANES), quarter)
-        gate = gate + dot(rows, w_gate[at, :])
-        up = up + dot(rows, w_up[at, :])
+        gate = gate + dot_t(rows, w_gate[:, at])
+        up = up + dot_t(rows, w_up[:, at])
     return gate, up
 
 
@@ -141,28 +136,28 @@
     return mains, jnp.concatenate(rests, axis=0)
 
 
-def own_kernel(quarter, core, block, shuffle, w_gate, w_up, gate_out, up_out):
-    gate, up = experts_in(quarter, core[0], block, shuffle, w_gate, w_up)
+def own_kernel(quarter, core, block, w_gate, w_up, gate_out, up_out):
+    gate, up = experts_in(quarter, core[0], block, w_gate, w_up)
     gate_out[...] = gate
     up_out[...] = up
 
 
 def other_kernel(
-    quarter, core, block, shuffle, unshuffle, w_gate, w_up, w_down, gate_in, up_in, hidden_out, away
+    quarter, core, block, w_gate, w_up, w_down, gate_in, up_in, hidden_out, away
 ):
     half = 2 * quarter
     there = 1 - core[0]
-    gate, up = experts_in(quarter, there, block, shuffle, w_gate, w_up)
+    gate, up = experts_in(quarter, there, block, w_gate, w_up)
     gate, up = gate + gate_in[...], up + up_in[...]
     hidden = (gate * jax.nn.sigmoid(gate) * up).astype(BF16)
     hidden_out[...] = hidden
     mains, rest = experts_out(quarter, there, hidden, w_down)
     for f in range(2):
         away[:, f * quarter : (f + 1) * quarter] = mains[f].astype(BF16)
-    away[:, half:] = dot(unshuffle[...], rest.astype(BF16)).astype(BF16)
-
-
-def sum_kernel(quarter, core, hidden, unshuffle, w_down, got, out):
+    away[:, half:] = dot(shuffle_table(True), rest.astype(BF16)).astype(BF16)
+
+
+def sum_kernel(quarter, core, hidden, w_down, got, out):
     half = 2 * quarter
     mains, rest = experts_out(quarter, core[0], hidden[...], w_down)
     for f in range(2):
@@ -170,30 +165,34 @@
         out[:, at] = (mains[f] + got[:, at].astype(F32)).astype(BF16)
     high = rest.astype(BF16)
     low = (rest - high.astype(F32)).astype(BF16)
-    rest = dot(unshuffle[...], high) + dot(unshuffle[...], low)
+    unshuffle = shuffle_table(True)
+    rest = dot(unshuffle, high) + dot(unshuffle, low)
     out[:, half:] = (rest + got[:, half:].astype(F32)).astype(BF16)
 
 
 def combine_kernel(quarter, *refs):
-    back, marks = refs[0], refs[1]
-    shares = refs[2:6]
-    back_main, back_mask, back_rest, back_rest_mask, spread = refs[6:11]
-    outs = refs[11:]
-    half, eighth = 2 * quarter, quarter // 2
+    back, marks, shares, outs = refs[0], refs[1], refs[2:6], refs[6:]
+    half = 2 * quarter
     share = jnp.concatenate([s[...] for s in shares], axis=0)
     high = share.astype(BF16)
     low = (share - high.astype(F32)).astype(BF16)
     chosen = marks[...]
-    main = dot(chosen, back_main[...]) * back_mask[...].astype(F32)
-    rest = dot(chosen, back_rest[...])
-    wide_high, wide_low = dot(high, spread[...]), dot(low, spread[...])
+    lane, slot = grid(LANES, PLANE * BLOCK)
+    same = fifth(lane) == slot >> 5
+    back_main = ones(same & (fifth_rest(lane) == fifth_rest(slot & 15))).astype(BF16)
+    back_rest = ones(same & (fifth_rest(lane) == 1 + (slot & 3))).astype(BF16)
+    spread = ones(lane == slot >> 5).astype(BF16)
+    row, slot = grid(ZLO * BLOCK, PLANE * BLOCK)
+    main = dot(chosen, back_main) * ones(fifth(slot & 15) == row >> 4)
+    rest = dot(chosen, back_rest) * ones(row >> 4 == 3)
+    wide_high, wide_low = dot(high, spread), dot(low, spread)
     total = dot((main * wide_high).astype(BF16), back[:, :half]) + dot(
         (main * wide_low).astype(BF16), back[:, :half]
     )
     tail = back[:, half:]
     pieces = []
     for i in range(4):
-        mask = rest * back_rest_mask[i].astype(F32)
+        mask = rest * ones((slot >> 2) & 3 == i)
         pieces.append(
             dot((mask * wide_high).astype(BF16), tail) + dot((mask * wide_low).astype(BF16), tail)
         )
@@ -226,10 +225,10 @@
 def shards(x_rows, route_ids, router, w_gate, w_up, w_down, queries, cache, lengths):
     model_width = x_rows.shape[1]
     hidden_count = w_gate.shape[1]
+    w_gate, w_up = w_gate.T, w_up.T
     quarter = model_width // 4
     half, eighth = 2 * quarter, quarter // 2
     width = half + eighth
-    table = tables()
     z_hi, core = lax.axis_index("zh"), lax.axis_index("c")
     core_ref = core.astype(jnp.int32).reshape(1)
 
@@ -257,7 +256,6 @@
             jax.ShapeDtypeStruct((ZLO * BLOCK, LANES), BF16),
         ),
         *blocks,
-        *table["pack"],
     )
     arrived = lax.all_to_all(
         packed.reshape(PLANE, BLOCK, width), ("y", "xh", "xl"), 0, 0, tiled=True
@@ -268,20 +266,22 @@
     gate, up = call(
         functools.partial(own_kernel, quarter),
         (partial, partial),
-        core_ref, arrived, table["shuffle"], w_gate, w_up,
+        core_ref, arrived, w_gate, w_up,
     )
     pieces = jax.ShapeDtypeStruct((PLANE * BLOCK, width), BF16)
     hidden, away = call(
         functools.partial(other_kernel, quarter),
         (jax.ShapeDtypeStruct((rows, hidden_count), BF16), pieces),
-        core_ref, beside, table["shuffle"], table["unshuffle"], w_gate, w_up, w_down, gate, up,
+        core_ref, beside, w_gate, w_up, w_down, gate, up,
     )
     got = lax.ppermute(away, "c", SWAP)
     summed = call(
         functools.partial(sum_kernel, quarter),
         pieces,
-        core_ref, hidden, table["unshuffle"], w_down, got,
-    )
+        core_ref, hidden, w_down, got,
+    )
+    summed, queries = lax.optimization_barrier((summed, queries))
+    attn_out = attention_block(queries, cache, lengths)
     returned = lax.all_to_all(
         summed.reshape(PLANE, BLOCK, width), ("y", "xh", "xl"), 0, 0, tiled=True
     ).reshape(PLANE * BLOCK, width)
@@ -293,10 +293,11 @@
     share = jnp.pad(jnp.where(picked, share, 0.0), ((0, 0), (0, LANES - EXPERTS)))
     shares = [share] + [z_send(share, -k) for k in REACH[1:]]
 
+    returned, attn_out = lax.optimization_barrier((returned, attn_out))
     parts = call(
         functools.partial(combine_kernel, quarter),
         tuple(jax.ShapeDtypeStruct((BLOCK, half), F32 if k == 0 else BF16) for k in range(ZLO)),
-        returned, marks, *shares, *table["back"],
+        returned, marks, *shares,
     )
     total = parts[0]
     for k in range(1, ZLO):
@@ -305,7 +306,6 @@
     lower = z_hi == 0
     sent = jnp.where(lower, high, low).astype(BF16)
     moe_out = jnp.where(lower, low, high) + lax.ppermute(sent, "zh", SWAP).astype(F32)
-    attn_out = attention_block(queries, cache, lengths)
     return (moe_out.astype(BF16), attn_out)
 
 

time: 150 us -> 132 us (0.88)
  local copies, waits for them, and re-layouts: 19.5 us -> 1.76 us
  waiting for transfers between devices: 42.6 us -> 45.6 us
  Pallas kernels: 11.4 us -> 8.75 us
    unnamed x41 -> x17, local copies, waits for them, and re-layouts: 18.6 us -> 0.8 us
    ppermute x1, waiting for transfers between devices: 0.01 us -> 2.93 us  [shards(): beside = lax.ppermute(arrived, 'c', SWAP)]
    ppermute x1, waiting for transfers between devices: 1.32 us -> 4.18 us  [shards(): lax.ppermute(sent, 'zh', SWAP).astype(F32)]
    pallas_call x5, Pallas kernels: 11.4 us -> 8.75 us  [call(): pl.pallas_call(kernel, out_shape=out_shape, in_specs=at, out_specs=jax.tr...]
    all_to_all x1, waiting for transfers between devices: 25.4 us -> 23 us  [shards(): lax.all_to_all(summed.reshape(PLANE, BLOCK, width), ('y', 'xh', 'xl'), 0,...]
  transfers between devices with their start and end apart: 13 -> 13, of which waited for: 7 -> 7; matrix products, arithmetic and copies ran while one was open for 11% -> 5% of each run, Pallas kernels for 1% -> 1%
where the time goes in v3:
time: 132 us; the launch traced here: 130 us
  waiting for transfers between devices  45.6 us (35%)
  blocking collectives  37.1 us (28%)
  starting transfers between devices  29.1 us (22%)
  Pallas kernels  8.75 us (7%)
  matrix products  5.16 us (4%)
  other arithmetic  1.84 us (1%)
  local copies, waits for them, and re-layouts  1.76 us (1%)
    all_to_all x1, blocking collectives, shards(): lax.all_to_all(packed.reshape(PLANE, BLOCK, width), ('y', 'xh', 'xl'), 0,...  37.1 us
    all_to_all x1, waiting for transfers between devices, shards(): lax.all_to_all(summed.reshape(PLANE, BLOCK, width), ('y', 'xh', 'xl'), 0,...  23 us
    ppermute x9, starting transfers between devices, z_send(): return lax.ppermute(value, ('zl', 'zh'), z_pairs(step))  21 us
    ppermute x9, waiting for transfers between devices, z_send(): return lax.ppermute(value, ('zl', 'zh'), z_pairs(step))  11.2 us
    pallas_call x5, Pallas kernels, call(): pl.pallas_call(kernel, out_shape=out_shape, in_specs=at, out_specs=jax.tr...  8.75 us
    ppermute x1, waiting for transfers between devices, shards(): got = lax.ppermute(away, 'c', SWAP)  4.3 us
    ppermute x1, waiting for transfers between devices, shards(): lax.ppermute(sent, 'zh', SWAP).astype(F32)  4.18 us
    ppermute x1, starting transfers between devices, shards(): lax.ppermute(sent, 'zh', SWAP).astype(F32)  3.99 us
  transfers between devices with their start and end apart: 13, of which 7 were waited for; matrix products, arithmetic and copies ran while one was open for 5% of the time, Pallas kernels for 1%

profile of v3, /device:TPU:32, one launch (start us, length us, event | category | flops | bytes accessed | tf_op | source)
XLA Modules:
  0.0 130.2 jit_solution(15165391741165521198)
XLA Ops:
  0.6 0.0 copy-start
  0.7 0.8 and_reduce_fusion
  1.5 0.1 select_reduce_fusion
  1.6 0.9 constant_dynamic-slice_fusion.1
  2.5 1.9 %collective-permute-start = (bf16[16,3712]{1,0:T(8,128)(2,1)S(1)}, bf16[16,3712]{1,0:T(8,128)(2,1)S(1)}, u32[]{:S(2)}, u32[]{:S(2)}) collective-permute-start(bf16[16,3712]{1,0:T(8,128)(2,1)S(1)} %pad_maximum_fusion.refs_0_), channel_id=1, source_target_pairs={{0,14},{4,0},{8,4},{12,8},{2,12},{6,2},{10,6},{14,10},{1,15},{5,1}... | collective-permute-start | bytes 356360 | tf_op jit(solution)/shard_map/ppermute | solution.py:36
  4.4 4.6 %collective-permute-start.1 = (bf16[16,3712]{1,0:T(8,128)(2,1)S(1)}, bf16[16,3712]{1,0:T(8,128)(2,1)S(1)}, u32[]{:S(2)}, u32[]{:S(2)}) collective-permute-start(bf16[16,3712]{1,0:T(8,128)(2,1)S(1)} %pad_maximum_fusion.refs_0_), channel_id=1, source_target_pairs={{0,10},{4,14},{8,0},{12,4},{2,8},{6,12},{10,2},{14,6},{1,11},{5,15... | collective-permute-start | bytes 356360 | tf_op jit(solution)/shard_map/ppermute | solution.py:36
  9.0 1.0 collective-permute-start.2
  10.0 0.0 collective-permute-done.refs_1_
  10.0 3.8 %collective-permute-done.1.refs_2_ = bf16[16,3712]{1,0:T(8,128)(2,1)S(1)} collective-permute-done((bf16[16,3712]{1,0:T(8,128)(2,1)S(1)}, bf16[16,3712]{1,0:T(8,128)(2,1)S(1)}, u32[]{:S(2)}, u32[]{:S(2)}) %collective-permute-start.1) | collective-permute-done | bytes 118816 | tf_op jit(solution)/shard_map/ppermute | solution.py:36
  13.8 0.0 collective-permute-done.2.refs_3_
  13.8 0.7 shard_map.104
  14.6 0.0 copy-start.2
  14.6 0.0 copy-start.3
  14.6 37.1 %all_to_all.10 = bf16[16,16,4480]{2,1,0:T(8,128)(2,1)S(1)} all-to-all(bf16[16,16,4480]{2,1,0:T(8,128)(2,1)S(1)} %bitcast.26), channel_id=1, replica_groups=mesh['y'=4,'xh'=2,'xl'=2,'zl'=4,'zh'=2,'c'=2] {'y','xh','xl'}, dimensions={0} | all-to-all | bytes 4587520 | tf_op jit(solution)/shard_map/all_to_all | solution.py:260
  51.7 0.0 collective-permute-start.3
  51.7 0.0 copy-start.1
  51.7 1.5 %shard_map.105 = (f32[320,160]{1,0:T(8,128)S(1)}, f32[320,160]{1,0:T(8,128)S(1)}) custom-call(s32[1]{0:T(128)} %bitcast.core, bf16[256,4480]{1,0:T(8,128)(2,1)S(1)} %bitcast.25, bf16[160,7168]{1,0:T(8,128)(2,1)S(1)} %bitcast.19, bf16[160,7168]{1,0:T(8,128)(2,1)S(1)} %bitcast.21), custom_call_target="tpu_custom_call" | custom-call | tf_op jit(solution)/shard_map/pallas_call | solution.py:76
  53.2 2.9 %collective-permute-done.3.block = bf16[256,4480]{1,0:T(8,128)(2,1)S(1)} collective-permute-done((bf16[256,4480]{1,0:T(8,128)(2,1)S(1)}, bf16[256,4480]{1,0:T(8,128)(2,1)S(1)}, u32[]{:S(2)}, u32[]{:S(2)}) %collective-permute-start.3) | collective-permute-done | bytes 2293792 | tf_op jit(solution)/shard_map/ppermute | solution.py:263
  56.1 2.4 %shard_map.106 = (bf16[320,160]{1,0:T(8,128)(2,1)S(1)}, bf16[256,4480]{1,0:T(8,128)(2,1)S(1)}) custom-call(s32[1]{0:T(128)} %bitcast.core, bf16[256,4480]{1,0:T(8,128)(2,1)S(1)} %collective-permute-done.3.block, bf16[160,7168]{1,0:T(8,128)(2,1)S(1)} %bitcast.20, bf16[160,7168]{1,0:T(8,128)(2,1)S(1)} %bitcast.22, bf16[160,7168]{1,0:T(8,128)(2,1)S(1)} %copy-done.1, ...), custom_call_target="tpu_custom_call" | custom-call | tf_op jit(solution)/shard_map/pallas_call | solution.py:76
  58.6 0.2 collective-permute-start.4
  58.8 4.3 %collective-permute-done.4.got = bf16[256,4480]{1,0:T(8,128)(2,1)S(1)} collective-permute-done((bf16[256,4480]{1,0:T(8,128)(2,1)S(1)}, bf16[256,4480]{1,0:T(8,128)(2,1)S(1)}, u32[]{:S(2)}, u32[]{:S(2)}) %collective-permute-start.4) | collective-permute-done | bytes 2293792 | tf_op jit(solution)/shard_map/ppermute | solution.py:277
  63.1 2.6 %shard_map.107 = bf16[256,4480]{1,0:T(8,128)(2,1)} custom-call(s32[1]{0:T(128)} %bitcast.core, bf16[320,160]{1,0:T(8,128)(2,1)S(1)} %get-tuple-element.19.hidden, bf16[160,7168]{1,0:T(8,128)(2,1)S(1)} %copy-done.1, bf16[256,4480]{1,0:T(8,128)(2,1)S(1)} %collective-permute-done.4.got), custom_call_target="tpu_custom_call" | custom-call | tf_op jit(solution)/shard_map/pallas_call | solution.py:76
  65.7 3.9 %all-to-all-start.1 = ((bf16[16,16,4480]{2,1,0:T(8,128)(2,1)}), bf16[16,16,4480]{2,1,0:T(8,128)(2,1)S(1)}, u32[]{:S(2)}, u32[]{:S(2)}) async-start(bf16[16,16,4480]{2,1,0:T(8,128)(2,1)} %bitcast.5), calls=%async_computation.1 | async-start | bytes 4587520 | tf_op jit(solution)/shard_map/all_to_all | solution.py:285
  69.7 0.1 copy.16
  69.8 0.5 select_reduce_fusion.1
  70.3 0.1 divide_select_fusion
  70.4 2.3 %collective-permute-start.5 = (f32[16,128]{1,0:T(8,128)S(1)}, f32[16,128]{1,0:T(8,128)S(1)}, u32[]{:S(2)}, u32[]{:S(2)}) collective-permute-start(f32[16,128]{1,0:T(8,128)S(1)} %pad.4.refs_2_), channel_id=1, source_target_pairs={{0,14},{4,0},{8,4},{12,8},{2,12},{6,2},{10,6},{14,10},{1,15},{5,1}... | collective-permute-start | bytes 24584 | tf_op jit(solution)/shard_map/ppermute | solution.py:36
  72.7 4.8 %collective-permute-start.6 = (f32[16,128]{1,0:T(8,128)S(1)}, f32[16,128]{1,0:T(8,128)S(1)}, u32[]{:S(2)}, u32[]{:S(2)}) collective-permute-start(f32[16,128]{1,0:T(8,128)S(1)} %pad.4.refs_2_), channel_id=1, source_target_pairs={{0,10},{4,14},{8,0},{12,4},{2,8},{6,12},{10,2},{14,6},{1,11},{5,15... | collective-permute-start | bytes 24584 | tf_op jit(solution)/shard_map/ppermute | solution.py:36
  77.5 0.0 collective-permute-start.7
  77.5 0.1 iota_compare_fusion
  77.6 2.6 %fusion.29 = (f32[4,64]{1,0:T(4,128)S(1)}, bf16[4,64,1024]{2,1,0:T(8,128)(2,1)S(1)}) fusion(pred[4,1024]{1,0:T(4,128)(4,1)S(1)} %iota_compare_fusion, bf16[4,1024,512]{2,1,0:T(8,128)(2,1)} %param.16, bf16[1,4,64,256]{3,1,2,0:T(4,128)(2,1)S(1)} %bitcast.28), kind=kOutput, calls=%fused_computation.40 | convolution fusion | flops 135791616 | bytes 2761728 | tf_op jit(solution)/shard_map/sub | solution.py:219
  80.2 2.1 %fusion.20 = bf16[1,4,64,256]{3,2,1,0:T(8,128)(2,1)S(1)} fusion(bf16[4,1024,512]{2,1,0:T(8,128)(2,1)} %param.16, bf16[4,64,1024]{2,1,0:T(8,128)(2,1)S(1)} %get-tuple-element.33, f32[4,64]{1,0:T(4,128)S(1)} %get-tuple-element.32), kind=kOutput, calls=%fused_computation.12 | convolution fusion | flops 134348800 | bytes 2753536 | tf_op jit(solution)/shard_map/bhp,bpd->bhd/dot_general | solution.py:221
  82.2 0.8 copy.19
  83.0 23.0 %all-to-all-done.1 = bf16[16,16,4480]{2,1,0:T(8,128)(2,1)S(1)} async-done(((bf16[16,16,4480]{2,1,0:T(8,128)(2,1)}), bf16[16,16,4480]{2,1,0:T(8,128)(2,1)S(1)}, u32[]{:S(2)}, u32[]{:S(2)}) %all-to-all-start.1) | async-done | bytes 2293792 | tf_op jit(solution)/shard_map/all_to_all | solution.py:285
  106.0 0.0 collective-permute-done.5.refs_3_
  106.0 0.0 collective-permute-done.6.refs_4_
  106.0 0.0 collective-permute-done.7.refs_5_
  106.0 1.5 %shard_map.108 = (f32[16,3584]{1,0:T(8,128)S(1)}, bf16[16,3584]{1,0:T(8,128)(2,1)S(1)}, bf16[16,3584]{1,0:T(8,128)(2,1)S(1)}, bf16[16,3584]{1,0:T(8,128)(2,1)S(1)}) custom-call(bf16[256,4480]{1,0:T(8,128)(2,1)S(1)} %bitcast.23, bf16[64,128]{1,0:T(8,128)(2,1)S(1)} %get-tuple-element.24.refs_1_, f32[16,128]{1,0:T(8,128)S(1)} %pad.4.refs_2_, ...), custom_call_target="tpu_custom_call" | custom-call | tf_op jit(solution)/shard_map/pallas_call | solution.py:76
  107.6 2.6 %collective-permute-start.10 = (bf16[16,3584]{1,0:T(8,128)(2,1)S(1)}, bf16[16,3584]{1,0:T(8,128)(2,1)S(1)}, u32[]{:S(2)}, u32[]{:S(2)}) collective-permute-start(bf16[16,3584]{1,0:T(8,128)(2,1)S(1)} %get-tuple-element.28), channel_id=1, source_target_pairs={{0,14},{4,0},{8,4},{12,8},{2,12},{6,2},{10,6},{14,10},{1,15},{5,1}... | collective-permute-start | bytes 344072 | tf_op jit(solution)/shard_map/ppermute | solution.py:36
  110.2 0.0 collective-permute-start.8
  110.2 3.8 %collective-permute-start.9 = (bf16[16,3584]{1,0:T(8,128)(2,1)S(1)}, bf16[16,3584]{1,0:T(8,128)(2,1)S(1)}, u32[]{:S(2)}, u32[]{:S(2)}) collective-permute-start(bf16[16,3584]{1,0:T(8,128)(2,1)S(1)} %get-tuple-element.27), channel_id=1, source_target_pairs={{0,8},{4,12},{8,2},{12,6},{2,10},{6,14},{10,0},{14,4},{1,9},{5,13}... | collective-permute-start | bytes 344072 | tf_op jit(solution)/shard_map/ppermute | solution.py:36
  113.9 0.0 collective-permute-done.10
  114.0 1.5 %collective-permute-done.8 = bf16[16,3584]{1,0:T(8,128)(2,1)S(1)} collective-permute-done((bf16[16,3584]{1,0:T(8,128)(2,1)S(1)}, bf16[16,3584]{1,0:T(8,128)(2,1)S(1)}, u32[]{:S(2)}, u32[]{:S(2)}) %collective-permute-start.8) | collective-permute-done | bytes 114720 | tf_op jit(solution)/shard_map/ppermute | solution.py:36
  115.5 5.8 %collective-permute-done.9 = bf16[16,3584]{1,0:T(8,128)(2,1)S(1)} collective-permute-done((bf16[16,3584]{1,0:T(8,128)(2,1)S(1)}, bf16[16,3584]{1,0:T(8,128)(2,1)S(1)}, u32[]{:S(2)}, u32[]{:S(2)}) %collective-permute-start.9) | collective-permute-done | bytes 114720 | tf_op jit(solution)/shard_map/ppermute | solution.py:36
  121.3 0.1 convert_add_fusion
  121.4 4.0 %collective-permute-start.11 = (bf16[16,1792]{1,0:T(8,128)(2,1)S(1)}, bf16[16,1792]{1,0:T(8,128)(2,1)S(1)}, u32[]{:S(2)}, u32[]{:S(2)}) collective-permute-start(bf16[16,1792]{1,0:T(8,128)(2,1)S(1)} %select_convert_fusion), channel_id=1, source_target_pairs={{0,2},{2,0},{1,3},{3,1},{4,6},{6,4},{5,7},{7,5},{8,10},{10,8},{9,1... | collective-permute-start | bytes 172040 | tf_op jit(solution)/shard_map/ppermute | solution.py:308
  125.4 4.2 %collective-permute-done.11 = bf16[16,1792]{1,0:T(8,128)(2,1)S(1)} collective-permute-done((bf16[16,1792]{1,0:T(8,128)(2,1)S(1)}, bf16[16,1792]{1,0:T(8,128)(2,1)S(1)}, u32[]{:S(2)}, u32[]{:S(2)}) %collective-permute-start.11) | collective-permute-done | bytes 57376 | tf_op jit(solution)/shard_map/ppermute | solution.py:308
  129.6 0.6 add_convert_fusion
  (21 shorter events, 0.1 us)
Async XLA Ops:
  0.6 69.1 %copy-start = (f32[7168,8]{0,1:T(8,128)S(1)}, f32[7168,8]{0,1:T(8,128)}, u32[]{:S(2)}) copy-start(f32[7168,8]{0,1:T(8,128)} %param.11) | copy-start | bytes 688132
  2.5 7.5 %collective-permute-start = (bf16[16,3712]{1,0:T(8,128)(2,1)S(1)}, bf16[16,3712]{1,0:T(8,128)(2,1)S(1)}, u32[]{:S(2)}, u32[]{:S(2)}) collective-permute-start(bf16[16,3712]{1,0:T(8,128)(2,1)S(1)} %pad_maximum_fusion.refs_0_), channel_id=1, source_target_pairs={{0,14},{4,0},{8,4},{12,8},{2,12},{6,2},{10,6},{14,10},{1,15},{5,1}... | collective-permute-start | bytes 356360 | tf_op jit(solution)/shard_map/ppermute | solution.py:36
  4.4 9.4 %collective-permute-start.1 = (bf16[16,3712]{1,0:T(8,128)(2,1)S(1)}, bf16[16,3712]{1,0:T(8,128)(2,1)S(1)}, u32[]{:S(2)}, u32[]{:S(2)}) collective-permute-start(bf16[16,3712]{1,0:T(8,128)(2,1)S(1)} %pad_maximum_fusion.refs_0_), channel_id=1, source_target_pairs={{0,10},{4,14},{8,0},{12,4},{2,8},{6,12},{10,2},{14,6},{1,11},{5,15... | collective-permute-start | bytes 356360 | tf_op jit(solution)/shard_map/ppermute | solution.py:36
  9.0 4.8 %collective-permute-start.2 = (bf16[16,3712]{1,0:T(8,128)(2,1)S(1)}, bf16[16,3712]{1,0:T(8,128)(2,1)S(1)}, u32[]{:S(2)}, u32[]{:S(2)}) collective-permute-start(bf16[16,3712]{1,0:T(8,128)(2,1)S(1)} %pad_maximum_fusion.refs_0_), channel_id=1, source_target_pairs={{0,4},{4,8},{8,12},{12,2},{2,6},{6,10},{10,14},{14,0},{1,5},{5,9},... | collective-permute-start | bytes 356360 | tf_op jit(solution)/shard_map/ppermute | solution.py:36
  14.6 37.1 %copy-start.2 = (bf16[7168,160]{0,1:T(8,128)(2,1)S(1)}, bf16[7168,160]{0,1:T(8,128)(2,1)}, u32[]{:S(2)}) copy-start(bf16[7168,160]{0,1:T(8,128)(2,1)} %param.12) | copy-start | bytes 6881284
  14.6 37.1 %copy-start.3 = (bf16[7168,160]{0,1:T(8,128)(2,1)S(1)}, bf16[7168,160]{0,1:T(8,128)(2,1)}, u32[]{:S(2)}) copy-start(bf16[7168,160]{0,1:T(8,128)(2,1)} %param.13) | copy-start | bytes 6881284
  51.7 4.4 %collective-permute-start.3 = (bf16[256,4480]{1,0:T(8,128)(2,1)S(1)}, bf16[256,4480]{1,0:T(8,128)(2,1)S(1)}, u32[]{:S(2)}, u32[]{:S(2)}) collective-permute-start(bf16[256,4480]{1,0:T(8,128)(2,1)S(1)} %bitcast.24), channel_id=1, source_target_pairs={{0,1},{1,0},{2,3},{3,2},{4,5},{5,4},{6,7},{7,6},{8,9},{9,8},{10,11... | collective-permute-start | bytes 6881288 | tf_op jit(solution)/shard_map/ppermute | solution.py:263
  51.7 4.4 %copy-start.1 = (bf16[160,7168]{1,0:T(8,128)(2,1)S(1)}, bf16[160,7168]{1,0:T(8,128)(2,1)}, u32[]{:S(2)}) copy-start(bf16[160,7168]{1,0:T(8,128)(2,1)} %w_down.3) | copy-start | bytes 6881284
  58.6 4.5 %collective-permute-start.4 = (bf16[256,4480]{1,0:T(8,128)(2,1)S(1)}, bf16[256,4480]{1,0:T(8,128)(2,1)S(1)}, u32[]{:S(2)}, u32[]{:S(2)}) collective-permute-start(bf16[256,4480]{1,0:T(8,128)(2,1)S(1)} %get-tuple-element.20), channel_id=1, source_target_pairs={{0,1},{1,0},{2,3},{3,2},{4,5},{5,4},{6,7},{7,6},{8,9},{9,8},{10,11... | collective-permute-start | bytes 6881288 | tf_op jit(solution)/shard_map/ppermute | solution.py:277
  65.7 3.9 %copy-start.5 = (s32[16,2]{0,1:T(2,128)S(1)}, s32[16,2]{0,1:T(2,128)}, u32[]{:S(2)}) copy-start(s32[16,2]{0,1:T(2,128)} %param.10) | copy-start | bytes 388
  65.7 4.1 %copy-start.4 = (bf16[16,7168]{1,0:T(8,128)(2,1)S(1)}, bf16[16,7168]{1,0:T(8,128)(2,1)}, u32[]{:S(2)}) copy-start(bf16[16,7168]{1,0:T(8,128)(2,1)} %param.9) | copy-start | bytes 688132
  65.7 11.8 %copy-start.6 = (s32[4]{0:T(128)S(1)}, s32[4]{0:T(128)}, u32[]{:S(2)}) copy-start(s32[4]{0:T(128)} %param.17) | copy-start | bytes 52
  65.7 11.9 %copy-start.7 = (bf16[4,16384]{1,0:T(4,128)(2,1)S(1)}, bf16[4,16384]{1,0:T(4,128)(2,1)}, u32[]{:S(2)}) copy-start(bf16[4,16384]{1,0:T(4,128)(2,1)} %param.15) | copy-start | bytes 393220
  65.7 40.3 %all-to-all-start.1 = ((bf16[16,16,4480]{2,1,0:T(8,128)(2,1)}), bf16[16,16,4480]{2,1,0:T(8,128)(2,1)S(1)}, u32[]{:S(2)}, u32[]{:S(2)}) async-start(bf16[16,16,4480]{2,1,0:T(8,128)(2,1)} %bitcast.5), calls=%async_computation.1 | async-start | bytes 4587520 | tf_op jit(solution)/shard_map/all_to_all | solution.py:285
  70.4 35.7 %collective-permute-start.5 = (f32[16,128]{1,0:T(8,128)S(1)}, f32[16,128]{1,0:T(8,128)S(1)}, u32[]{:S(2)}, u32[]{:S(2)}) collective-permute-start(f32[16,128]{1,0:T(8,128)S(1)} %pad.4.refs_2_), channel_id=1, source_target_pairs={{0,14},{4,0},{8,4},{12,8},{2,12},{6,2},{10,6},{14,10},{1,15},{5,1}... | collective-permute-start | bytes 24584 | tf_op jit(solution)/shard_map/ppermute | solution.py:36
  72.7 33.3 %collective-permute-start.6 = (f32[16,128]{1,0:T(8,128)S(1)}, f32[16,128]{1,0:T(8,128)S(1)}, u32[]{:S(2)}, u32[]{:S(2)}) collective-permute-start(f32[16,128]{1,0:T(8,128)S(1)} %pad.4.refs_2_), channel_id=1, source_target_pairs={{0,10},{4,14},{8,0},{12,4},{2,8},{6,12},{10,2},{14,6},{1,11},{5,15... | collective-permute-start | bytes 24584 | tf_op jit(solution)/shard_map/ppermute | solution.py:36
  77.5 28.5 %collective-permute-start.7 = (f32[16,128]{1,0:T(8,128)S(1)}, f32[16,128]{1,0:T(8,128)S(1)}, u32[]{:S(2)}, u32[]{:S(2)}) collective-permute-start(f32[16,128]{1,0:T(8,128)S(1)} %pad.4.refs_2_), channel_id=1, source_target_pairs={{0,4},{4,8},{8,12},{12,2},{2,6},{6,10},{10,14},{14,0},{1,5},{5,9},... | collective-permute-start | bytes 24584 | tf_op jit(solution)/shard_map/ppermute | solution.py:36
  107.6 6.4 %collective-permute-start.10 = (bf16[16,3584]{1,0:T(8,128)(2,1)S(1)}, bf16[16,3584]{1,0:T(8,128)(2,1)S(1)}, u32[]{:S(2)}, u32[]{:S(2)}) collective-permute-start(bf16[16,3584]{1,0:T(8,128)(2,1)S(1)} %get-tuple-element.28), channel_id=1, source_target_pairs={{0,14},{4,0},{8,4},{12,8},{2,12},{6,2},{10,6},{14,10},{1,15},{5,1}... | collective-permute-start | bytes 344072 | tf_op jit(solution)/shard_map/ppermute | solution.py:36
  110.2 5.3 %collective-permute-start.8 = (bf16[16,3584]{1,0:T(8,128)(2,1)S(1)}, bf16[16,3584]{1,0:T(8,128)(2,1)S(1)}, u32[]{:S(2)}, u32[]{:S(2)}) collective-permute-start(bf16[16,3584]{1,0:T(8,128)(2,1)S(1)} %get-tuple-element.26), channel_id=1, source_target_pairs={{0,4},{4,8},{8,12},{12,2},{2,6},{6,10},{10,14},{14,0},{1,5},{5,9},... | collective-permute-start | bytes 344072 | tf_op jit(solution)/shard_map/ppermute | solution.py:36
  110.2 11.1 %collective-permute-start.9 = (bf16[16,3584]{1,0:T(8,128)(2,1)S(1)}, bf16[16,3584]{1,0:T(8,128)(2,1)S(1)}, u32[]{:S(2)}, u32[]{:S(2)}) collective-permute-start(bf16[16,3584]{1,0:T(8,128)(2,1)S(1)} %get-tuple-element.27), channel_id=1, source_target_pairs={{0,8},{4,12},{8,2},{12,6},{2,10},{6,14},{10,0},{14,4},{1,9},{5,13}... | collective-permute-start | bytes 344072 | tf_op jit(solution)/shard_map/ppermute | solution.py:36
  121.4 8.2 %collective-permute-start.11 = (bf16[16,1792]{1,0:T(8,128)(2,1)S(1)}, bf16[16,1792]{1,0:T(8,128)(2,1)S(1)}, u32[]{:S(2)}, u32[]{:S(2)}) collective-permute-start(bf16[16,1792]{1,0:T(8,128)(2,1)S(1)} %select_convert_fusion), channel_id=1, source_target_pairs={{0,2},{2,0},{1,3},{3,1},{4,6},{6,4},{5,7},{7,5},{8,10},{10,8},{9,1... | collective-permute-start | bytes 172040 | tf_op jit(solution)/shard_map/ppermute | solution.py:308

commit v4 on v3

--- a/solution.py
+++ b/solution.py
@@ -17,6 +17,7 @@
 PLANE = 16
 LANES = 128
 REACH = (0, 1, 2, -1)
+HIGH, LOW = 64, 72
 BF16, F32 = jnp.bfloat16, jnp.float32
 VMEM_BYTES = 40 * 1024 * 1024
 
@@ -82,6 +83,35 @@
     )(*args)
 
 
+def rows_kernel(quarter, where, x_rows, ids, router, out):
+    half = 2 * quarter
+    values = x_rows[...].astype(F32)
+    first, second = ids[:, 0:1], ids[:, 1:2]
+    row, lane = grid(BLOCK, LANES)
+    squashed, total = [], 0.0
+    for e in range(EXPERTS):
+        logit = jnp.sum(values * router[e : e + 1, :], axis=1, keepdims=True)
+        kept = jnp.where((first == e) | (second == e), jax.nn.sigmoid(logit), 0.0)
+        squashed.append(kept)
+        total = total + kept
+    tail = jnp.zeros((BLOCK, LANES), F32)
+    for e in range(EXPERTS):
+        share = squashed[e] / total
+        high = share.astype(BF16).astype(F32)
+        low = (share - high).astype(BF16).astype(F32)
+        tail = jnp.where(lane == HIGH + e, high, jnp.where(lane == LOW + e, low, tail))
+    expert = fifth(lane)
+    named = (first == expert) | (second == expert)
+    row, column = grid(BLOCK, BLOCK)
+    rank = dot(ones(row > column).astype(BF16), ones(named).astype(BF16))
+    marks = ones(named & (rank == fifth_rest(lane).astype(F32)))
+    tail = jnp.where(lane < EXPERTS * CAP, marks, tail)
+    for f in range(2):
+        at = pl.ds(pl.multiple_of(f * half + where[0] * quarter, LANES), quarter)
+        out[:, f * quarter : (f + 1) * quarter] = x_rows[:, at]
+    out[:, half:] = tail.astype(BF16)
+
+
 def pack_kernel(quarter, *refs):
     blocks, (out, marks) = refs[:4], refs[4:]
     half = 2 * quarter
@@ -89,6 +119,8 @@
     rows = jnp.concatenate([b[:, :half] for b in blocks], axis=0)
     chosen = jnp.concatenate([b[:, half:] for b in blocks], axis=0)
     marks[...] = chosen
+    lane = grid(ZLO * BLOCK, LANES)[1]
+    chosen = jnp.where(lane < EXPERTS * CAP, chosen, jnp.zeros_like(chosen))
     slot, lane = grid(EXPERTS * BLOCK, LANES)
     same = fifth(lane) == slot >> 4
     pick_main = ones(same & (fifth_rest(lane) == fifth_rest(slot & 15))).astype(BF16)
@@ -170,22 +202,19 @@
     out[:, half:] = (rest + got[:, half:].astype(F32)).astype(BF16)
 
 
-def combine_kernel(quarter, *refs):
-    back, marks, shares, outs = refs[0], refs[1], refs[2:6], refs[6:]
-    half = 2 * quarter
-    share = jnp.concatenate([s[...] for s in shares], axis=0)
-    high = share.astype(BF16)
-    low = (share - high.astype(F32)).astype(BF16)
+def combine_kernel(quarter, where, back, marks, out):
+    half = 2 * quarter
     chosen = marks[...]
     lane, slot = grid(LANES, PLANE * BLOCK)
-    same = fifth(lane) == slot >> 5
+    expert = slot >> 5
+    same = fifth(lane) == expert
     back_main = ones(same & (fifth_rest(lane) == fifth_rest(slot & 15))).astype(BF16)
     back_rest = ones(same & (fifth_rest(lane) == 1 + (slot & 3))).astype(BF16)
-    spread = ones(lane == slot >> 5).astype(BF16)
+    wide_high = dot(chosen, ones(lane == HIGH + expert).astype(BF16))
+    wide_low = dot(chosen, ones(lane == LOW + expert).astype(BF16))
     row, slot = grid(ZLO * BLOCK, PLANE * BLOCK)
     main = dot(chosen, back_main) * ones(fifth(slot & 15) == row >> 4)
     rest = dot(chosen, back_rest) * ones(row >> 4 == 3)
-    wide_high, wide_low = dot(high, spread), dot(low, spread)
     total = dot((main * wide_high).astype(BF16), back[:, :half]) + dot(
         (main * wide_low).astype(BF16), back[:, :half]
     )
@@ -197,9 +226,11 @@
             dot((mask * wide_high).astype(BF16), tail) + dot((mask * wide_low).astype(BF16), tail)
         )
     total = total + jnp.concatenate(pieces, axis=1)
-    outs[0][...] = total[:BLOCK]
-    for k in range(1, ZLO):
-        outs[k][...] = total[k * BLOCK : (k + 1) * BLOCK].astype(BF16)
+    for k in range(ZLO):
+        owner = (where[1] + (REACH[k] % ZLO)) & (ZLO - 1)
+        for f in range(2):
+            piece = total[k * BLOCK : (k + 1) * BLOCK, f * quarter : (f + 1) * quarter]
+            out[owner * 2 + f] = piece.astype(BF16)
 
 
 def attention_block(queries, cache, lengths):
@@ -229,26 +260,17 @@
     quarter = model_width // 4
     half, eighth = 2 * quarter, quarter // 2
     width = half + eighth
-    z_hi, core = lax.axis_index("zh"), lax.axis_index("c")
-    core_ref = core.astype(jnp.int32).reshape(1)
-
-    lane = jnp.arange(LANES)
-    named = jnp.any(
-        (route_ids[:, :, None] == (lane // CAP)[None, None, :]) & (lane < EXPERTS * CAP), axis=1
-    )
-    earlier = jnp.arange(BLOCK)[:, None] > jnp.arange(BLOCK)[None, :]
-    rank = jnp.sum(jnp.where(earlier[:, :, None], named[None].astype(jnp.int32), 0), axis=1)
-    marks = (named & (rank == (lane % CAP)[None, :])).astype(BF16)
-    payload = jnp.concatenate(
-        [
-            lax.dynamic_slice_in_dim(x_rows, core * quarter, quarter, 1),
-            lax.dynamic_slice_in_dim(x_rows, half + core * quarter, quarter, 1),
-            marks,
-        ],
-        axis=1,
+    where = jnp.stack([lax.axis_index("c"), lax.axis_index("zl")]).astype(jnp.int32)
+    payload = call(
+        functools.partial(rows_kernel, quarter),
+        jax.ShapeDtypeStruct((BLOCK, half + LANES), BF16),
+        where, x_rows, route_ids.astype(F32), router.T,
     )
     blocks = [payload] + [z_send(payload, -k) for k in REACH[1:]]
 
+    payload, queries = lax.optimization_barrier((payload, queries))
+    attn_out = attention_block(queries, cache, lengths)
+    blocks, attn_out = lax.optimization_barrier((blocks, attn_out))
     packed, marks = call(
         functools.partial(pack_kernel, quarter),
         (
@@ -266,46 +288,31 @@
     gate, up = call(
         functools.partial(own_kernel, quarter),
         (partial, partial),
-        core_ref, arrived, w_gate, w_up,
+        where, arrived, w_gate, w_up,
     )
     pieces = jax.ShapeDtypeStruct((PLANE * BLOCK, width), BF16)
     hidden, away = call(
         functools.partial(other_kernel, quarter),
         (jax.ShapeDtypeStruct((rows, hidden_count), BF16), pieces),
-        core_ref, beside, w_gate, w_up, w_down, gate, up,
+        where, beside, w_gate, w_up, w_down, gate, up,
     )
     got = lax.ppermute(away, "c", SWAP)
     summed = call(
         functools.partial(sum_kernel, quarter),
         pieces,
-        core_ref, hidden, w_down, got,
-    )
-    summed, queries = lax.optimization_barrier((summed, queries))
-    attn_out = attention_block(queries, cache, lengths)
+        where, hidden, w_down, got,
+    )
     returned = lax.all_to_all(
         summed.reshape(PLANE, BLOCK, width), ("y", "xh", "xl"), 0, 0, tiled=True
     ).reshape(PLANE * BLOCK, width)
 
-    logits = jnp.dot(x_rows.astype(F32), router, precision=lax.Precision.HIGHEST)
-    squashed = jax.nn.sigmoid(logits)
-    picked = jnp.any(route_ids[:, :, None] == jnp.arange(EXPERTS)[None, None, :], axis=1)
-    share = squashed / jnp.sum(jnp.where(picked, squashed, 0.0), axis=1, keepdims=True)
-    share = jnp.pad(jnp.where(picked, share, 0.0), ((0, 0), (0, LANES - EXPERTS)))
-    shares = [share] + [z_send(share, -k) for k in REACH[1:]]
-
-    returned, attn_out = lax.optimization_barrier((returned, attn_out))
     parts = call(
         functools.partial(combine_kernel, quarter),
-        tuple(jax.ShapeDtypeStruct((BLOCK, half), F32 if k == 0 else BF16) for k in range(ZLO)),
-        returned, marks, *shares,
-    )
-    total = parts[0]
-    for k in range(1, ZLO):
-        total = total + z_send(parts[k], REACH[k]).astype(F32)
-    low, high = total[:, :quarter], total[:, quarter:]
-    lower = z_hi == 0
-    sent = jnp.where(lower, high, low).astype(BF16)
-    moe_out = jnp.where(lower, low, high) + lax.ppermute(sent, "zh", SWAP).astype(F32)
+        jax.ShapeDtypeStruct((ZALL, BLOCK, quarter), BF16),
+        where, returned, marks,
+    )
+    parts = lax.all_to_all(parts, ("zl", "zh"), 0, 0, tiled=True)
+    moe_out = jnp.sum(parts.astype(F32), axis=0)
     return (moe_out.astype(BF16), attn_out)
 
 

time: 132 us -> 127 us (0.962)
  blocking collectives: 37.1 us -> 90.9 us
  waiting for transfers between devices: 45.6 us -> 6.71 us
  starting transfers between devices: 29.1 us -> 7.72 us
  Pallas kernels: 8.75 us -> 10.6 us
    all_to_all x0 -> x2, blocking collectives: none -> 53.9 us  [the longest x1 33.8 us: shards(): lax.all_to_all(summed.reshape(PLANE, BLOCK, width), ('y', 'xh', 'xl'), 0,...]
    all_to_all x1 -> x0, waiting for transfers between devices: 23 us -> none  [shards(): lax.all_to_all(summed.reshape(PLANE, BLOCK, width), ('y', 'xh', 'xl'), 0,...]
    ppermute x9 -> x3, starting transfers between devices: 21 us -> 7.5 us  [z_send(): return lax.ppermute(value, ('zl', 'zh'), z_pairs(step))]
    ppermute x9 -> x3, waiting for transfers between devices: 11.2 us -> 0.01 us  [z_send(): return lax.ppermute(value, ('zl', 'zh'), z_pairs(step))]
    ppermute x1 -> x0, waiting for transfers between devices: 4.18 us -> none  [shards(): lax.ppermute(sent, 'zh', SWAP).astype(F32)]
    ppermute x1 -> x0, starting transfers between devices: 3.99 us -> none  [shards(): lax.ppermute(sent, 'zh', SWAP).astype(F32)]
    all_to_all x1 -> x0, starting transfers between devices: 3.92 us -> none  [shards(): lax.all_to_all(summed.reshape(PLANE, BLOCK, width), ('y', 'xh', 'xl'), 0,...]
    pallas_call x5 -> x6, Pallas kernels: 8.75 us -> 10.6 us  [call(): pl.pallas_call(kernel, out_shape=out_shape, in_specs=at, out_specs=jax.tr...]
  transfers between devices with their start and end apart: 13 -> 5, of which waited for: 7 -> 2; matrix products, arithmetic and copies ran while one was open for 5% -> 5% of each run, Pallas kernels for 1% -> 2%
where the time goes in v4:
time: 127 us; the launch traced here: 126 us
  blocking collectives  90.9 us (72%)
  Pallas kernels  10.6 us (8%)
  starting transfers between devices  7.72 us (6%)
  waiting for transfers between devices  6.71 us (5%)
  matrix products  4.72 us (4%)
  local copies, waits for them, and re-layouts  2.74 us (2%)
  other arithmetic  2.17 us (2%)
    all_to_all x1, blocking collectives, shards(): lax.all_to_all(packed.reshape(PLANE, BLOCK, width), ('y', 'xh', 'xl'), 0,...  36.9 us
    all_to_all x1, blocking collectives, shards(): lax.all_to_all(summed.reshape(PLANE, BLOCK, width), ('y', 'xh', 'xl'), 0,...  33.8 us
    all_to_all x1, blocking collectives, shards(): parts = lax.all_to_all(parts, ('zl', 'zh'), 0, 0, tiled=True)  20.2 us
    pallas_call x6, Pallas kernels, call(): pl.pallas_call(kernel, out_shape=out_shape, in_specs=at, out_specs=jax.tr...  10.6 us
    ppermute x3, starting transfers between devices, z_send(): return lax.ppermute(value, ('zl', 'zh'), z_pairs(step))  7.5 us
    ppermute x1, waiting for transfers between devices, shards(): got = lax.ppermute(away, 'c', SWAP)  4.31 us
    unnamed x11, local copies, waits for them, and re-layouts  2.65 us
    sub x1, matrix products, attention_block(): weights = jnp.where(live[:, None, :], jnp.exp(scores - largest), 0.0)  2.64 us
  transfers between devices with their start and end apart: 5, of which 2 were waited for; matrix products, arithmetic and copies ran while one was open for 5% of the time, Pallas kernels for 2%

profile of v4, /device:TPU:32, one launch (start us, length us, event | category | flops | bytes accessed | tf_op | source)
XLA Modules:
  0.0 126.3 jit_solution(10018305036494304846)
XLA Ops:
  0.6 0.7 convert_element_type.11
  1.3 0.1 copy.12.ids
  1.4 0.1 pad_add_fusion.where.core
  1.5 0.0 copy-start.3
  1.5 0.9 copy-done.3
  2.4 0.0 copy-start.4
  2.4 0.9 copy-done.4
  3.4 1.1 shard_map.104.refs_0_
  4.5 2.0 %collective-permute-start.2 = (bf16[16,3712]{1,0:T(8,128)(2,1)S(1)}, bf16[16,3712]{1,0:T(8,128)(2,1)S(1)}, u32[]{:S(2)}, u32[]{:S(2)}) collective-permute-start(bf16[16,3712]{1,0:T(8,128)(2,1)S(1)} %shard_map.104.refs_0_), channel_id=1, source_target_pairs={{0,4},{4,8},{8,12},{12,2},{2,6},{6,10},{10,14},{14,0},{1,5},{5,9},... | collective-permute-start | bytes 356360 | tf_op jit(solution)/shard_map/ppermute | solution.py:37
  6.5 3.6 %collective-permute-start.1 = (bf16[16,3712]{1,0:T(8,128)(2,1)S(1)}, bf16[16,3712]{1,0:T(8,128)(2,1)S(1)}, u32[]{:S(2)}, u32[]{:S(2)}) collective-permute-start(bf16[16,3712]{1,0:T(8,128)(2,1)S(1)} %shard_map.104.refs_0_), channel_id=1, source_target_pairs={{0,10},{4,14},{8,0},{12,4},{2,8},{6,12},{10,2},{14,6},{1,11},{5,15... | collective-permute-start | bytes 356360 | tf_op jit(solution)/shard_map/ppermute | solution.py:37
  10.1 1.9 %collective-permute-start = (bf16[16,3712]{1,0:T(8,128)(2,1)S(1)}, bf16[16,3712]{1,0:T(8,128)(2,1)S(1)}, u32[]{:S(2)}, u32[]{:S(2)}) collective-permute-start(bf16[16,3712]{1,0:T(8,128)(2,1)S(1)} %shard_map.104.refs_0_), channel_id=1, source_target_pairs={{0,14},{4,0},{8,4},{12,8},{2,12},{6,2},{10,6},{14,10},{1,15},{5,1}... | collective-permute-start | bytes 356360 | tf_op jit(solution)/shard_map/ppermute | solution.py:37
  12.0 0.7 iota_compare_fusion
  12.7 2.6 %fusion.26 = (f32[4,64]{1,0:T(4,128)S(1)}, bf16[4,64,1024]{2,1,0:T(8,128)(2,1)S(1)}) fusion(pred[4,1024]{1,0:T(4,128)(4,1)S(1)} %iota_compare_fusion, bf16[4,1024,512]{2,1,0:T(8,128)(2,1)} %param.16, bf16[1,4,64,256]{3,1,2,0:T(4,128)(2,1)} %bitcast.30), kind=kOutput, calls=%fused_computation.18 | convolution fusion | flops 135791616 | bytes 2761728 | tf_op jit(solution)/shard_map/sub | solution.py:250
  15.4 2.1 %fusion.20 = bf16[1,4,64,256]{3,2,1,0:T(8,128)(2,1)S(1)} fusion(bf16[4,1024,512]{2,1,0:T(8,128)(2,1)} %param.16, bf16[4,64,1024]{2,1,0:T(8,128)(2,1)S(1)} %get-tuple-element.27, f32[4,64]{1,0:T(4,128)S(1)} %get-tuple-element.26), kind=kOutput, calls=%fused_computation.12 | convolution fusion | flops 134348800 | bytes 2753536 | tf_op jit(solution)/shard_map/bhp,bpd->bhd/dot_general | solution.py:252
  17.5 0.8 copy.14
  18.2 0.0 collective-permute-done.2.refs_3_
  18.2 0.0 collective-permute-done.1.refs_2_
  18.2 0.0 collective-permute-done.refs_1_
  18.2 0.7 shard_map.105
  19.0 0.0 copy-start.1
  19.0 0.0 copy-start.2
  19.0 36.9 %all_to_all.15 = bf16[16,16,4480]{2,1,0:T(8,128)(2,1)S(1)} all-to-all(bf16[16,16,4480]{2,1,0:T(8,128)(2,1)S(1)} %bitcast.27), channel_id=1, replica_groups=mesh['y'=4,'xh'=2,'xl'=2,'zl'=4,'zh'=2,'c'=2] {'y','xh','xl'}, dimensions={0} | all-to-all | bytes 4587520 | tf_op jit(solution)/shard_map/all_to_all | solution.py:282
  55.9 0.0 collective-permute-start.3
  55.9 0.0 copy-done.1
  55.9 0.0 copy-done.2
  55.9 0.0 copy-start
  55.9 2.0 %shard_map.106 = (f32[320,160]{1,0:T(8,128)S(1)}, f32[320,160]{1,0:T(8,128)S(1)}) custom-call(s32[2]{0:T(128)S(1)} %pad_add_fusion.where.core, bf16[256,4480]{1,0:T(8,128)(2,1)S(1)} %bitcast.25, bf16[160,7168]{1,0:T(8,128)(2,1)S(1)} %bitcast.19, bf16[160,7168]{1,0:T(8,128)(2,1)S(1)} %bitcast.21), custom_call_target="tpu_custom_call" | custom-call | tf_op jit(solution)/shard_map/pallas_call | solution.py:77
  58.0 2.4 %collective-permute-done.3.block = bf16[256,4480]{1,0:T(8,128)(2,1)S(1)} collective-permute-done((bf16[256,4480]{1,0:T(8,128)(2,1)S(1)}, bf16[256,4480]{1,0:T(8,128)(2,1)S(1)}, u32[]{:S(2)}, u32[]{:S(2)}) %collective-permute-start.3) | collective-permute-done | bytes 2293792 | tf_op jit(solution)/shard_map/ppermute | solution.py:285
  60.4 0.0 copy-done
  60.4 3.0 %shard_map.107 = (bf16[320,160]{1,0:T(8,128)(2,1)S(1)}, bf16[256,4480]{1,0:T(8,128)(2,1)S(1)}) custom-call(s32[2]{0:T(128)S(1)} %pad_add_fusion.where.core, bf16[256,4480]{1,0:T(8,128)(2,1)S(1)} %collective-permute-done.3.block, bf16[160,7168]{1,0:T(8,128)(2,1)S(1)} %bitcast.20, bf16[160,7168]{1,0:T(8,128)(2,1)S(1)} %bitcast.22, ...), custom_call_target="tpu_custom_call" | custom-call | tf_op jit(solution)/shard_map/pallas_call | solution.py:77
  63.3 0.2 collective-permute-start.4
  63.6 4.3 %collective-permute-done.4.got = bf16[256,4480]{1,0:T(8,128)(2,1)S(1)} collective-permute-done((bf16[256,4480]{1,0:T(8,128)(2,1)S(1)}, bf16[256,4480]{1,0:T(8,128)(2,1)S(1)}, u32[]{:S(2)}, u32[]{:S(2)}) %collective-permute-start.4) | collective-permute-done | bytes 2293792 | tf_op jit(solution)/shard_map/ppermute | solution.py:299
  67.9 1.7 %shard_map.108 = bf16[256,4480]{1,0:T(8,128)(2,1)S(1)} custom-call(s32[2]{0:T(128)S(1)} %pad_add_fusion.where.core, bf16[320,160]{1,0:T(8,128)(2,1)S(1)} %get-tuple-element.22.hidden, bf16[160,7168]{1,0:T(8,128)(2,1)S(1)} %copy-done, bf16[256,4480]{1,0:T(8,128)(2,1)S(1)} %collective-permute-done.4.got), custom_call_target="tpu_custom_call" | custom-call | tf_op jit(solution)/shard_map/pallas_call | solution.py:77
  69.6 33.8 %all_to_all.16 = bf16[16,16,4480]{2,1,0:T(8,128)(2,1)S(1)} all-to-all(bf16[16,16,4480]{2,1,0:T(8,128)(2,1)S(1)} %bitcast.23), channel_id=1, replica_groups=mesh['y'=4,'xh'=2,'xl'=2,'zl'=4,'zh'=2,'c'=2] {'y','xh','xl'}, dimensions={0} | all-to-all | bytes 4587520 | tf_op jit(solution)/shard_map/all_to_all | solution.py:305
  103.4 2.0 %shard_map.109 = bf16[8,16,1792]{2,1,0:T(8,128)(2,1)S(1)} custom-call(s32[2]{0:T(128)S(1)} %pad_add_fusion.where.core, bf16[256,4480]{1,0:T(8,128)(2,1)S(1)} %bitcast.26, bf16[64,128]{1,0:T(8,128)(2,1)S(1)} %get-tuple-element.24.marks), custom_call_target="tpu_custom_call" | custom-call | tf_op jit(solution)/shard_map/pallas_call | solution.py:77
  105.4 20.2 %all_to_all.17 = bf16[8,16,1792]{2,1,0:T(8,128)(2,1)S(1)} all-to-all(bf16[8,16,1792]{2,1,0:T(8,128)(2,1)S(1)} %shard_map.109), channel_id=1, replica_groups=mesh['y'=4,'xh'=2,'xl'=2,'zl'=4,'zh'=2,'c'=2] {'zl','zh'}, dimensions={0} | all-to-all | bytes 917504 | tf_op jit(solution)/shard_map/all_to_all | solution.py:314
  125.6 0.7 reduce_sum.22
Async XLA Ops:
  1.5 0.9 copy-start.3
  2.4 0.9 copy-start.4
  4.5 13.7 %collective-permute-start.2 = (bf16[16,3712]{1,0:T(8,128)(2,1)S(1)}, bf16[16,3712]{1,0:T(8,128)(2,1)S(1)}, u32[]{:S(2)}, u32[]{:S(2)}) collective-permute-start(bf16[16,3712]{1,0:T(8,128)(2,1)S(1)} %shard_map.104.refs_0_), channel_id=1, source_target_pairs={{0,4},{4,8},{8,12},{12,2},{2,6},{6,10},{10,14},{14,0},{1,5},{5,9},... | collective-permute-start | bytes 356360 | tf_op jit(solution)/shard_map/ppermute | solution.py:37
  6.5 11.7 %collective-permute-start.1 = (bf16[16,3712]{1,0:T(8,128)(2,1)S(1)}, bf16[16,3712]{1,0:T(8,128)(2,1)S(1)}, u32[]{:S(2)}, u32[]{:S(2)}) collective-permute-start(bf16[16,3712]{1,0:T(8,128)(2,1)S(1)} %shard_map.104.refs_0_), channel_id=1, source_target_pairs={{0,10},{4,14},{8,0},{12,4},{2,8},{6,12},{10,2},{14,6},{1,11},{5,15... | collective-permute-start | bytes 356360 | tf_op jit(solution)/shard_map/ppermute | solution.py:37
  10.1 8.2 %collective-permute-start = (bf16[16,3712]{1,0:T(8,128)(2,1)S(1)}, bf16[16,3712]{1,0:T(8,128)(2,1)S(1)}, u32[]{:S(2)}, u32[]{:S(2)}) collective-permute-start(bf16[16,3712]{1,0:T(8,128)(2,1)S(1)} %shard_map.104.refs_0_), channel_id=1, source_target_pairs={{0,14},{4,0},{8,4},{12,8},{2,12},{6,2},{10,6},{14,10},{1,15},{5,1}... | collective-permute-start | bytes 356360 | tf_op jit(solution)/shard_map/ppermute | solution.py:37
  19.0 37.0 %copy-start.1 = (bf16[7168,160]{0,1:T(8,128)(2,1)S(1)}, bf16[7168,160]{0,1:T(8,128)(2,1)}, u32[]{:S(2)}) copy-start(bf16[7168,160]{0,1:T(8,128)(2,1)} %param.12) | copy-start | bytes 6881284
  19.0 36.9 %copy-start.2 = (bf16[7168,160]{0,1:T(8,128)(2,1)S(1)}, bf16[7168,160]{0,1:T(8,128)(2,1)}, u32[]{:S(2)}) copy-start(bf16[7168,160]{0,1:T(8,128)(2,1)} %param.13) | copy-start | bytes 6881284
  55.9 4.4 %collective-permute-start.3 = (bf16[256,4480]{1,0:T(8,128)(2,1)S(1)}, bf16[256,4480]{1,0:T(8,128)(2,1)S(1)}, u32[]{:S(2)}, u32[]{:S(2)}) collective-permute-start(bf16[256,4480]{1,0:T(8,128)(2,1)S(1)} %bitcast.24), channel_id=1, source_target_pairs={{0,1},{1,0},{2,3},{3,2},{4,5},{5,4},{6,7},{7,6},{8,9},{9,8},{10,11... | collective-permute-start | bytes 6881288 | tf_op jit(solution)/shard_map/ppermute | solution.py:285
  55.9 4.4 %copy-start = (bf16[160,7168]{1,0:T(8,128)(2,1)S(1)}, bf16[160,7168]{1,0:T(8,128)(2,1)}, u32[]{:S(2)}) copy-start(bf16[160,7168]{1,0:T(8,128)(2,1)} %w_down.3) | copy-start | bytes 6881284
  63.3 4.5 %collective-permute-start.4 = (bf16[256,4480]{1,0:T(8,128)(2,1)S(1)}, bf16[256,4480]{1,0:T(8,128)(2,1)S(1)}, u32[]{:S(2)}, u32[]{:S(2)}) collective-permute-start(bf16[256,4480]{1,0:T(8,128)(2,1)S(1)} %get-tuple-element.23), channel_id=1, source_target_pairs={{0,1},{1,0},{2,3},{3,2},{4,5},{5,4},{6,7},{7,6},{8,9},{9,8},{10,11... | collective-permute-start | bytes 6881288 | tf_op jit(solution)/shard_map/ppermute | solution.py:299

commit v5 on v4

--- a/solution.py
+++ b/solution.py
@@ -18,6 +18,7 @@
 LANES = 128
 REACH = (0, 1, 2, -1)
 HIGH, LOW = 64, 72
+PLAIN, RING = 3, 2
 BF16, F32 = jnp.bfloat16, jnp.float32
 VMEM_BYTES = 40 * 1024 * 1024
 
@@ -50,6 +51,10 @@
 
 def fifth_rest(value):
     return value - CAP * fifth(value)
+
+
+def third(value):
+    return (value * 86) >> 8
 
 
 def ones(condition):
@@ -83,7 +88,7 @@
     )(*args)
 
 
-def rows_kernel(quarter, where, x_rows, ids, router, out):
+def rows_kernel(quarter, where, x_rows, ids, router, out, ring_out):
     half = 2 * quarter
     values = x_rows[...].astype(F32)
     first, second = ids[:, 0:1], ids[:, 1:2]
@@ -110,6 +115,29 @@
         at = pl.ds(pl.multiple_of(f * half + where[0] * quarter, LANES), quarter)
         out[:, f * quarter : (f + 1) * quarter] = x_rows[:, at]
     out[:, half:] = tail.astype(BF16)
+    at = pl.ds(pl.multiple_of(where[2] * half + where[0] * quarter, LANES), quarter)
+    mine = x_rows[:, at]
+    slot, lane = grid(PLANE * 2 * RING, LANES)
+    pick = (fifth(lane) == slot >> 3) & (fifth_rest(lane) == PLAIN + ((slot >> 1) & 1))
+    select = dot_t(ones(pick).astype(BF16), marks.astype(BF16))
+    second_half = grid(PLANE * 2 * RING, BLOCK)[0] & 1
+    ring_out[...] = (
+        dot((select * ones(second_half == 0)).astype(BF16), mine[:, : quarter // 2])
+        + dot((select * ones(second_half == 1)).astype(BF16), mine[:, quarter // 2 :])
+    ).astype(BF16)
+
+
+def ring_kernel(*refs):
+    blocks, out = refs[:-1], refs[-1]
+    width = blocks[0].shape[1]
+    for k in range(ZALL):
+        at = slice(k * width, (k + 1) * width)
+        if k < 4:
+            out[:, at] = blocks[k][...]
+        elif k == 4:
+            out[:, at] = jnp.concatenate([blocks[4][...], blocks[5][...]], axis=0)
+        else:
+            out[:, at] = blocks[k + 1][...]
 
 
 def pack_kernel(quarter, *refs):
@@ -121,39 +149,63 @@
     marks[...] = chosen
     lane = grid(ZLO * BLOCK, LANES)[1]
     chosen = jnp.where(lane < EXPERTS * CAP, chosen, jnp.zeros_like(chosen))
-    slot, lane = grid(EXPERTS * BLOCK, LANES)
-    same = fifth(lane) == slot >> 4
-    pick_main = ones(same & (fifth_rest(lane) == fifth_rest(slot & 15))).astype(BF16)
-    pick_rest = ones(same & (fifth_rest(lane) == 1 + (slot & 3))).astype(BF16)
-    slot, row = grid(EXPERTS * BLOCK, ZLO * BLOCK)
-    mask = ones(fifth(slot & 15) == row >> 4)
-    main = dot((dot_t(pick_main, chosen) * mask).astype(BF16), rows)
-    main = main.astype(BF16).reshape(EXPERTS, BLOCK, half)
     chosen4 = jnp.concatenate([chosen] * 4, axis=0)
     rows4 = jnp.concatenate([rows[:, i * eighth : (i + 1) * eighth] for i in range(4)], axis=0)
-    slot, row = grid(EXPERTS * BLOCK, 4 * ZLO * BLOCK)
-    mask = ones(((slot >> 2) & 3 == row >> 6) & ((row >> 4) & 3 == 3))
-    rest = dot((dot_t(pick_rest, chosen4) * mask).astype(BF16), rows4)
-    rest = rest.astype(BF16).reshape(EXPERTS, BLOCK, eighth)
-    for x in range(2):
-        out[:, x, :, :half] = main
-        out[:, x, :, half:] = rest
-
-
-def experts_in(quarter, core, block, w_gate, w_up):
-    half = 2 * quarter
-    rest = dot(shuffle_table(False), block[:, half:]).astype(BF16)
+    for j in range(PLAIN):
+        slot, lane = grid(EXPERTS * BLOCK, LANES)
+        number = 4 * j + (slot & 3)
+        same = (fifth(lane) == slot >> 4) & (fifth_rest(lane) == number - PLAIN * third(number))
+        slot, row = grid(EXPERTS * BLOCK, 4 * ZLO * BLOCK)
+        number = 4 * j + (slot & 3)
+        mask = ones(((slot >> 2) & 3 == row >> 6) & ((row >> 4) & 3 == third(number)))
+        select = dot_t(ones(same).astype(BF16), chosen4) * mask
+        part = dot(select.astype(BF16), rows4).astype(BF16).reshape(EXPERTS, BLOCK, eighth)
+        for x in range(2):
+            out[:, x, :, j * eighth : (j + 1) * eighth] = part
+
+
+def experts_in(quarter, where, core, block, ring, w_gate, w_up):
+    half, eighth = 2 * quarter, quarter // 2
+    plain = dot(shuffle_table(False), block[...]).astype(BF16)
+    new, old = grid(PLANE * 2 * RING, PLANE * 2 * RING)
+    spot = (old & 1) * 2 * BLOCK + (old >> 1)
+    split = ones(new == spot).astype(BF16)
+    z_pos = where[2] * ZLO + where[1]
     gate, up = 0.0, 0.0
     for f in range(2):
-        top = block[:, f * quarter : (f + 1) * quarter]
-        tail = jnp.concatenate(
-            [rest[(2 * f + i) * 64 : (2 * f + i + 1) * 64] for i in range(2)], axis=1
-        )
-        rows = jnp.concatenate([top, tail], axis=0)
+        rows = []
+        for j in range(PLAIN):
+            at = slice(j * eighth, (j + 1) * eighth)
+            pair = [plain[g * 64 : (g + 1) * 64, at] for g in (2 * f, 2 * f + 1)]
+            rows.append(jnp.concatenate(pair, axis=1))
+        for k in range(ZLO):
+            near = ((z_pos + k) & (ZALL - 1)) >> 2 == f
+            piece = jnp.where(
+                near,
+                ring[:, k * eighth : (k + 1) * eighth],
+                ring[:, (k + ZLO) * eighth : (k + ZLO + 1) * eighth],
+            )
+            piece = dot(split, piece).astype(BF16)
+            rows.append(jnp.concatenate([piece[: 2 * BLOCK], piece[2 * BLOCK :]], axis=1))
+        rows = jnp.concatenate(rows, axis=0)
         at = pl.ds(pl.multiple_of(f * half + core * quarter, LANES), quarter)
         gate = gate + dot_t(rows, w_gate[:, at])
         up = up + dot_t(rows, w_up[:, at])
     return gate, up
+
+
+def return_order(hidden):
+    count = PLANE * (BLOCK + ZLO)
+    new, old = grid(count, count)
+    main = new < PLANE * BLOCK
+    src = jnp.where(main, new >> 4, (new - PLANE * BLOCK) >> 2)
+    slot = jnp.where(main, new & 15, 16 + (new & 3))
+    k, s = fifth(slot), fifth_rest(slot)
+    number = k * PLAIN + s
+    plain = (number >> 2) * 64 + src * 4 + (number & 3)
+    ring = PLAIN * 64 + k * 2 * BLOCK + src * 2 + s - PLAIN
+    spot = jnp.where(s < PLAIN, plain, ring)
+    return dot(ones(old == spot).astype(BF16), hidden).astype(BF16)
 
 
 def experts_out(quarter, core, hidden, w_down):
@@ -168,20 +220,20 @@
     return mains, jnp.concatenate(rests, axis=0)
 
 
-def own_kernel(quarter, core, block, w_gate, w_up, gate_out, up_out):
-    gate, up = experts_in(quarter, core[0], block, w_gate, w_up)
+def own_kernel(quarter, where, block, ring, w_gate, w_up, gate_out, up_out):
+    gate, up = experts_in(quarter, where, where[0], block, ring, w_gate, w_up)
     gate_out[...] = gate
     up_out[...] = up
 
 
 def other_kernel(
-    quarter, core, block, w_gate, w_up, w_down, gate_in, up_in, hidden_out, away
+    quarter, where, block, ring, w_gate, w_up, w_down, gate_in, up_in, hidden_out, away
 ):
     half = 2 * quarter
-    there = 1 - core[0]
-    gate, up = experts_in(quarter, there, block, w_gate, w_up)
+    there = 1 - where[0]
+    gate, up = experts_in(quarter, where, there, block, ring, w_gate, w_up)
     gate, up = gate + gate_in[...], up + up_in[...]
-    hidden = (gate * jax.nn.sigmoid(gate) * up).astype(BF16)
+    hidden = return_order((gate * jax.nn.sigmoid(gate) * up).astype(BF16))
     hidden_out[...] = hidden
     mains, rest = experts_out(quarter, there, hidden, w_down)
     for f in range(2):
@@ -260,41 +312,57 @@
     quarter = model_width // 4
     half, eighth = 2 * quarter, quarter // 2
     width = half + eighth
-    where = jnp.stack([lax.axis_index("c"), lax.axis_index("zl")]).astype(jnp.int32)
-    payload = call(
+    where = jnp.stack([lax.axis_index(a) for a in ("c", "zl", "zh")]).astype(jnp.int32)
+    payload, ring = call(
         functools.partial(rows_kernel, quarter),
-        jax.ShapeDtypeStruct((BLOCK, half + LANES), BF16),
+        (
+            jax.ShapeDtypeStruct((BLOCK, half + LANES), BF16),
+            jax.ShapeDtypeStruct((PLANE * 2 * RING, eighth), BF16),
+        ),
         where, x_rows, route_ids.astype(F32), router.T,
     )
     blocks = [payload] + [z_send(payload, -k) for k in REACH[1:]]
-
+    ring = lax.all_to_all(
+        ring.reshape(PLANE, 2 * RING, eighth), ("y", "xh", "xl"), 0, 0, tiled=True
+    ).reshape(PLANE * 2 * RING, eighth)
     payload, queries = lax.optimization_barrier((payload, queries))
     attn_out = attention_block(queries, cache, lengths)
-    blocks, attn_out = lax.optimization_barrier((blocks, attn_out))
+    blocks, ring, attn_out = lax.optimization_barrier((blocks, ring, attn_out))
+    ups, downs = [ring], [ring]
+    for _ in range(3):
+        ups.append(z_send(ups[-1], -1))
+        downs.append(z_send(downs[-1], 1))
+    middle = PLANE * RING
+    ring = call(
+        ring_kernel,
+        jax.ShapeDtypeStruct((PLANE * 2 * RING, ZALL * eighth), BF16),
+        *ups, z_send(ups[-1][:middle], -1), z_send(downs[-1][middle:], 1), *downs[:0:-1],
+    )
+    ring_beside = lax.ppermute(ring, "c", SWAP)
     packed, marks = call(
         functools.partial(pack_kernel, quarter),
         (
-            jax.ShapeDtypeStruct((EXPERTS, 2, BLOCK, width), BF16),
+            jax.ShapeDtypeStruct((EXPERTS, 2, BLOCK, PLAIN * eighth), BF16),
             jax.ShapeDtypeStruct((ZLO * BLOCK, LANES), BF16),
         ),
         *blocks,
     )
     arrived = lax.all_to_all(
-        packed.reshape(PLANE, BLOCK, width), ("y", "xh", "xl"), 0, 0, tiled=True
-    ).reshape(PLANE * BLOCK, width)
+        packed.reshape(PLANE, BLOCK, PLAIN * eighth), ("y", "xh", "xl"), 0, 0, tiled=True
+    ).reshape(PLANE * BLOCK, PLAIN * eighth)
     beside = lax.ppermute(arrived, "c", SWAP)
     rows = PLANE * (BLOCK + ZLO)
     partial = jax.ShapeDtypeStruct((rows, hidden_count), F32)
     gate, up = call(
         functools.partial(own_kernel, quarter),
         (partial, partial),
-        where, arrived, w_gate, w_up,
+        where, arrived, ring, w_gate, w_up,
     )
     pieces = jax.ShapeDtypeStruct((PLANE * BLOCK, width), BF16)
     hidden, away = call(
         functools.partial(other_kernel, quarter),
         (jax.ShapeDtypeStruct((rows, hidden_count), BF16), pieces),
-        where, beside, w_gate, w_up, w_down, gate, up,
+        where, beside, ring_beside, w_gate, w_up, w_down, gate, up,
     )
     got = lax.ppermute(away, "c", SWAP)
     summed = call(

time: 127 us -> 148 us (1.17)
  starting transfers between devices: 7.72 us -> 25.9 us
  waiting for transfers between devices: 6.71 us -> 17.1 us
  blocking collectives: 90.9 us -> 80.8 us
  Pallas kernels: 10.6 us -> 12.4 us
    all_to_all x1, blocking collectives: 36.9 us -> 25.3 us  [shards(): lax.all_to_all(packed.reshape(PLANE, BLOCK, PLAIN * eighth), ('y', 'xh',...]
    ppermute x3 -> x11, waiting for transfers between devices: 0.01 us -> 11.4 us  [z_send(): return lax.ppermute(value, ('zl', 'zh'), z_pairs(step))]
    ppermute x3 -> x11, starting transfers between devices: 7.5 us -> 18.1 us  [z_send(): return lax.ppermute(value, ('zl', 'zh'), z_pairs(step))]
    all_to_all x0 -> x1, starting transfers between devices: none -> 7.04 us  [shards(): lax.all_to_all(ring.reshape(PLANE, 2 * RING, eighth), ('y', 'xh', 'xl'),...]
    ppermute x1, waiting for transfers between devices: 2.39 us -> 0.01 us  [shards(): beside = lax.ppermute(arrived, 'c', SWAP)]
    pallas_call x6 -> x7, Pallas kernels: 10.6 us -> 12.4 us  [call(): pl.pallas_call(kernel, out_shape=out_shape, in_specs=at, out_specs=jax.tr...]
    all_to_all x0 -> x1, waiting for transfers between devices: none -> 1.69 us  [shards(): lax.all_to_all(ring.reshape(PLANE, 2 * RING, eighth), ('y', 'xh', 'xl'),...]
  transfers between devices with their start and end apart: 5 -> 15, of which waited for: 2 -> 6; matrix products, arithmetic and copies ran while one was open for 5% -> 5% of each run, Pallas kernels for 2% -> 2%
where the time goes in v5:
time: 148 us; the launch traced here: 147 us
  blocking collectives  80.8 us (55%)
  starting transfers between devices  25.9 us (18%)
  waiting for transfers between devices  17.1 us (12%)
  Pallas kernels  12.4 us (8%)
  matrix products  4.71 us (3%)
  local copies, waits for them, and re-layouts  3.46 us (2%)
  other arithmetic  2.18 us (1%)
    all_to_all x1, blocking collectives, shards(): lax.all_to_all(summed.reshape(PLANE, BLOCK, width), ('y', 'xh', 'xl'), 0,...  34.1 us
    all_to_all x1, blocking collectives, shards(): lax.all_to_all(packed.reshape(PLANE, BLOCK, PLAIN * eighth), ('y', 'xh',...  25.3 us
    all_to_all x1, blocking collectives, shards(): parts = lax.all_to_all(parts, ('zl', 'zh'), 0, 0, tiled=True)  21.5 us
    ppermute x11, starting transfers between devices, z_send(): return lax.ppermute(value, ('zl', 'zh'), z_pairs(step))  18.1 us
    pallas_call x7, Pallas kernels, call(): pl.pallas_call(kernel, out_shape=out_shape, in_specs=at, out_specs=jax.tr...  12.4 us
    ppermute x11, waiting for transfers between devices, z_send(): return lax.ppermute(value, ('zl', 'zh'), z_pairs(step))  11.4 us
    all_to_all x1, starting transfers between devices, shards(): lax.all_to_all(ring.reshape(PLANE, 2 * RING, eighth), ('y', 'xh', 'xl'),...  7.04 us
    ppermute x1, waiting for transfers between devices, shards(): got = lax.ppermute(away, 'c', SWAP)  4.07 us
  transfers between devices with their start and end apart: 15, of which 6 were waited for; matrix products, arithmetic and copies ran while one was open for 5% of the time, Pallas kernels for 2%

profile of v5, /device:TPU:32, one launch (start us, length us, event | category | flops | bytes accessed | tf_op | source)
XLA Modules:
  0.0 147.4 jit_solution(15846125392558863757)
XLA Ops:
  0.6 0.7 convert_element_type.11
  1.3 0.1 copy.12.ids
  1.4 0.1 pad_add_fusion.where.core
  1.5 0.9 copy-done.3
  2.4 0.9 copy-done.4
  3.4 1.3 shard_map.104
  4.6 2.0 %collective-permute-start.2 = (bf16[16,3712]{1,0:T(8,128)(2,1)S(1)}, bf16[16,3712]{1,0:T(8,128)(2,1)S(1)}, u32[]{:S(2)}, u32[]{:S(2)}) collective-permute-start(bf16[16,3712]{1,0:T(8,128)(2,1)S(1)} %get-tuple-element.20.refs_0_), channel_id=1, source_target_pairs={{0,4},{4,8},{8,12},{12,2},{2,6},{6,10},{10,14},{14,0},{1,5},{5,9},... | collective-permute-start | bytes 356360 | tf_op jit(solution)/shard_map/ppermute | solution.py:38
  6.6 3.6 %collective-permute-start.1 = (bf16[16,3712]{1,0:T(8,128)(2,1)S(1)}, bf16[16,3712]{1,0:T(8,128)(2,1)S(1)}, u32[]{:S(2)}, u32[]{:S(2)}) collective-permute-start(bf16[16,3712]{1,0:T(8,128)(2,1)S(1)} %get-tuple-element.20.refs_0_), channel_id=1, source_target_pairs={{0,10},{4,14},{8,0},{12,4},{2,8},{6,12},{10,2},{14,6},{1,11},{5,15... | collective-permute-start | bytes 356360 | tf_op jit(solution)/shard_map/ppermute | solution.py:38
  10.2 1.9 %collective-permute-start = (bf16[16,3712]{1,0:T(8,128)(2,1)S(1)}, bf16[16,3712]{1,0:T(8,128)(2,1)S(1)}, u32[]{:S(2)}, u32[]{:S(2)}) collective-permute-start(bf16[16,3712]{1,0:T(8,128)(2,1)S(1)} %get-tuple-element.20.refs_0_), channel_id=1, source_target_pairs={{0,14},{4,0},{8,4},{12,8},{2,12},{6,2},{10,6},{14,10},{1,15},{5,1}... | collective-permute-start | bytes 356360 | tf_op jit(solution)/shard_map/ppermute | solution.py:38
  12.1 0.7 reshape.47
  12.8 7.0 %all-to-all-start = ((bf16[16,4,896]{2,1,0:T(4,128)(2,1)}), bf16[16,4,896]{2,1,0:T(4,128)(2,1)S(1)}, u32[]{:S(2)}, u32[]{:S(2)}) async-start(bf16[16,4,896]{2,1,0:T(4,128)(2,1)} %reshape.47), calls=%async_computation | async-start | bytes 229376 | tf_op jit(solution)/shard_map/all_to_all | solution.py:325
  19.9 0.7 iota_compare_fusion
  20.6 2.6 %fusion.26 = (f32[4,64]{1,0:T(4,128)S(1)}, bf16[4,64,1024]{2,1,0:T(8,128)(2,1)S(1)}) fusion(pred[4,1024]{1,0:T(4,128)(4,1)S(1)} %iota_compare_fusion, bf16[4,1024,512]{2,1,0:T(8,128)(2,1)} %param.16, bf16[1,4,64,256]{3,1,2,0:T(4,128)(2,1)} %bitcast.31), kind=kOutput, calls=%fused_computation.18 | convolution fusion | flops 135791616 | bytes 2761728 | tf_op jit(solution)/shard_map/sub | solution.py:302
  23.2 2.1 %fusion.20 = bf16[1,4,64,256]{3,2,1,0:T(8,128)(2,1)S(1)} fusion(bf16[4,1024,512]{2,1,0:T(8,128)(2,1)} %param.16, bf16[4,64,1024]{2,1,0:T(8,128)(2,1)S(1)} %get-tuple-element.33, f32[4,64]{1,0:T(4,128)S(1)} %get-tuple-element.32), kind=kOutput, calls=%fused_computation.12 | convolution fusion | flops 134348800 | bytes 2753536 | tf_op jit(solution)/shard_map/bhp,bpd->bhd/dot_general | solution.py:304
  25.3 0.8 copy.14
  26.1 1.7 %all-to-all-done = bf16[16,4,896]{2,1,0:T(4,128)(2,1)S(1)} async-done(((bf16[16,4,896]{2,1,0:T(4,128)(2,1)}), bf16[16,4,896]{2,1,0:T(4,128)(2,1)S(1)}, u32[]{:S(2)}, u32[]{:S(2)}) %all-to-all-start) | async-done | bytes 114720 | tf_op jit(solution)/shard_map/all_to_all | solution.py:325
  27.8 0.0 collective-permute-done.refs_1_
  27.8 0.8 shard_map.105
  28.6 0.0 copy-start.1
  28.7 0.0 copy-start.2
  28.7 25.3 %all_to_all.20 = bf16[16,16,2688]{2,1,0:T(8,128)(2,1)S(1)} all-to-all(bf16[16,16,2688]{2,1,0:T(8,128)(2,1)S(1)} %bitcast.28), channel_id=1, replica_groups=mesh['y'=4,'xh'=2,'xl'=2,'zl'=4,'zh'=2,'c'=2] {'y','xh','xl'}, dimensions={0} | all-to-all | bytes 2752512 | tf_op jit(solution)/shard_map/all_to_all | solution.py:350
  53.9 0.0 collective-permute-start.3
  53.9 0.2 collective-permute-start.8
  54.2 1.8 %collective-permute-start.4 = (bf16[64,896]{1,0:T(8,128)(2,1)S(1)}, bf16[64,896]{1,0:T(8,128)(2,1)S(1)}, u32[]{:S(2)}, u32[]{:S(2)}) collective-permute-start(bf16[64,896]{1,0:T(8,128)(2,1)S(1)} %reshape.48.refs_0_), channel_id=1, source_target_pairs={{0,14},{4,0},{8,4},{12,8},{2,12},{6,2},{10,6},{14,10},{1,15},{5,1}... | collective-permute-start | bytes 344072 | tf_op jit(solution)/shard_map/ppermute | solution.py:38
  56.0 3.5 %collective-permute-done.8.refs_8_ = bf16[64,896]{1,0:T(8,128)(2,1)S(1)} collective-permute-done((bf16[64,896]{1,0:T(8,128)(2,1)S(1)}, bf16[64,896]{1,0:T(8,128)(2,1)S(1)}, u32[]{:S(2)}, u32[]{:S(2)}) %collective-permute-start.8) | collective-permute-done | bytes 114720 | tf_op jit(solution)/shard_map/ppermute | solution.py:38
  59.5 0.3 collective-permute-start.9
  59.8 2.0 %collective-permute-start.5 = (bf16[64,896]{1,0:T(8,128)(2,1)S(1)}, bf16[64,896]{1,0:T(8,128)(2,1)S(1)}, u32[]{:S(2)}, u32[]{:S(2)}) collective-permute-start(bf16[64,896]{1,0:T(8,128)(2,1)S(1)} %collective-permute-done.4.refs_1_), channel_id=1, source_target_pairs={{0,14},{4,0},{8,4},{12,8},{2,12},{6,2},{10,6},{14,10},{1,15},{5,1}... | collective-permute-start | bytes 344072 | tf_op jit(solution)/shard_map/ppermute | solution.py:38
  61.8 3.0 %collective-permute-done.9.refs_7_ = bf16[64,896]{1,0:T(8,128)(2,1)S(1)} collective-permute-done((bf16[64,896]{1,0:T(8,128)(2,1)S(1)}, bf16[64,896]{1,0:T(8,128)(2,1)S(1)}, u32[]{:S(2)}, u32[]{:S(2)}) %collective-permute-start.9) | collective-permute-done | bytes 114720 | tf_op jit(solution)/shard_map/ppermute | solution.py:38
  64.8 0.0 collective-permute-start.10
  64.8 0.0 collective-permute-done.5.refs_2_
  64.8 3.0 %collective-permute-start.6 = (bf16[64,896]{1,0:T(8,128)(2,1)S(1)}, bf16[64,896]{1,0:T(8,128)(2,1)S(1)}, u32[]{:S(2)}, u32[]{:S(2)}) collective-permute-start(bf16[64,896]{1,0:T(8,128)(2,1)S(1)} %collective-permute-done.5.refs_2_), channel_id=1, source_target_pairs={{0,14},{4,0},{8,4},{12,8},{2,12},{6,2},{10,6},{14,10},{1,15},{5,1}... | collective-permute-start | bytes 344072 | tf_op jit(solution)/shard_map/ppermute | solution.py:38
  67.8 2.8 %collective-permute-done.10.refs_6_ = bf16[64,896]{1,0:T(8,128)(2,1)S(1)} collective-permute-done((bf16[64,896]{1,0:T(8,128)(2,1)S(1)}, bf16[64,896]{1,0:T(8,128)(2,1)S(1)}, u32[]{:S(2)}, u32[]{:S(2)}) %collective-permute-start.10) | collective-permute-done | bytes 114720 | tf_op jit(solution)/shard_map/ppermute | solution.py:38
  70.6 3.3 %collective-permute-start.7 = (bf16[32,896]{1,0:T(8,128)(2,1)S(1)}, bf16[32,896]{1,0:T(8,128)(2,1)S(1)}, u32[]{:S(2)}, u32[]{:S(2)}) collective-permute-start(bf16[32,896]{1,0:T(8,128)(2,1)S(1)} %slice.16), channel_id=1, source_target_pairs={{0,14},{4,0},{8,4},{12,8},{2,12},{6,2},{10,6},{14,10},{1,15},{5,1}... | collective-permute-start | bytes 172040 | tf_op jit(solution)/shard_map/ppermute | solution.py:38
  73.9 2.0 %collective-permute-done.11.refs_5_ = bf16[32,896]{1,0:T(8,128)(2,1)S(1)} collective-permute-done((bf16[32,896]{1,0:T(8,128)(2,1)S(1)}, bf16[32,896]{1,0:T(8,128)(2,1)S(1)}, u32[]{:S(2)}, u32[]{:S(2)}) %collective-permute-start.11) | collective-permute-done | bytes 57376 | tf_op jit(solution)/shard_map/ppermute | solution.py:38
  75.9 0.0 collective-permute-done.7.refs_4_
  75.9 0.1 shard_map.106.ring
  76.0 0.3 collective-permute-start.12
  76.3 0.0 copy-start
  76.3 2.6 %shard_map.107 = (f32[320,160]{1,0:T(8,128)S(1)}, f32[320,160]{1,0:T(8,128)S(1)}) custom-call(s32[3]{0:T(128)S(1)} %pad_add_fusion.where.core, bf16[256,2688]{1,0:T(8,128)(2,1)S(1)} %bitcast.27, bf16[64,7168]{1,0:T(8,128)(2,1)S(1)} %shard_map.106.ring, bf16[160,7168]{1,0:T(8,128)(2,1)S(1)} %bitcast.20, bf16[160,7168]{1,0:T(8,128)(2,1)S(1)} %bitcast.22), custom_call_target="tpu_custom_call" | custom-call | tf_op jit(solution)/shard_map/pallas_call | solution.py:82
  78.9 0.0 collective-permute-done.3.block
  78.9 3.9 %shard_map.108 = (bf16[320,160]{1,0:T(8,128)(2,1)S(1)}, bf16[256,4480]{1,0:T(8,128)(2,1)S(1)}) custom-call(s32[3]{0:T(128)S(1)} %pad_add_fusion.where.core, bf16[256,2688]{1,0:T(8,128)(2,1)S(1)} %collective-permute-done.3.block, bf16[64,7168]{1,0:T(8,128)(2,1)S(1)} %collective-permute-done.12.ring, bf16[160,7168]{1,0:T(8,128)(2,1)S(1)} %bitcast.21, ...), custom_call_target="tpu_custom_call" | custom-call | tf_op jit(solution)/shard_map/pallas_call | solution.py:82
  82.8 0.6 collective-permute-start.13
  83.3 4.1 %collective-permute-done.13.got = bf16[256,4480]{1,0:T(8,128)(2,1)S(1)} collective-permute-done((bf16[256,4480]{1,0:T(8,128)(2,1)S(1)}, bf16[256,4480]{1,0:T(8,128)(2,1)S(1)}, u32[]{:S(2)}, u32[]{:S(2)}) %collective-permute-start.13) | collective-permute-done | bytes 2293792 | tf_op jit(solution)/shard_map/ppermute | solution.py:367
  87.4 1.7 %shard_map.109 = bf16[256,4480]{1,0:T(8,128)(2,1)S(1)} custom-call(s32[3]{0:T(128)S(1)} %pad_add_fusion.where.core, bf16[320,160]{1,0:T(8,128)(2,1)S(1)} %get-tuple-element.28.hidden, bf16[160,7168]{1,0:T(8,128)(2,1)S(1)} %copy-done, bf16[256,4480]{1,0:T(8,128)(2,1)S(1)} %collective-permute-done.13.got), custom_call_target="tpu_custom_call" | custom-call | tf_op jit(solution)/shard_map/pallas_call | solution.py:82
  89.2 34.1 %all_to_all.21 = bf16[16,16,4480]{2,1,0:T(8,128)(2,1)S(1)} all-to-all(bf16[16,16,4480]{2,1,0:T(8,128)(2,1)S(1)} %bitcast.24), channel_id=1, replica_groups=mesh['y'=4,'xh'=2,'xl'=2,'zl'=4,'zh'=2,'c'=2] {'y','xh','xl'}, dimensions={0} | all-to-all | bytes 4587520 | tf_op jit(solution)/shard_map/all_to_all | solution.py:373
  123.2 2.1 %shard_map.110 = bf16[8,16,1792]{2,1,0:T(8,128)(2,1)S(1)} custom-call(s32[3]{0:T(128)S(1)} %pad_add_fusion.where.core, bf16[256,4480]{1,0:T(8,128)(2,1)S(1)} %bitcast.25, bf16[64,128]{1,0:T(8,128)(2,1)S(1)} %get-tuple-element.30.marks), custom_call_target="tpu_custom_call" | custom-call | tf_op jit(solution)/shard_map/pallas_call | solution.py:82
  125.3 21.5 %all_to_all.22 = bf16[8,16,1792]{2,1,0:T(8,128)(2,1)S(1)} all-to-all(bf16[8,16,1792]{2,1,0:T(8,128)(2,1)S(1)} %shard_map.110), channel_id=1, replica_groups=mesh['y'=4,'xh'=2,'xl'=2,'zl'=4,'zh'=2,'c'=2] {'zl','zh'}, dimensions={0} | all-to-all | bytes 917504 | tf_op jit(solution)/shard_map/all_to_all | solution.py:382
  146.7 0.7 reduce_sum.22
  (14 shorter events, 0.1 us)
Async XLA Ops:
  1.5 0.9 copy-start.3
  2.4 0.9 copy-start.4
  4.6 23.2 %collective-permute-start.2 = (bf16[16,3712]{1,0:T(8,128)(2,1)S(1)}, bf16[16,3712]{1,0:T(8,128)(2,1)S(1)}, u32[]{:S(2)}, u32[]{:S(2)}) collective-permute-start(bf16[16,3712]{1,0:T(8,128)(2,1)S(1)} %get-tuple-element.20.refs_0_), channel_id=1, source_target_pairs={{0,4},{4,8},{8,12},{12,2},{2,6},{6,10},{10,14},{14,0},{1,5},{5,9},... | collective-permute-start | bytes 356360 | tf_op jit(solution)/shard_map/ppermute | solution.py:38
  6.6 21.2 %collective-permute-start.1 = (bf16[16,3712]{1,0:T(8,128)(2,1)S(1)}, bf16[16,3712]{1,0:T(8,128)(2,1)S(1)}, u32[]{:S(2)}, u32[]{:S(2)}) collective-permute-start(bf16[16,3712]{1,0:T(8,128)(2,1)S(1)} %get-tuple-element.20.refs_0_), channel_id=1, source_target_pairs={{0,10},{4,14},{8,0},{12,4},{2,8},{6,12},{10,2},{14,6},{1,11},{5,15... | collective-permute-start | bytes 356360 | tf_op jit(solution)/shard_map/ppermute | solution.py:38
  10.2 17.6 %collective-permute-start = (bf16[16,3712]{1,0:T(8,128)(2,1)S(1)}, bf16[16,3712]{1,0:T(8,128)(2,1)S(1)}, u32[]{:S(2)}, u32[]{:S(2)}) collective-permute-start(bf16[16,3712]{1,0:T(8,128)(2,1)S(1)} %get-tuple-element.20.refs_0_), channel_id=1, source_target_pairs={{0,14},{4,0},{8,4},{12,8},{2,12},{6,2},{10,6},{14,10},{1,15},{5,1}... | collective-permute-start | bytes 356360 | tf_op jit(solution)/shard_map/ppermute | solution.py:38
  12.8 14.9 %all-to-all-start = ((bf16[16,4,896]{2,1,0:T(4,128)(2,1)}), bf16[16,4,896]{2,1,0:T(4,128)(2,1)S(1)}, u32[]{:S(2)}, u32[]{:S(2)}) async-start(bf16[16,4,896]{2,1,0:T(4,128)(2,1)} %reshape.47), calls=%async_computation | async-start | bytes 229376 | tf_op jit(solution)/shard_map/all_to_all | solution.py:325
  28.6 47.6 %copy-start.1 = (bf16[7168,160]{0,1:T(8,128)(2,1)S(1)}, bf16[7168,160]{0,1:T(8,128)(2,1)}, u32[]{:S(2)}) copy-start(bf16[7168,160]{0,1:T(8,128)(2,1)} %param.12) | copy-start | bytes 6881284
  28.7 47.6 %copy-start.2 = (bf16[7168,160]{0,1:T(8,128)(2,1)S(1)}, bf16[7168,160]{0,1:T(8,128)(2,1)}, u32[]{:S(2)}) copy-start(bf16[7168,160]{0,1:T(8,128)(2,1)} %param.13) | copy-start | bytes 6881284
  53.9 24.9 %collective-permute-start.3 = (bf16[256,2688]{1,0:T(8,128)(2,1)S(1)}, bf16[256,2688]{1,0:T(8,128)(2,1)S(1)}, u32[]{:S(2)}, u32[]{:S(2)}) collective-permute-start(bf16[256,2688]{1,0:T(8,128)(2,1)S(1)} %bitcast.26), channel_id=1, source_target_pairs={{0,1},{1,0},{2,3},{3,2},{4,5},{5,4},{6,7},{7,6},{8,9},{9,8},{10,11... | collective-permute-start | bytes 4128776 | tf_op jit(solution)/shard_map/ppermute | solution.py:353
  53.9 5.6 %collective-permute-start.8 = (bf16[64,896]{1,0:T(8,128)(2,1)S(1)}, bf16[64,896]{1,0:T(8,128)(2,1)S(1)}, u32[]{:S(2)}, u32[]{:S(2)}) collective-permute-start(bf16[64,896]{1,0:T(8,128)(2,1)S(1)} %reshape.48.refs_0_), channel_id=1, source_target_pairs={{0,4},{4,8},{8,12},{12,2},{2,6},{6,10},{10,14},{14,0},{1,5},{5,9},... | collective-permute-start | bytes 344072 | tf_op jit(solution)/shard_map/ppermute | solution.py:38
  54.2 5.6 %collective-permute-start.4 = (bf16[64,896]{1,0:T(8,128)(2,1)S(1)}, bf16[64,896]{1,0:T(8,128)(2,1)S(1)}, u32[]{:S(2)}, u32[]{:S(2)}) collective-permute-start(bf16[64,896]{1,0:T(8,128)(2,1)S(1)} %reshape.48.refs_0_), channel_id=1, source_target_pairs={{0,14},{4,0},{8,4},{12,8},{2,12},{6,2},{10,6},{14,10},{1,15},{5,1}... | collective-permute-start | bytes 344072 | tf_op jit(solution)/shard_map/ppermute | solution.py:38
  59.5 5.3 %collective-permute-start.9 = (bf16[64,896]{1,0:T(8,128)(2,1)S(1)}, bf16[64,896]{1,0:T(8,128)(2,1)S(1)}, u32[]{:S(2)}, u32[]{:S(2)}) collective-permute-start(bf16[64,896]{1,0:T(8,128)(2,1)S(1)} %collective-permute-done.8.refs_8_), channel_id=1, source_target_pairs={{0,4},{4,8},{8,12},{12,2},{2,6},{6,10},{10,14},{14,0},{1,5},{5,9},... | collective-permute-start | bytes 344072 | tf_op jit(solution)/shard_map/ppermute | solution.py:38
  59.8 5.0 %collective-permute-start.5 = (bf16[64,896]{1,0:T(8,128)(2,1)S(1)}, bf16[64,896]{1,0:T(8,128)(2,1)S(1)}, u32[]{:S(2)}, u32[]{:S(2)}) collective-permute-start(bf16[64,896]{1,0:T(8,128)(2,1)S(1)} %collective-permute-done.4.refs_1_), channel_id=1, source_target_pairs={{0,14},{4,0},{8,4},{12,8},{2,12},{6,2},{10,6},{14,10},{1,15},{5,1}... | collective-permute-start | bytes 344072 | tf_op jit(solution)/shard_map/ppermute | solution.py:38
  64.8 5.7 %collective-permute-start.10 = (bf16[64,896]{1,0:T(8,128)(2,1)S(1)}, bf16[64,896]{1,0:T(8,128)(2,1)S(1)}, u32[]{:S(2)}, u32[]{:S(2)}) collective-permute-start(bf16[64,896]{1,0:T(8,128)(2,1)S(1)} %collective-permute-done.9.refs_7_), channel_id=1, source_target_pairs={{0,4},{4,8},{8,12},{12,2},{2,6},{6,10},{10,14},{14,0},{1,5},{5,9},... | collective-permute-start | bytes 344072 | tf_op jit(solution)/shard_map/ppermute | solution.py:38
  64.8 5.8 %collective-permute-start.6 = (bf16[64,896]{1,0:T(8,128)(2,1)S(1)}, bf16[64,896]{1,0:T(8,128)(2,1)S(1)}, u32[]{:S(2)}, u32[]{:S(2)}) collective-permute-start(bf16[64,896]{1,0:T(8,128)(2,1)S(1)} %collective-permute-done.5.refs_2_), channel_id=1, source_target_pairs={{0,14},{4,0},{8,4},{12,8},{2,12},{6,2},{10,6},{14,10},{1,15},{5,1}... | collective-permute-start | bytes 344072 | tf_op jit(solution)/shard_map/ppermute | solution.py:38
  70.5 5.4 %collective-permute-start.11 = (bf16[32,896]{1,0:T(8,128)(2,1)S(1)}, bf16[32,896]{1,0:T(8,128)(2,1)S(1)}, u32[]{:S(2)}, u32[]{:S(2)}) collective-permute-start(bf16[32,896]{1,0:T(8,128)(2,1)S(1)} %slice.17), channel_id=1, source_target_pairs={{0,4},{4,8},{8,12},{12,2},{2,6},{6,10},{10,14},{14,0},{1,5},{5,9},... | collective-permute-start | bytes 172040 | tf_op jit(solution)/shard_map/ppermute | solution.py:38
  70.6 5.4 %collective-permute-start.7 = (bf16[32,896]{1,0:T(8,128)(2,1)S(1)}, bf16[32,896]{1,0:T(8,128)(2,1)S(1)}, u32[]{:S(2)}, u32[]{:S(2)}) collective-permute-start(bf16[32,896]{1,0:T(8,128)(2,1)S(1)} %slice.16), channel_id=1, source_target_pairs={{0,14},{4,0},{8,4},{12,8},{2,12},{6,2},{10,6},{14,10},{1,15},{5,1}... | collective-permute-start | bytes 172040 | tf_op jit(solution)/shard_map/ppermute | solution.py:38
  76.0 2.9 %collective-permute-start.12 = (bf16[64,7168]{1,0:T(8,128)(2,1)S(1)}, bf16[64,7168]{1,0:T(8,128)(2,1)S(1)}, u32[]{:S(2)}, u32[]{:S(2)}) collective-permute-start(bf16[64,7168]{1,0:T(8,128)(2,1)S(1)} %shard_map.106.ring), channel_id=1, source_target_pairs={{0,1},{1,0},{2,3},{3,2},{4,5},{5,4},{6,7},{7,6},{8,9},{9,8},{10,11... | collective-permute-start | bytes 2752520 | tf_op jit(solution)/shard_map/ppermute | solution.py:341
  76.3 2.6 %copy-start = (bf16[160,7168]{1,0:T(8,128)(2,1)S(1)}, bf16[160,7168]{1,0:T(8,128)(2,1)}, u32[]{:S(2)}) copy-start(bf16[160,7168]{1,0:T(8,128)(2,1)} %w_down.3) | copy-start | bytes 6881284
  82.8 4.6 %collective-permute-start.13 = (bf16[256,4480]{1,0:T(8,128)(2,1)S(1)}, bf16[256,4480]{1,0:T(8,128)(2,1)S(1)}, u32[]{:S(2)}, u32[]{:S(2)}) collective-permute-start(bf16[256,4480]{1,0:T(8,128)(2,1)S(1)} %get-tuple-element.29), channel_id=1, source_target_pairs={{0,1},{1,0},{2,3},{3,2},{4,5},{5,4},{6,7},{7,6},{8,9},{9,8},{10,11... | collective-permute-start | bytes 6881288 | tf_op jit(solution)/shard_map/ppermute | solution.py:367

commit v6 on v4

--- a/solution.py
+++ b/solution.py
@@ -20,6 +20,7 @@
 HIGH, LOW = 64, 72
 BF16, F32 = jnp.bfloat16, jnp.float32
 VMEM_BYTES = 40 * 1024 * 1024
+ALL_VMEM_BYTES = 60 * 1024 * 1024
 
 
 def place(z):
@@ -70,6 +71,10 @@
 
 def dot_t(a, b):
     return lax.dot_general(a, b, (((1,), (1,)), ((), ())), preferred_element_type=F32)
+
+
+def scalars(array):
+    return pl.BlockSpec(memory_space=pltpu.SMEM)
 
 
 def call(kernel, out_shape, *args):
@@ -86,8 +91,11 @@
 def rows_kernel(quarter, where, x_rows, ids, router, out):
     half = 2 * quarter
     values = x_rows[...].astype(F32)
-    first, second = ids[:, 0:1], ids[:, 1:2]
     row, lane = grid(BLOCK, LANES)
+    first, second = jnp.zeros_like(row), jnp.zeros_like(row)
+    for r in range(BLOCK):
+        first = jnp.where(row == r, ids[0, r], first)
+        second = jnp.where(row == r, ids[1, r], second)
     squashed, total = [], 0.0
     for e in range(EXPERTS):
         logit = jnp.sum(values * router[e : e + 1, :], axis=1, keepdims=True)
@@ -156,16 +164,16 @@
     return gate, up
 
 
-def experts_out(quarter, core, hidden, w_down):
-    half, eighth = 2 * quarter, quarter // 2
-    mains, rests = [], []
+def columns(quarter, core, f):
+    return pl.ds(pl.multiple_of(f * 2 * quarter + core * quarter, LANES), quarter)
+
+
+def tails_out(quarter, core, hidden, w_down):
+    tails = []
     for f in range(2):
-        at = pl.ds(pl.multiple_of(f * half + core * quarter, LANES), quarter)
-        y = dot(hidden, w_down[:, at])
-        mains.append(y[: PLANE * BLOCK])
-        tail = y[PLANE * BLOCK :]
-        rests += [tail[:, :eighth], tail[:, eighth:]]
-    return mains, jnp.concatenate(rests, axis=0)
+        y = dot(hidden[PLANE * BLOCK :], w_down[:, columns(quarter, core, f)])
+        tails += [y[:, : quarter // 2], y[:, quarter // 2 :]]
+    return jnp.concatenate(tails, axis=0)
 
 
 def own_kernel(quarter, core, block, w_gate, w_up, gate_out, up_out):
@@ -177,29 +185,33 @@
 def other_kernel(
     quarter, core, block, w_gate, w_up, w_down, gate_in, up_in, hidden_out, away
 ):
-    half = 2 * quarter
     there = 1 - core[0]
     gate, up = experts_in(quarter, there, block, w_gate, w_up)
     gate, up = gate + gate_in[...], up + up_in[...]
     hidden = (gate * jax.nn.sigmoid(gate) * up).astype(BF16)
     hidden_out[...] = hidden
-    mains, rest = experts_out(quarter, there, hidden, w_down)
-    for f in range(2):
-        away[:, f * quarter : (f + 1) * quarter] = mains[f].astype(BF16)
-    away[:, half:] = dot(shuffle_table(True), rest.astype(BF16)).astype(BF16)
-
-
-def sum_kernel(quarter, core, hidden, w_down, got, out):
-    half = 2 * quarter
-    mains, rest = experts_out(quarter, core[0], hidden[...], w_down)
-    for f in range(2):
-        at = slice(f * quarter, (f + 1) * quarter)
-        out[:, at] = (mains[f] + got[:, at].astype(F32)).astype(BF16)
+    away[...] = dot(hidden[: PLANE * BLOCK], w_down[:, columns(quarter, there, 0)]).astype(BF16)
+
+
+def away_kernel(quarter, where, hidden, w_down, away):
+    there = 1 - where[0]
+    main = dot(hidden[: PLANE * BLOCK, :], w_down[:, columns(quarter, there, 1)])
+    away[:, :quarter] = main.astype(BF16)
+    rest = tails_out(quarter, there, hidden[...], w_down).astype(BF16)
+    away[:, quarter:] = dot(shuffle_table(True), rest).astype(BF16)
+
+
+def sum_kernel(quarter, where, hidden, w_down, got_first, got_second, out):
+    for f, got in enumerate((got_first, got_second)):
+        main = dot(hidden[: PLANE * BLOCK, :], w_down[:, columns(quarter, where[0], f)])
+        main = main + got[:, :quarter].astype(F32)
+        out[:, f * quarter : (f + 1) * quarter] = main.astype(BF16)
+    rest = tails_out(quarter, where[0], hidden[...], w_down)
     high = rest.astype(BF16)
     low = (rest - high.astype(F32)).astype(BF16)
     unshuffle = shuffle_table(True)
     rest = dot(unshuffle, high) + dot(unshuffle, low)
-    out[:, half:] = (rest + got[:, half:].astype(F32)).astype(BF16)
+    out[:, 2 * quarter :] = (rest + got_second[:, quarter:].astype(F32)).astype(BF16)
 
 
 def combine_kernel(quarter, where, back, marks, out):
@@ -215,17 +227,17 @@
     row, slot = grid(ZLO * BLOCK, PLANE * BLOCK)
     main = dot(chosen, back_main) * ones(fifth(slot & 15) == row >> 4)
     rest = dot(chosen, back_rest) * ones(row >> 4 == 3)
-    total = dot((main * wide_high).astype(BF16), back[:, :half]) + dot(
-        (main * wide_low).astype(BF16), back[:, :half]
-    )
-    tail = back[:, half:]
-    pieces = []
-    for i in range(4):
-        mask = rest * ones((slot >> 2) & 3 == i)
-        pieces.append(
-            dot((mask * wide_high).astype(BF16), tail) + dot((mask * wide_low).astype(BF16), tail)
-        )
-    total = total + jnp.concatenate(pieces, axis=1)
+    wides = (wide_high, wide_low)
+    count = ZLO * BLOCK
+    both = dot(jnp.concatenate([(main * w).astype(BF16) for w in wides], axis=0), back[:, :half])
+    picked = [rest * ones((slot >> 2) & 3 == i) for i in range(4)]
+    stack = jnp.concatenate([(p * w).astype(BF16) for p in picked for w in wides], axis=0)
+    tails = dot(stack, back[:, half:])
+    pieces = [
+        tails[2 * i * count : (2 * i + 1) * count] + tails[(2 * i + 1) * count : (2 * i + 2) * count]
+        for i in range(4)
+    ]
+    total = both[:count] + both[count:] + jnp.concatenate(pieces, axis=1)
     for k in range(ZLO):
         owner = (where[1] + (REACH[k] % ZLO)) & (ZLO - 1)
         for f in range(2):
@@ -233,24 +245,37 @@
             out[owner * 2 + f] = piece.astype(BF16)
 
 
+def attention_kernel(lengths, queries, cache, out):
+    live_count = lengths[pl.program_id(0)]
+    head_dim = queries.shape[2]
+    scores = dot_t(queries[0], cache[0, :, :head_dim]) / math.sqrt(head_dim)
+    live = lax.broadcasted_iota(jnp.int32, scores.shape, 1) < live_count
+    scores = jnp.where(live, scores, -1e30)
+    largest = jnp.max(scores, axis=1, keepdims=True)
+    weights = jnp.where(live, jnp.exp(scores - largest), 0.0)
+    denominator = jnp.sum(weights, axis=1, keepdims=True)
+    mixed = dot(weights.astype(BF16), cache[0, :, head_dim:])
+    out[0] = (mixed / denominator).astype(BF16)
+
+
 def attention_block(queries, cache, lengths):
-    head_dim = cache.shape[2] // 2
-    head_count = queries.shape[1] // head_dim
-    requests = queries.shape[0]
-    position_count = cache.shape[1]
-    query_heads = queries.reshape(requests, head_count, head_dim)
-    key_block = cache[:, :, :head_dim]
-    value_block = cache[:, :, head_dim:]
-    scores = jnp.einsum(
-        "bhd,bpd->bhp", query_heads, key_block, preferred_element_type=F32
-    ) / math.sqrt(head_dim)
-    live = jnp.arange(position_count)[None, :] < lengths[:, None]
-    scores = jnp.where(live[:, None, :], scores, -1e30)
-    largest = jnp.max(scores, axis=2, keepdims=True)
-    weights = jnp.where(live[:, None, :], jnp.exp(scores - largest), 0.0)
-    denominator = jnp.sum(weights, axis=2, keepdims=True)
-    mixed = jnp.einsum("bhp,bpd->bhd", weights.astype(BF16), value_block, preferred_element_type=F32)
-    return (mixed / denominator).astype(BF16).reshape(requests, head_count * head_dim)
+    requests, positions, both = cache.shape
+    head_dim = both // 2
+    heads = queries.shape[1] // head_dim
+    rows = pl.BlockSpec((1, heads, head_dim), lambda i: (i, 0, 0))
+    mixed = pl.pallas_call(
+        attention_kernel,
+        grid=(requests,),
+        out_shape=jax.ShapeDtypeStruct((requests, heads, head_dim), BF16),
+        in_specs=[
+            scalars(lengths),
+            rows,
+            pl.BlockSpec((1, positions, both), lambda i: (i, 0, 0)),
+        ],
+        out_specs=rows,
+        compiler_params=pltpu.CompilerParams(vmem_limit_bytes=ALL_VMEM_BYTES),
+    )(lengths, queries.reshape(requests, heads, head_dim), cache)
+    return mixed.reshape(queries.shape)
 
 
 def shards(x_rows, route_ids, router, w_gate, w_up, w_down, queries, cache, lengths):
@@ -261,11 +286,18 @@
     half, eighth = 2 * quarter, quarter // 2
     width = half + eighth
     where = jnp.stack([lax.axis_index("c"), lax.axis_index("zl")]).astype(jnp.int32)
-    payload = call(
+    def whole(array):
+        return pl.BlockSpec(array.shape, lambda i: (0, 0))
+
+    payload = jax.ShapeDtypeStruct((BLOCK, half + LANES), BF16)
+    payload = pl.pallas_call(
         functools.partial(rows_kernel, quarter),
-        jax.ShapeDtypeStruct((BLOCK, half + LANES), BF16),
-        where, x_rows, route_ids.astype(F32), router.T,
-    )
+        grid=(1,),
+        out_shape=payload,
+        in_specs=[scalars(where), whole(x_rows), scalars(route_ids), whole(router.T)],
+        out_specs=whole(payload),
+        compiler_params=pltpu.CompilerParams(vmem_limit_bytes=ALL_VMEM_BYTES),
+    )(where, x_rows, route_ids.T, router.T)
     blocks = [payload] + [z_send(payload, -k) for k in REACH[1:]]
 
     payload, queries = lax.optimization_barrier((payload, queries))
@@ -290,17 +322,26 @@
         (partial, partial),
         where, arrived, w_gate, w_up,
     )
-    pieces = jax.ShapeDtypeStruct((PLANE * BLOCK, width), BF16)
+    main = PLANE * BLOCK
     hidden, away = call(
         functools.partial(other_kernel, quarter),
-        (jax.ShapeDtypeStruct((rows, hidden_count), BF16), pieces),
+        (
+            jax.ShapeDtypeStruct((rows, hidden_count), BF16),
+            jax.ShapeDtypeStruct((main, quarter), BF16),
+        ),
         where, beside, w_gate, w_up, w_down, gate, up,
     )
-    got = lax.ppermute(away, "c", SWAP)
+    got_first = lax.ppermute(away, "c", SWAP)
+    away = call(
+        functools.partial(away_kernel, quarter),
+        jax.ShapeDtypeStruct((main, quarter + eighth), BF16),
+        where, hidden, w_down,
+    )
+    got_second = lax.ppermute(away, "c", SWAP)
     summed = call(
         functools.partial(sum_kernel, quarter),
-        pieces,
-        where, hidden, w_down, got,
+        jax.ShapeDtypeStruct((main, width), BF16),
+        where, hidden, w_down, got_first, got_second,
     )
     returned = lax.all_to_all(
         summed.reshape(PLANE, BLOCK, width), ("y", "xh", "xl"), 0, 0, tiled=True

time: 127 us -> 126 us (level)
  Pallas kernels: 10.6 us -> 17.1 us
  matrix products: 4.72 us -> 0 us
  blocking collectives: 90.9 us -> 88.6 us
    pallas_call x0 -> x2, Pallas kernels: none -> 7.48 us  [the longest x1 5.25 us: attention_block(): pl.pallas_call(attention_kernel, grid=(requests,), out_shape=jax.ShapeDty...]
    sub x1 -> x0, matrix products: 2.64 us -> none  [attention_block(): weights = jnp.where(live[:, None, :], jnp.exp(scores - largest), 0.0)]
    all_to_all x1, blocking collectives: 20.2 us -> 17.9 us  [shards(): parts = lax.all_to_all(parts, ('zl', 'zh'), 0, 0, tiled=True)]
    dot_general x1 -> x0, matrix products: 2.07 us -> none  [attention_block(): jnp.einsum('bhp,bpd->bhd', weights.astype(BF16), value_block, preferred_e...]
    unnamed x11 -> x12, local copies, waits for them, and re-layouts: 2.65 us -> 3.26 us
    ppermute x1 -> x2, waiting for transfers between devices: 4.31 us -> 3.93 us  [the longest x1 3.93 us: shards(): got_first = lax.ppermute(away, 'c', SWAP)]
  transfers between devices with their start and end apart: 5 -> 6, of which waited for: 2 -> 2; matrix products, arithmetic and copies ran while one was open for 5% -> 3% of each run, Pallas kernels for 2% -> 6%
where the time goes in v6:
time: 126 us; the launch traced here: 125 us
  blocking collectives  88.6 us (70%)
  Pallas kernels  17.1 us (14%)
  starting transfers between devices  8.03 us (6%)
  waiting for transfers between devices  6.33 us (5%)
  local copies, waits for them, and re-layouts  3.26 us (3%)
  other arithmetic  1.34 us (1%)
    all_to_all x1, blocking collectives, shards(): lax.all_to_all(packed.reshape(PLANE, BLOCK, width), ('y', 'xh', 'xl'), 0,...  36.9 us
    all_to_all x1, blocking collectives, shards(): lax.all_to_all(summed.reshape(PLANE, BLOCK, width), ('y', 'xh', 'xl'), 0,...  33.8 us
    all_to_all x1, blocking collectives, shards(): parts = lax.all_to_all(parts, ('zl', 'zh'), 0, 0, tiled=True)  17.9 us
    pallas_call x6, Pallas kernels, call(): pl.pallas_call(kernel, out_shape=out_shape, in_specs=at, out_specs=jax.tr...  9.67 us
    ppermute x3, starting transfers between devices, z_send(): return lax.ppermute(value, ('zl', 'zh'), z_pairs(step))  7.43 us
    pallas_call x1, Pallas kernels, attention_block(): pl.pallas_call(attention_kernel, grid=(requests,), out_shape=jax.ShapeDty...  5.25 us
    ppermute x1, waiting for transfers between devices, shards(): got_first = lax.ppermute(away, 'c', SWAP)  3.93 us
    unnamed x12, local copies, waits for them, and re-layouts  3.26 us
  transfers between devices with their start and end apart: 6, of which 2 were waited for; matrix products, arithmetic and copies ran while one was open for 3% of the time, Pallas kernels for 6%

profile of v6, /device:TPU:32, one launch (start us, length us, event | category | flops | bytes accessed | tf_op | source)
XLA Modules:
  0.0 125.4 jit_solution(18049950645487254428)
XLA Ops:
  0.6 0.6 pad_add_fusion.where.core
  1.3 2.2 %shard_map.104.refs_0_ = bf16[16,3712]{1,0:T(8,128)(2,1)} custom-call(s32[2]{0:T(128)} %pad_add_fusion.where.core, bf16[16,7168]{1,0:T(8,128)(2,1)} %x_rows.1, s32[2,16]{1,0:T(2,128)} %bitcast.30, f32[8,7168]{1,0:T(8,128)} %bitcast.27), custom_call_target="tpu_custom_call" | custom-call | tf_op jit(solution)/shard_map/pallas_call | solution.py:293
  3.5 1.8 %collective-permute-start = (bf16[16,3712]{1,0:T(8,128)(2,1)}, bf16[16,3712]{1,0:T(8,128)(2,1)S(1)}, u32[]{:S(2)}, u32[]{:S(2)}) collective-permute-start(bf16[16,3712]{1,0:T(8,128)(2,1)} %shard_map.104.refs_0_), channel_id=1, source_target_pairs={{0,14},{4,0},{8,4},{12,8},{2,12},{6,2},{10,6},{14,10},{1,15},{5,1}... | collective-permute-start | bytes 356360 | tf_op jit(solution)/shard_map/ppermute | solution.py:38
  5.4 4.6 %collective-permute-start.1 = (bf16[16,3712]{1,0:T(8,128)(2,1)}, bf16[16,3712]{1,0:T(8,128)(2,1)S(1)}, u32[]{:S(2)}, u32[]{:S(2)}) collective-permute-start(bf16[16,3712]{1,0:T(8,128)(2,1)} %shard_map.104.refs_0_), channel_id=1, source_target_pairs={{0,10},{4,14},{8,0},{12,4},{2,8},{6,12},{10,2},{14,6},{1,11},{5,15... | collective-permute-start | bytes 356360 | tf_op jit(solution)/shard_map/ppermute | solution.py:38
  9.9 1.0 collective-permute-start.2
  10.9 1.6 %copy.14 = bf16[1,4,64,256]{3,2,1,0:T(8,128)(2,1)} copy(bf16[1,4,64,256]{3,1,2,0:T(4,128)(2,1)} %bitcast.28) | data formatting | bytes 262144
  12.5 0.0 copy-start.3
  12.5 5.3 %shard_map.105 = bf16[4,64,256]{2,1,0:T(8,128)(2,1)} custom-call(s32[4]{0:T(128)} %lengths.1, bf16[4,64,256]{2,1,0:T(8,128)(2,1)} %bitcast.26, bf16[4,1024,512]{2,1,0:T(8,128)(2,1)} %cache.1), custom_call_target="tpu_custom_call" | custom-call | tf_op jit(solution)/shard_map/pallas_call | solution.py:266
  17.8 1.7 %copy.12 = bf16[1,4,64,256]{3,1,2,0:T(4,128)(2,1)} copy(bf16[1,4,64,256]{3,2,1,0:T(8,128)(2,1)} %bitcast.25) | data formatting | bytes 262144
  19.4 0.0 collective-permute-done.refs_1_
  19.4 0.0 collective-permute-done.1.refs_2_
  19.4 0.0 collective-permute-done.2.refs_3_
  19.4 0.0 copy-done.3
  19.5 0.7 shard_map.106
  20.2 0.0 copy-start.1
  20.2 0.0 copy-start.2
  20.2 0.0 copy-start.4
  20.2 36.9 %all_to_all.15 = bf16[16,16,4480]{2,1,0:T(8,128)(2,1)S(1)} all-to-all(bf16[16,16,4480]{2,1,0:T(8,128)(2,1)S(1)} %bitcast.24), channel_id=1, replica_groups=mesh['y'=4,'xh'=2,'xl'=2,'zl'=4,'zh'=2,'c'=2] {'y','xh','xl'}, dimensions={0} | all-to-all | bytes 4587520 | tf_op jit(solution)/shard_map/all_to_all | solution.py:314
  57.1 0.0 collective-permute-start.3
  57.1 0.0 copy-done.1
  57.1 0.0 copy-done.2
  57.1 0.0 copy-done.4
  57.2 0.0 copy-start
  57.2 2.0 %shard_map.107 = (f32[320,160]{1,0:T(8,128)S(1)}, f32[320,160]{1,0:T(8,128)S(1)}) custom-call(s32[2]{0:T(128)S(1)} %copy-done.4, bf16[256,4480]{1,0:T(8,128)(2,1)S(1)} %bitcast.22, bf16[160,7168]{1,0:T(8,128)(2,1)S(1)} %bitcast.16, bf16[160,7168]{1,0:T(8,128)(2,1)S(1)} %bitcast.18), custom_call_target="tpu_custom_call" | custom-call | tf_op jit(solution)/shard_map/pallas_call | solution.py:82
  59.2 2.4 %collective-permute-done.3.block = bf16[256,4480]{1,0:T(8,128)(2,1)S(1)} collective-permute-done((bf16[256,4480]{1,0:T(8,128)(2,1)S(1)}, bf16[256,4480]{1,0:T(8,128)(2,1)S(1)}, u32[]{:S(2)}, u32[]{:S(2)}) %collective-permute-start.3) | collective-permute-done | bytes 2293792 | tf_op jit(solution)/shard_map/ppermute | solution.py:317
  61.6 0.0 copy-done
  61.6 2.4 %shard_map.108 = (bf16[320,160]{1,0:T(8,128)(2,1)S(1)}, bf16[256,1792]{1,0:T(8,128)(2,1)S(1)}) custom-call(s32[2]{0:T(128)S(1)} %copy-done.4, bf16[256,4480]{1,0:T(8,128)(2,1)S(1)} %collective-permute-done.3.block, bf16[160,7168]{1,0:T(8,128)(2,1)S(1)} %bitcast.17, bf16[160,7168]{1,0:T(8,128)(2,1)S(1)} %bitcast.19, bf16[160,7168]{1,0:T(8,128)(2,1)S(1)} %copy-done, ...), custom_call_target="tpu_custom_call" | custom-call | tf_op jit(solution)/shard_map/pallas_call | solution.py:82
  64.0 1.4 %shard_map.109 = bf16[256,2688]{1,0:T(8,128)(2,1)S(1)} custom-call(s32[2]{0:T(128)S(1)} %copy-done.4, bf16[320,160]{1,0:T(8,128)(2,1)S(1)} %get-tuple-element.22.hidden, bf16[160,7168]{1,0:T(8,128)(2,1)S(1)} %copy-done), custom_call_target="tpu_custom_call" | custom-call | tf_op jit(solution)/shard_map/pallas_call | solution.py:82
  65.4 0.2 collective-permute-start.5
  65.6 0.4 collective-permute-start.4
  66.0 3.9 %collective-permute-done.4.got_first = bf16[256,1792]{1,0:T(8,128)(2,1)S(1)} collective-permute-done((bf16[256,1792]{1,0:T(8,128)(2,1)S(1)}, bf16[256,1792]{1,0:T(8,128)(2,1)S(1)}, u32[]{:S(2)}, u32[]{:S(2)}) %collective-permute-start.4) | collective-permute-done | bytes 917536 | tf_op jit(solution)/shard_map/ppermute | solution.py:334
  69.9 0.0 collective-permute-done.5.got_second
  69.9 1.8 %shard_map.110 = bf16[256,4480]{1,0:T(8,128)(2,1)S(1)} custom-call(s32[2]{0:T(128)S(1)} %copy-done.4, bf16[320,160]{1,0:T(8,128)(2,1)S(1)} %get-tuple-element.22.hidden, bf16[160,7168]{1,0:T(8,128)(2,1)S(1)} %copy-done, bf16[256,1792]{1,0:T(8,128)(2,1)S(1)} %collective-permute-done.4.got_first, bf16[256,2688]{1,0:T(8,128)(2,1)S(1)} %collective-permute-done.5.got_second), custom_call_target="tpu_custom_call" | custom-call | tf_op jit(solution)/shard_map/pallas_call | solution.py:82
  71.7 33.8 %all_to_all.16 = bf16[16,16,4480]{2,1,0:T(8,128)(2,1)S(1)} all-to-all(bf16[16,16,4480]{2,1,0:T(8,128)(2,1)S(1)} %bitcast.20), channel_id=1, replica_groups=mesh['y'=4,'xh'=2,'xl'=2,'zl'=4,'zh'=2,'c'=2] {'y','xh','xl'}, dimensions={0} | all-to-all | bytes 4587520 | tf_op jit(solution)/shard_map/all_to_all | solution.py:346
  105.5 1.4 %shard_map.111 = bf16[8,16,1792]{2,1,0:T(8,128)(2,1)S(1)} custom-call(s32[2]{0:T(128)S(1)} %copy-done.4, bf16[256,4480]{1,0:T(8,128)(2,1)S(1)} %bitcast.23, bf16[64,128]{1,0:T(8,128)(2,1)S(1)} %get-tuple-element.24.marks), custom_call_target="tpu_custom_call" | custom-call | tf_op jit(solution)/shard_map/pallas_call | solution.py:82
  106.9 17.9 %all_to_all.17 = bf16[8,16,1792]{2,1,0:T(8,128)(2,1)S(1)} all-to-all(bf16[8,16,1792]{2,1,0:T(8,128)(2,1)S(1)} %shard_map.111), channel_id=1, replica_groups=mesh['y'=4,'xh'=2,'xl'=2,'zl'=4,'zh'=2,'c'=2] {'zl','zh'}, dimensions={0} | all-to-all | bytes 917504 | tf_op jit(solution)/shard_map/all_to_all | solution.py:355
  124.7 0.7 reduce_sum.12
Async XLA Ops:
  3.5 15.9 %collective-permute-start = (bf16[16,3712]{1,0:T(8,128)(2,1)}, bf16[16,3712]{1,0:T(8,128)(2,1)S(1)}, u32[]{:S(2)}, u32[]{:S(2)}) collective-permute-start(bf16[16,3712]{1,0:T(8,128)(2,1)} %shard_map.104.refs_0_), channel_id=1, source_target_pairs={{0,14},{4,0},{8,4},{12,8},{2,12},{6,2},{10,6},{14,10},{1,15},{5,1}... | collective-permute-start | bytes 356360 | tf_op jit(solution)/shard_map/ppermute | solution.py:38
  5.4 14.1 %collective-permute-start.1 = (bf16[16,3712]{1,0:T(8,128)(2,1)}, bf16[16,3712]{1,0:T(8,128)(2,1)S(1)}, u32[]{:S(2)}, u32[]{:S(2)}) collective-permute-start(bf16[16,3712]{1,0:T(8,128)(2,1)} %shard_map.104.refs_0_), channel_id=1, source_target_pairs={{0,10},{4,14},{8,0},{12,4},{2,8},{6,12},{10,2},{14,6},{1,11},{5,15... | collective-permute-start | bytes 356360 | tf_op jit(solution)/shard_map/ppermute | solution.py:38
  9.9 9.5 %collective-permute-start.2 = (bf16[16,3712]{1,0:T(8,128)(2,1)}, bf16[16,3712]{1,0:T(8,128)(2,1)S(1)}, u32[]{:S(2)}, u32[]{:S(2)}) collective-permute-start(bf16[16,3712]{1,0:T(8,128)(2,1)} %shard_map.104.refs_0_), channel_id=1, source_target_pairs={{0,4},{4,8},{8,12},{12,2},{2,6},{6,10},{10,14},{14,0},{1,5},{5,9},... | collective-permute-start | bytes 356360 | tf_op jit(solution)/shard_map/ppermute | solution.py:38
  12.5 6.9 %copy-start.3 = (bf16[16,3712]{1,0:T(8,128)(2,1)S(1)}, bf16[16,3712]{1,0:T(8,128)(2,1)}, u32[]{:S(2)}) copy-start(bf16[16,3712]{1,0:T(8,128)(2,1)} %shard_map.104.refs_0_) | copy-start | bytes 356356
  20.2 37.0 %copy-start.1 = (bf16[7168,160]{0,1:T(8,128)(2,1)S(1)}, bf16[7168,160]{0,1:T(8,128)(2,1)}, u32[]{:S(2)}) copy-start(bf16[7168,160]{0,1:T(8,128)(2,1)} %param.12) | copy-start | bytes 6881284
  20.2 37.0 %copy-start.2 = (bf16[7168,160]{0,1:T(8,128)(2,1)S(1)}, bf16[7168,160]{0,1:T(8,128)(2,1)}, u32[]{:S(2)}) copy-start(bf16[7168,160]{0,1:T(8,128)(2,1)} %param.13) | copy-start | bytes 6881284
  20.2 36.9 %copy-start.4 = (s32[2]{0:T(128)S(1)}, s32[2]{0:T(128)}, u32[]{:S(2)}) copy-start(s32[2]{0:T(128)} %pad_add_fusion.where.core) | copy-start | bytes 28
  57.1 4.4 %collective-permute-start.3 = (bf16[256,4480]{1,0:T(8,128)(2,1)S(1)}, bf16[256,4480]{1,0:T(8,128)(2,1)S(1)}, u32[]{:S(2)}, u32[]{:S(2)}) collective-permute-start(bf16[256,4480]{1,0:T(8,128)(2,1)S(1)} %bitcast.21), channel_id=1, source_target_pairs={{0,1},{1,0},{2,3},{3,2},{4,5},{5,4},{6,7},{7,6},{8,9},{9,8},{10,11... | collective-permute-start | bytes 6881288 | tf_op jit(solution)/shard_map/ppermute | solution.py:317
  57.2 4.4 %copy-start = (bf16[160,7168]{1,0:T(8,128)(2,1)S(1)}, bf16[160,7168]{1,0:T(8,128)(2,1)}, u32[]{:S(2)}) copy-start(bf16[160,7168]{1,0:T(8,128)(2,1)} %w_down.5) | copy-start | bytes 6881284
  65.4 4.5 %collective-permute-start.5 = (bf16[256,2688]{1,0:T(8,128)(2,1)S(1)}, bf16[256,2688]{1,0:T(8,128)(2,1)S(1)}, u32[]{:S(2)}, u32[]{:S(2)}) collective-permute-start(bf16[256,2688]{1,0:T(8,128)(2,1)S(1)} %shard_map.109), channel_id=1, source_target_pairs={{0,1},{1,0},{2,3},{3,2},{4,5},{5,4},{6,7},{7,6},{8,9},{9,8},{10,11... | collective-permute-start | bytes 4128776 | tf_op jit(solution)/shard_map/ppermute | solution.py:340
  65.6 4.3 %collective-permute-start.4 = (bf16[256,1792]{1,0:T(8,128)(2,1)S(1)}, bf16[256,1792]{1,0:T(8,128)(2,1)S(1)}, u32[]{:S(2)}, u32[]{:S(2)}) collective-permute-start(bf16[256,1792]{1,0:T(8,128)(2,1)S(1)} %get-tuple-element.23), channel_id=1, source_target_pairs={{0,1},{1,0},{2,3},{3,2},{4,5},{5,4},{6,7},{7,6},{8,9},{9,8},{10,11... | collective-permute-start | bytes 2752520 | tf_op jit(solution)/shard_map/ppermute | solution.py:334

commit v7 on v6

--- a/solution.py
+++ b/solution.py
@@ -78,17 +78,16 @@
 
 
 def call(kernel, out_shape, *args):
-    at = [pl.BlockSpec(memory_space=pltpu.SMEM if a.dtype == jnp.int32 else pltpu.VMEM) for a in args]
     return pl.pallas_call(
         kernel,
         out_shape=out_shape,
-        in_specs=at,
+        in_specs=[pl.BlockSpec(memory_space=pltpu.VMEM)] * len(args),
         out_specs=jax.tree.map(lambda _: pl.BlockSpec(memory_space=pltpu.VMEM), out_shape),
         compiler_params=pltpu.CompilerParams(vmem_limit_bytes=VMEM_BYTES),
     )(*args)
 
 
-def rows_kernel(quarter, where, x_rows, ids, router, out):
+def rows_kernel(quarter, x_rows, ids, router, out):
     half = 2 * quarter
     values = x_rows[...].astype(F32)
     row, lane = grid(BLOCK, LANES)
@@ -115,7 +114,7 @@
     marks = ones(named & (rank == fifth_rest(lane).astype(F32)))
     tail = jnp.where(lane < EXPERTS * CAP, marks, tail)
     for f in range(2):
-        at = pl.ds(pl.multiple_of(f * half + where[0] * quarter, LANES), quarter)
+        at = columns(quarter, lax.axis_index("c"), f)
         out[:, f * quarter : (f + 1) * quarter] = x_rows[:, at]
     out[:, half:] = tail.astype(BF16)
 
@@ -176,45 +175,42 @@
     return jnp.concatenate(tails, axis=0)
 
 
-def own_kernel(quarter, core, block, w_gate, w_up, gate_out, up_out):
-    gate, up = experts_in(quarter, core[0], block, w_gate, w_up)
+def own_kernel(quarter, block, w_gate, w_up, gate_out, up_out):
+    gate, up = experts_in(quarter, lax.axis_index("c"), block, w_gate, w_up)
     gate_out[...] = gate
     up_out[...] = up
 
 
 def other_kernel(
-    quarter, core, block, w_gate, w_up, w_down, gate_in, up_in, hidden_out, away
+    quarter, block, w_gate, w_up, w_down, gate_in, up_in, hidden_out, away
 ):
-    there = 1 - core[0]
+    there = 1 - lax.axis_index("c")
     gate, up = experts_in(quarter, there, block, w_gate, w_up)
     gate, up = gate + gate_in[...], up + up_in[...]
     hidden = (gate * jax.nn.sigmoid(gate) * up).astype(BF16)
     hidden_out[...] = hidden
-    away[...] = dot(hidden[: PLANE * BLOCK], w_down[:, columns(quarter, there, 0)]).astype(BF16)
-
-
-def away_kernel(quarter, where, hidden, w_down, away):
-    there = 1 - where[0]
-    main = dot(hidden[: PLANE * BLOCK, :], w_down[:, columns(quarter, there, 1)])
-    away[:, :quarter] = main.astype(BF16)
-    rest = tails_out(quarter, there, hidden[...], w_down).astype(BF16)
-    away[:, quarter:] = dot(shuffle_table(True), rest).astype(BF16)
-
-
-def sum_kernel(quarter, where, hidden, w_down, got_first, got_second, out):
-    for f, got in enumerate((got_first, got_second)):
-        main = dot(hidden[: PLANE * BLOCK, :], w_down[:, columns(quarter, where[0], f)])
-        main = main + got[:, :quarter].astype(F32)
-        out[:, f * quarter : (f + 1) * quarter] = main.astype(BF16)
-    rest = tails_out(quarter, where[0], hidden[...], w_down)
+    for f in range(2):
+        main = dot(hidden[: PLANE * BLOCK], w_down[:, columns(quarter, there, f)])
+        away[:, f * quarter : (f + 1) * quarter] = main.astype(BF16)
+    rest = tails_out(quarter, there, hidden, w_down).astype(BF16)
+    away[:, 2 * quarter :] = dot(shuffle_table(True), rest).astype(BF16)
+
+
+def sum_kernel(quarter, hidden, w_down, got, out):
+    core = lax.axis_index("c")
+    for f in range(2):
+        at = slice(f * quarter, (f + 1) * quarter)
+        main = dot(hidden[: PLANE * BLOCK, :], w_down[:, columns(quarter, core, f)])
+        out[:, at] = (main + got[:, at].astype(F32)).astype(BF16)
+    rest = tails_out(quarter, core, hidden[...], w_down)
     high = rest.astype(BF16)
     low = (rest - high.astype(F32)).astype(BF16)
     unshuffle = shuffle_table(True)
     rest = dot(unshuffle, high) + dot(unshuffle, low)
-    out[:, 2 * quarter :] = (rest + got_second[:, quarter:].astype(F32)).astype(BF16)
-
-
-def combine_kernel(quarter, where, back, marks, out):
+    out[:, 2 * quarter :] = (rest + got[:, 2 * quarter :].astype(F32)).astype(BF16)
+
+
+def combine_kernel(quarter, back, marks, out):
     half = 2 * quarter
     chosen = marks[...]
     lane, slot = grid(LANES, PLANE * BLOCK)
@@ -239,43 +235,32 @@
     ]
     total = both[:count] + both[count:] + jnp.concatenate(pieces, axis=1)
     for k in range(ZLO):
-        owner = (where[1] + (REACH[k] % ZLO)) & (ZLO - 1)
+        owner = (lax.axis_index("zl") + (REACH[k] % ZLO)) & (ZLO - 1)
         for f in range(2):
             piece = total[k * BLOCK : (k + 1) * BLOCK, f * quarter : (f + 1) * quarter]
             out[owner * 2 + f] = piece.astype(BF16)
 
 
-def attention_kernel(lengths, queries, cache, out):
-    live_count = lengths[pl.program_id(0)]
-    head_dim = queries.shape[2]
-    scores = dot_t(queries[0], cache[0, :, :head_dim]) / math.sqrt(head_dim)
-    live = lax.broadcasted_iota(jnp.int32, scores.shape, 1) < live_count
-    scores = jnp.where(live, scores, -1e30)
-    largest = jnp.max(scores, axis=1, keepdims=True)
-    weights = jnp.where(live, jnp.exp(scores - largest), 0.0)
-    denominator = jnp.sum(weights, axis=1, keepdims=True)
-    mixed = dot(weights.astype(BF16), cache[0, :, head_dim:])
-    out[0] = (mixed / denominator).astype(BF16)
-
-
-def attention_block(queries, cache, lengths):
-    requests, positions, both = cache.shape
-    head_dim = both // 2
+def attention_weights(queries, cache, lengths):
+    head_dim = cache.shape[2] // 2
     heads = queries.shape[1] // head_dim
-    rows = pl.BlockSpec((1, heads, head_dim), lambda i: (i, 0, 0))
-    mixed = pl.pallas_call(
-        attention_kernel,
-        grid=(requests,),
-        out_shape=jax.ShapeDtypeStruct((requests, heads, head_dim), BF16),
-        in_specs=[
-            scalars(lengths),
-            rows,
-            pl.BlockSpec((1, positions, both), lambda i: (i, 0, 0)),
-        ],
-        out_specs=rows,
-        compiler_params=pltpu.CompilerParams(vmem_limit_bytes=ALL_VMEM_BYTES),
-    )(lengths, queries.reshape(requests, heads, head_dim), cache)
-    return mixed.reshape(queries.shape)
+    query_heads = queries.reshape(queries.shape[0], heads, head_dim)
+    scores = jnp.einsum(
+        "bhd,bpd->bhp", query_heads, cache[:, :, :head_dim], preferred_element_type=F32
+    ) / math.sqrt(head_dim)
+    live = jnp.arange(cache.shape[1])[None, :] < lengths[:, None]
+    scores = jnp.where(live[:, None, :], scores, -1e30)
+    largest = jnp.max(scores, axis=2, keepdims=True)
+    weights = jnp.where(live[:, None, :], jnp.exp(scores - largest), 0.0)
+    return weights.astype(BF16), jnp.sum(weights, axis=2, keepdims=True)
+
+
+def attention_mix(weights, denominator, cache):
+    head_dim = cache.shape[2] // 2
+    mixed = jnp.einsum(
+        "bhp,bpd->bhd", weights, cache[:, :, head_dim:], preferred_element_type=F32
+    )
+    return (mixed / denominator).astype(BF16).reshape(cache.shape[0], -1)
 
 
 def shards(x_rows, route_ids, router, w_gate, w_up, w_down, queries, cache, lengths):
@@ -285,7 +270,7 @@
     quarter = model_width // 4
     half, eighth = 2 * quarter, quarter // 2
     width = half + eighth
-    where = jnp.stack([lax.axis_index("c"), lax.axis_index("zl")]).astype(jnp.int32)
+
     def whole(array):
         return pl.BlockSpec(array.shape, lambda i: (0, 0))
 
@@ -294,15 +279,15 @@
         functools.partial(rows_kernel, quarter),
         grid=(1,),
         out_shape=payload,
-        in_specs=[scalars(where), whole(x_rows), scalars(route_ids), whole(router.T)],
+        in_specs=[whole(x_rows), scalars(route_ids), whole(router.T)],
         out_specs=whole(payload),
         compiler_params=pltpu.CompilerParams(vmem_limit_bytes=ALL_VMEM_BYTES),
-    )(where, x_rows, route_ids.T, router.T)
+    )(x_rows, route_ids.T, router.T)
     blocks = [payload] + [z_send(payload, -k) for k in REACH[1:]]
 
     payload, queries = lax.optimization_barrier((payload, queries))
-    attn_out = attention_block(queries, cache, lengths)
-    blocks, attn_out = lax.optimization_barrier((blocks, attn_out))
+    weights, denominator = attention_weights(queries, cache, lengths)
+    blocks[0], weights, denominator = lax.optimization_barrier((payload, weights, denominator))
     packed, marks = call(
         functools.partial(pack_kernel, quarter),
         (
@@ -320,29 +305,19 @@
     gate, up = call(
         functools.partial(own_kernel, quarter),
         (partial, partial),
-        where, arrived, w_gate, w_up,
-    )
-    main = PLANE * BLOCK
+        arrived, w_gate, w_up,
+    )
+    pieces = jax.ShapeDtypeStruct((PLANE * BLOCK, width), BF16)
     hidden, away = call(
         functools.partial(other_kernel, quarter),
-        (
-            jax.ShapeDtypeStruct((rows, hidden_count), BF16),
-            jax.ShapeDtypeStruct((main, quarter), BF16),
-        ),
-        where, beside, w_gate, w_up, w_down, gate, up,
-    )
-    got_first = lax.ppermute(away, "c", SWAP)
-    away = call(
-        functools.partial(away_kernel, quarter),
-        jax.ShapeDtypeStruct((main, quarter + eighth), BF16),
-        where, hidden, w_down,
-    )
-    got_second = lax.ppermute(away, "c", SWAP)
-    summed = call(
-        functools.partial(sum_kernel, quarter),
-        jax.ShapeDtypeStruct((main, width), BF16),
-        where, hidden, w_down, got_first, got_second,
-    )
+        (jax.ShapeDtypeStruct((rows, hidden_count), BF16), pieces),
+        beside, w_gate, w_up, w_down, gate, up,
+    )
+    away, weights = lax.optimization_barrier((away, weights))
+    attn_out = attention_mix(weights, denominator, cache)
+    got = lax.ppermute(away, "c", SWAP)
+    hidden, attn_out = lax.optimization_barrier((hidden, attn_out))
+    summed = call(functools.partial(sum_kernel, quarter), pieces, hidden, w_down, got)
     returned = lax.all_to_all(
         summed.reshape(PLANE, BLOCK, width), ("y", "xh", "xl"), 0, 0, tiled=True
     ).reshape(PLANE * BLOCK, width)
@@ -350,7 +325,7 @@
     parts = call(
         functools.partial(combine_kernel, quarter),
         jax.ShapeDtypeStruct((ZALL, BLOCK, quarter), BF16),
-        where, returned, marks,
+        returned, marks,
     )
     parts = lax.all_to_all(parts, ("zl", "zh"), 0, 0, tiled=True)
     moe_out = jnp.sum(parts.astype(F32), axis=0)

time: 126 us -> 123 us (0.976)
  Pallas kernels: 17.1 us -> 8.97 us
  blocking collectives: 88.6 us -> 91.8 us
  matrix products: 0 us -> 3.14 us
  local copies, waits for them, and re-layouts: 3.26 us -> 0.79 us
  waiting for transfers between devices: 6.33 us -> 8.12 us
    pallas_call x7 -> x5, Pallas kernels: 14.9 us -> 6.76 us  [call(): pl.pallas_call(kernel, out_shape=out_shape, in_specs=[pl.BlockSpec(memory...]
    all_to_all x1, blocking collectives: 17.9 us -> 22.1 us  [shards(): parts = lax.all_to_all(parts, ('zl', 'zh'), 0, 0, tiled=True)]
    sub x0 -> x1, matrix products: none -> 2.68 us  [attention_weights(): weights = jnp.where(live[:, None, :], jnp.exp(scores - largest), 0.0)]
    unnamed x12 -> x11, local copies, waits for them, and re-layouts: 3.26 us -> 0.79 us
    ppermute x3, waiting for transfers between devices: 0.01 us -> 2.11 us  [z_send(): return lax.ppermute(value, ('zl', 'zh'), z_pairs(step))]
    ppermute x2 -> x1, waiting for transfers between devices: 3.93 us -> 3.07 us  [shards(): got = lax.ppermute(away, 'c', SWAP)]
  transfers between devices with their start and end apart: 6 -> 5, of which waited for: 2 -> 3; matrix products, arithmetic and copies ran while one was open for 3% -> 4% of each run, Pallas kernels for 6% -> 1%
where the time goes in v7:
time: 123 us
  blocking collectives  91.8 us (75%)
  Pallas kernels  8.97 us (7%)
  waiting for transfers between devices  8.12 us (7%)
  starting transfers between devices  7.65 us (6%)
  matrix products  3.14 us (3%)
  other arithmetic  1.42 us (1%)
    all_to_all x1, blocking collectives, shards(): lax.all_to_all(packed.reshape(PLANE, BLOCK, width), ('y', 'xh', 'xl'), 0,...  35.9 us
    all_to_all x1, blocking collectives, shards(): lax.all_to_all(summed.reshape(PLANE, BLOCK, width), ('y', 'xh', 'xl'), 0,...  33.8 us
    all_to_all x1, blocking collectives, shards(): parts = lax.all_to_all(parts, ('zl', 'zh'), 0, 0, tiled=True)  22.1 us
    ppermute x3, starting transfers between devices, z_send(): return lax.ppermute(value, ('zl', 'zh'), z_pairs(step))  7.43 us
    pallas_call x5, Pallas kernels, call(): pl.pallas_call(kernel, out_shape=out_shape, in_specs=[pl.BlockSpec(memory...  6.76 us
    ppermute x1, waiting for transfers between devices, shards(): got = lax.ppermute(away, 'c', SWAP)  3.07 us
    ppermute x1, waiting for transfers between devices, shards(): beside = lax.ppermute(arrived, 'c', SWAP)  2.93 us
    sub x1, matrix products, attention_weights(): weights = jnp.where(live[:, None, :], jnp.exp(scores - largest), 0.0)  2.68 us
  transfers between devices with their start and end apart: 5, of which 3 were waited for; matrix products, arithmetic and copies ran while one was open for 4% of the time, Pallas kernels for 1%

profile of v7, /device:TPU:32, one launch (start us, length us, event | category | flops | bytes accessed | tf_op | source)
XLA Modules:
  0.0 122.6 jit_solution(11799040025536178218)
XLA Ops:
  0.6 2.2 %shard_map.104.refs_0_ = bf16[16,3712]{1,0:T(8,128)(2,1)} custom-call(bf16[16,7168]{1,0:T(8,128)(2,1)} %x_rows.1, s32[2,16]{1,0:T(2,128)} %bitcast.31, f32[8,7168]{1,0:T(8,128)} %bitcast.29), custom_call_target="tpu_custom_call" | custom-call | tf_op jit(solution)/shard_map/pallas_call | solution.py:278
  2.8 1.9 %collective-permute-start.2 = (bf16[16,3712]{1,0:T(8,128)(2,1)}, bf16[16,3712]{1,0:T(8,128)(2,1)S(1)}, u32[]{:S(2)}, u32[]{:S(2)}) collective-permute-start(bf16[16,3712]{1,0:T(8,128)(2,1)} %shard_map.104.refs_0_), channel_id=1, source_target_pairs={{0,4},{4,8},{8,12},{12,2},{2,6},{6,10},{10,14},{14,0},{1,5},{5,9},... | collective-permute-start | bytes 356360 | tf_op jit(solution)/shard_map/ppermute | solution.py:38
  4.8 3.5 %collective-permute-start.1 = (bf16[16,3712]{1,0:T(8,128)(2,1)}, bf16[16,3712]{1,0:T(8,128)(2,1)S(1)}, u32[]{:S(2)}, u32[]{:S(2)}) collective-permute-start(bf16[16,3712]{1,0:T(8,128)(2,1)} %shard_map.104.refs_0_), channel_id=1, source_target_pairs={{0,10},{4,14},{8,0},{12,4},{2,8},{6,12},{10,2},{14,6},{1,11},{5,15... | collective-permute-start | bytes 356360 | tf_op jit(solution)/shard_map/ppermute | solution.py:38
  8.3 2.0 %collective-permute-start = (bf16[16,3712]{1,0:T(8,128)(2,1)}, bf16[16,3712]{1,0:T(8,128)(2,1)S(1)}, u32[]{:S(2)}, u32[]{:S(2)}) collective-permute-start(bf16[16,3712]{1,0:T(8,128)(2,1)} %shard_map.104.refs_0_), channel_id=1, source_target_pairs={{0,14},{4,0},{8,4},{12,8},{2,12},{6,2},{10,6},{14,10},{1,15},{5,1}... | collective-permute-start | bytes 356360 | tf_op jit(solution)/shard_map/ppermute | solution.py:38
  10.3 0.7 iota_compare_fusion
  11.0 0.0 copy-start.3
  11.0 2.7 %fusion.25 = (f32[4,64]{1,0:T(4,128)S(1)}, bf16[4,64,1024]{2,1,0:T(8,128)(2,1)S(1)}) fusion(pred[4,1024]{1,0:T(4,128)(4,1)S(1)} %iota_compare_fusion, bf16[4,1024,512]{2,1,0:T(8,128)(2,1)} %param.16, bf16[1,4,64,256]{3,1,2,0:T(4,128)(2,1)} %bitcast.32), kind=kOutput, calls=%fused_computation.16 | convolution fusion | flops 135791616 | bytes 2761728 | tf_op jit(solution)/shard_map/sub | solution.py:254
  13.7 0.0 collective-permute-done.2.refs_3_
  13.7 2.1 %collective-permute-done.1.refs_2_ = bf16[16,3712]{1,0:T(8,128)(2,1)S(1)} collective-permute-done((bf16[16,3712]{1,0:T(8,128)(2,1)}, bf16[16,3712]{1,0:T(8,128)(2,1)S(1)}, u32[]{:S(2)}, u32[]{:S(2)}) %collective-permute-start.1) | collective-permute-done | bytes 118816 | tf_op jit(solution)/shard_map/ppermute | solution.py:38
  15.8 0.0 collective-permute-done.refs_1_
  15.8 0.0 copy-done.3
  15.8 0.7 shard_map.105
  16.5 0.0 copy-start.1
  16.5 0.0 copy-start.2
  16.5 35.9 %all_to_all.15 = bf16[16,16,4480]{2,1,0:T(8,128)(2,1)S(1)} all-to-all(bf16[16,16,4480]{2,1,0:T(8,128)(2,1)S(1)} %bitcast.28), channel_id=1, replica_groups=mesh['y'=4,'xh'=2,'xl'=2,'zl'=4,'zh'=2,'c'=2] {'y','xh','xl'}, dimensions={0} | all-to-all | bytes 4587520 | tf_op jit(solution)/shard_map/all_to_all | solution.py:299
  52.4 0.0 collective-permute-start.3
  52.4 0.0 copy-done.1
  52.4 0.0 copy-done.2
  52.4 0.0 copy-start
  52.4 1.5 %shard_map.106 = (f32[320,160]{1,0:T(8,128)S(1)}, f32[320,160]{1,0:T(8,128)S(1)}) custom-call(bf16[256,4480]{1,0:T(8,128)(2,1)S(1)} %bitcast.26, bf16[160,7168]{1,0:T(8,128)(2,1)S(1)} %bitcast.21, bf16[160,7168]{1,0:T(8,128)(2,1)S(1)} %bitcast.23), custom_call_target="tpu_custom_call" | custom-call | tf_op jit(solution)/shard_map/pallas_call | solution.py:81
  53.9 2.9 %collective-permute-done.3.block = bf16[256,4480]{1,0:T(8,128)(2,1)S(1)} collective-permute-done((bf16[256,4480]{1,0:T(8,128)(2,1)S(1)}, bf16[256,4480]{1,0:T(8,128)(2,1)S(1)}, u32[]{:S(2)}, u32[]{:S(2)}) %collective-permute-start.3) | collective-permute-done | bytes 2293792 | tf_op jit(solution)/shard_map/ppermute | solution.py:302
  56.9 0.0 copy-done
  56.9 0.0 copy-start.4
  56.9 2.5 %shard_map.107 = (bf16[320,160]{1,0:T(8,128)(2,1)S(1)}, bf16[256,4480]{1,0:T(8,128)(2,1)S(1)}) custom-call(bf16[256,4480]{1,0:T(8,128)(2,1)S(1)} %collective-permute-done.3.block, bf16[160,7168]{1,0:T(8,128)(2,1)S(1)} %bitcast.22, bf16[160,7168]{1,0:T(8,128)(2,1)S(1)} %bitcast.24, bf16[160,7168]{1,0:T(8,128)(2,1)S(1)} %copy-done, ...), custom_call_target="tpu_custom_call" | custom-call | tf_op jit(solution)/shard_map/pallas_call | solution.py:81
  59.3 0.2 collective-permute-start.4
  59.6 0.0 copy-done.4
  59.6 0.5 fusion.20
  60.0 0.8 copy.12
  60.8 3.1 %collective-permute-done.4.got = bf16[256,4480]{1,0:T(8,128)(2,1)S(1)} collective-permute-done((bf16[256,4480]{1,0:T(8,128)(2,1)S(1)}, bf16[256,4480]{1,0:T(8,128)(2,1)S(1)}, u32[]{:S(2)}, u32[]{:S(2)}) %collective-permute-start.4) | collective-permute-done | bytes 2293792 | tf_op jit(solution)/shard_map/ppermute | solution.py:318
  63.9 1.2 %shard_map.108 = bf16[256,4480]{1,0:T(8,128)(2,1)S(1)} custom-call(bf16[320,160]{1,0:T(8,128)(2,1)S(1)} %get-tuple-element.28.hidden, bf16[160,7168]{1,0:T(8,128)(2,1)S(1)} %copy-done, bf16[256,4480]{1,0:T(8,128)(2,1)S(1)} %collective-permute-done.4.got), custom_call_target="tpu_custom_call" | custom-call | tf_op jit(solution)/shard_map/pallas_call | solution.py:81
  65.1 33.8 %all_to_all.16 = bf16[16,16,4480]{2,1,0:T(8,128)(2,1)S(1)} all-to-all(bf16[16,16,4480]{2,1,0:T(8,128)(2,1)S(1)} %bitcast.20), channel_id=1, replica_groups=mesh['y'=4,'xh'=2,'xl'=2,'zl'=4,'zh'=2,'c'=2] {'y','xh','xl'}, dimensions={0} | all-to-all | bytes 4587520 | tf_op jit(solution)/shard_map/all_to_all | solution.py:321
  98.9 0.9 shard_map.109
  99.8 22.1 %all_to_all.17 = bf16[8,16,1792]{2,1,0:T(8,128)(2,1)S(1)} all-to-all(bf16[8,16,1792]{2,1,0:T(8,128)(2,1)S(1)} %shard_map.109), channel_id=1, replica_groups=mesh['y'=4,'xh'=2,'xl'=2,'zl'=4,'zh'=2,'c'=2] {'zl','zh'}, dimensions={0} | all-to-all | bytes 917504 | tf_op jit(solution)/shard_map/all_to_all | solution.py:330
  121.9 0.7 reduce_sum.22
Async XLA Ops:
  2.8 10.8 %collective-permute-start.2 = (bf16[16,3712]{1,0:T(8,128)(2,1)}, bf16[16,3712]{1,0:T(8,128)(2,1)S(1)}, u32[]{:S(2)}, u32[]{:S(2)}) collective-permute-start(bf16[16,3712]{1,0:T(8,128)(2,1)} %shard_map.104.refs_0_), channel_id=1, source_target_pairs={{0,4},{4,8},{8,12},{12,2},{2,6},{6,10},{10,14},{14,0},{1,5},{5,9},... | collective-permute-start | bytes 356360 | tf_op jit(solution)/shard_map/ppermute | solution.py:38
  4.8 11.0 %collective-permute-start.1 = (bf16[16,3712]{1,0:T(8,128)(2,1)}, bf16[16,3712]{1,0:T(8,128)(2,1)S(1)}, u32[]{:S(2)}, u32[]{:S(2)}) collective-permute-start(bf16[16,3712]{1,0:T(8,128)(2,1)} %shard_map.104.refs_0_), channel_id=1, source_target_pairs={{0,10},{4,14},{8,0},{12,4},{2,8},{6,12},{10,2},{14,6},{1,11},{5,15... | collective-permute-start | bytes 356360 | tf_op jit(solution)/shard_map/ppermute | solution.py:38
  8.3 7.5 %collective-permute-start = (bf16[16,3712]{1,0:T(8,128)(2,1)}, bf16[16,3712]{1,0:T(8,128)(2,1)S(1)}, u32[]{:S(2)}, u32[]{:S(2)}) collective-permute-start(bf16[16,3712]{1,0:T(8,128)(2,1)} %shard_map.104.refs_0_), channel_id=1, source_target_pairs={{0,14},{4,0},{8,4},{12,8},{2,12},{6,2},{10,6},{14,10},{1,15},{5,1}... | collective-permute-start | bytes 356360 | tf_op jit(solution)/shard_map/ppermute | solution.py:38
  11.0 4.8 %copy-start.3 = (bf16[16,3712]{1,0:T(8,128)(2,1)S(1)}, bf16[16,3712]{1,0:T(8,128)(2,1)}, u32[]{:S(2)}) copy-start(bf16[16,3712]{1,0:T(8,128)(2,1)} %shard_map.104.refs_0_) | copy-start | bytes 356356
  16.5 35.9 %copy-start.1 = (bf16[7168,160]{0,1:T(8,128)(2,1)S(1)}, bf16[7168,160]{0,1:T(8,128)(2,1)}, u32[]{:S(2)}) copy-start(bf16[7168,160]{0,1:T(8,128)(2,1)} %param.12) | copy-start | bytes 6881284
  16.5 35.9 %copy-start.2 = (bf16[7168,160]{0,1:T(8,128)(2,1)S(1)}, bf16[7168,160]{0,1:T(8,128)(2,1)}, u32[]{:S(2)}) copy-start(bf16[7168,160]{0,1:T(8,128)(2,1)} %param.13) | copy-start | bytes 6881284
  52.4 4.4 %collective-permute-start.3 = (bf16[256,4480]{1,0:T(8,128)(2,1)S(1)}, bf16[256,4480]{1,0:T(8,128)(2,1)S(1)}, u32[]{:S(2)}, u32[]{:S(2)}) collective-permute-start(bf16[256,4480]{1,0:T(8,128)(2,1)S(1)} %bitcast.25), channel_id=1, source_target_pairs={{0,1},{1,0},{2,3},{3,2},{4,5},{5,4},{6,7},{7,6},{8,9},{9,8},{10,11... | collective-permute-start | bytes 6881288 | tf_op jit(solution)/shard_map/ppermute | solution.py:302
  52.4 4.4 %copy-start = (bf16[160,7168]{1,0:T(8,128)(2,1)S(1)}, bf16[160,7168]{1,0:T(8,128)(2,1)}, u32[]{:S(2)}) copy-start(bf16[160,7168]{1,0:T(8,128)(2,1)} %w_down.3) | copy-start | bytes 6881284
  56.9 2.7 %copy-start.4 = (bf16[4,1024,512]{2,1,0:T(8,128)(2,1)S(1)}, bf16[4,1024,512]{2,1,0:T(8,128)(2,1)}, u32[]{:S(2)}) copy-start(bf16[4,1024,512]{2,1,0:T(8,128)(2,1)} %param.16) | copy-start | bytes 12582916
  59.3 4.5 %collective-permute-start.4 = (bf16[256,4480]{1,0:T(8,128)(2,1)S(1)}, bf16[256,4480]{1,0:T(8,128)(2,1)S(1)}, u32[]{:S(2)}, u32[]{:S(2)}) collective-permute-start(bf16[256,4480]{1,0:T(8,128)(2,1)S(1)} %get-tuple-element.29), channel_id=1, source_target_pairs={{0,1},{1,0},{2,3},{3,2},{4,5},{5,4},{6,7},{7,6},{8,9},{9,8},{10,11... | collective-permute-start | bytes 6881288 | tf_op jit(solution)/shard_map/ppermute | solution.py:318

commit v8 on v7

--- a/solution.py
+++ b/solution.py
@@ -38,6 +38,11 @@
     return lax.ppermute(value, ("zl", "zh"), z_pairs(step))
 
 
+def z_send_apart(value, step):
+    both = [[(2 * a + c, 2 * b + c) for a, b in z_pairs(way)] for c, way in enumerate((step, -step))]
+    return lax.ppermute(value, ("zl", "zh", "c"), both[0] + both[1])
+
+
 def grid(rows, columns):
     return (
         lax.broadcasted_iota(jnp.int32, (rows, columns), 0),
@@ -71,10 +76,6 @@
 
 def dot_t(a, b):
     return lax.dot_general(a, b, (((1,), (1,)), ((), ())), preferred_element_type=F32)
-
-
-def scalars(array):
-    return pl.BlockSpec(memory_space=pltpu.SMEM)
 
 
 def call(kernel, out_shape, *args):
@@ -87,8 +88,18 @@
     )(*args)
 
 
-def rows_kernel(quarter, x_rows, ids, router, out):
+def rows_kernel(quarter, x_far, ids_far, router_far, out, x_rows, ids, router, arrived):
     half = 2 * quarter
+    loads = [
+        pltpu.make_async_copy(source, target, arrived.at[i])
+        for i, (source, target) in enumerate(
+            ((x_far, x_rows), (router_far, router), (ids_far, ids))
+        )
+    ]
+    for load in loads:
+        load.start()
+    for load in loads:
+        load.wait()
     values = x_rows[...].astype(F32)
     row, lane = grid(BLOCK, LANES)
     first, second = jnp.zeros_like(row), jnp.zeros_like(row)
@@ -271,19 +282,21 @@
     half, eighth = 2 * quarter, quarter // 2
     width = half + eighth
 
-    def whole(array):
-        return pl.BlockSpec(array.shape, lambda i: (0, 0))
-
-    payload = jax.ShapeDtypeStruct((BLOCK, half + LANES), BF16)
+    far = pl.BlockSpec(memory_space=pl.ANY)
     payload = pl.pallas_call(
         functools.partial(rows_kernel, quarter),
-        grid=(1,),
-        out_shape=payload,
-        in_specs=[whole(x_rows), scalars(route_ids), whole(router.T)],
-        out_specs=whole(payload),
+        out_shape=jax.ShapeDtypeStruct((BLOCK, half + LANES), BF16),
+        in_specs=[far, far, far],
+        out_specs=pl.BlockSpec(memory_space=pltpu.VMEM),
+        scratch_shapes=[
+            pltpu.VMEM(x_rows.shape, BF16),
+            pltpu.SMEM(route_ids.T.shape, jnp.int32),
+            pltpu.VMEM(router.T.shape, F32),
+            pltpu.SemaphoreType.DMA((3,)),
+        ],
         compiler_params=pltpu.CompilerParams(vmem_limit_bytes=ALL_VMEM_BYTES),
     )(x_rows, route_ids.T, router.T)
-    blocks = [payload] + [z_send(payload, -k) for k in REACH[1:]]
+    blocks = [payload, z_send(payload, -1), z_send_apart(payload, -2), z_send(payload, 1)]
 
     payload, queries = lax.optimization_barrier((payload, queries))
     weights, denominator = attention_weights(queries, cache, lengths)

time: 123 us -> 121 us (0.984)
  blocking collectives: 91.8 us -> 90.5 us
    ppermute x0 -> x1, starting transfers between devices: none -> 3.57 us  [z_send_apart(): return lax.ppermute(value, ('zl', 'zh', 'c'), both[0] + both[1])]
    ppermute x3 -> x2, starting transfers between devices: 7.43 us -> 3.93 us  [z_send(): return lax.ppermute(value, ('zl', 'zh'), z_pairs(step))]
    all_to_all x1, blocking collectives: 22.1 us -> 19 us  [shards(): parts = lax.all_to_all(parts, ('zl', 'zh'), 0, 0, tiled=True)]
    all_to_all x1, blocking collectives: 35.9 us -> 37.7 us  [shards(): lax.all_to_all(packed.reshape(PLANE, BLOCK, width), ('y', 'xh', 'xl'), 0,...]
    ppermute x3 -> x2, waiting for transfers between devices: 2.11 us -> 0.72 us  [z_send(): return lax.ppermute(value, ('zl', 'zh'), z_pairs(step))]
  transfers between devices with their start and end apart: 5 -> 5, of which waited for: 3 -> 4; matrix products, arithmetic and copies ran while one was open for 4% -> 4% of each run, Pallas kernels for 1% -> 1%
where the time goes in v8:
time: 121 us; the launch traced here: 120 us
  blocking collectives  90.5 us (75%)
  Pallas kernels  8.99 us (7%)
  starting transfers between devices  7.73 us (6%)
  waiting for transfers between devices  7.17 us (6%)
  matrix products  3.14 us (3%)
  other arithmetic  1.42 us (1%)
    all_to_all x1, blocking collectives, shards(): lax.all_to_all(packed.reshape(PLANE, BLOCK, width), ('y', 'xh', 'xl'), 0,...  37.7 us
    all_to_all x1, blocking collectives, shards(): lax.all_to_all(summed.reshape(PLANE, BLOCK, width), ('y', 'xh', 'xl'), 0,...  33.8 us
    all_to_all x1, blocking collectives, shards(): parts = lax.all_to_all(parts, ('zl', 'zh'), 0, 0, tiled=True)  19 us
    pallas_call x5, Pallas kernels, call(): pl.pallas_call(kernel, out_shape=out_shape, in_specs=[pl.BlockSpec(memory...  6.75 us
    ppermute x2, starting transfers between devices, z_send(): return lax.ppermute(value, ('zl', 'zh'), z_pairs(step))  3.93 us
    ppermute x1, starting transfers between devices, z_send_apart(): return lax.ppermute(value, ('zl', 'zh', 'c'), both[0] + both[1])  3.57 us
    ppermute x1, waiting for transfers between devices, shards(): got = lax.ppermute(away, 'c', SWAP)  3.07 us
    ppermute x1, waiting for transfers between devices, shards(): beside = lax.ppermute(arrived, 'c', SWAP)  2.93 us
  transfers between devices with their start and end apart: 5, of which 4 were waited for; matrix products, arithmetic and copies ran while one was open for 4% of the time, Pallas kernels for 1%

profile of v8, /device:TPU:32, one launch (start us, length us, event | category | flops | bytes accessed | tf_op | source)
XLA Modules:
  0.0 120.4 jit_solution(8194713335084823065)
XLA Ops:
  0.6 2.2 %shard_map.104.refs_0_ = bf16[16,3712]{1,0:T(8,128)(2,1)} custom-call(bf16[16,7168]{1,0:T(8,128)(2,1)} %x_far.1, s32[2,16]{1,0:T(2,128)} %bitcast.31, f32[8,7168]{1,0:T(8,128)} %bitcast.29), custom_call_target="tpu_custom_call" | custom-call | tf_op jit(solution)/shard_map/pallas_call | solution.py:286
  2.9 2.0 %collective-permute-start.2 = (bf16[16,3712]{1,0:T(8,128)(2,1)}, bf16[16,3712]{1,0:T(8,128)(2,1)S(1)}, u32[]{:S(2)}, u32[]{:S(2)}) collective-permute-start(bf16[16,3712]{1,0:T(8,128)(2,1)} %shard_map.104.refs_0_), channel_id=1, source_target_pairs={{0,4},{4,8},{8,12},{12,2},{2,6},{6,10},{10,14},{14,0},{1,5},{5,9},... | collective-permute-start | bytes 356360 | tf_op jit(solution)/shard_map/ppermute | solution.py:38
  4.9 3.6 %collective-permute-start.1 = (bf16[16,3712]{1,0:T(8,128)(2,1)}, bf16[16,3712]{1,0:T(8,128)(2,1)S(1)}, u32[]{:S(2)}, u32[]{:S(2)}) collective-permute-start(bf16[16,3712]{1,0:T(8,128)(2,1)} %shard_map.104.refs_0_), channel_id=1, source_target_pairs={{0,10},{4,14},{8,0},{12,4},{2,8},{6,12},{10,2},{14,6},{1,9},{5,13}... | collective-permute-start | bytes 356360 | tf_op jit(solution)/shard_map/ppermute | solution.py:43
  8.4 1.9 %collective-permute-start = (bf16[16,3712]{1,0:T(8,128)(2,1)}, bf16[16,3712]{1,0:T(8,128)(2,1)S(1)}, u32[]{:S(2)}, u32[]{:S(2)}) collective-permute-start(bf16[16,3712]{1,0:T(8,128)(2,1)} %shard_map.104.refs_0_), channel_id=1, source_target_pairs={{0,14},{4,0},{8,4},{12,8},{2,12},{6,2},{10,6},{14,10},{1,15},{5,1}... | collective-permute-start | bytes 356360 | tf_op jit(solution)/shard_map/ppermute | solution.py:38
  10.4 0.7 iota_compare_fusion
  11.1 0.0 copy-start.3
  11.1 2.7 %fusion.25 = (f32[4,64]{1,0:T(4,128)S(1)}, bf16[4,64,1024]{2,1,0:T(8,128)(2,1)S(1)}) fusion(pred[4,1024]{1,0:T(4,128)(4,1)S(1)} %iota_compare_fusion, bf16[4,1024,512]{2,1,0:T(8,128)(2,1)} %param.16, bf16[1,4,64,256]{3,1,2,0:T(4,128)(2,1)} %bitcast.32), kind=kOutput, calls=%fused_computation.16 | convolution fusion | flops 135791616 | bytes 2761728 | tf_op jit(solution)/shard_map/sub | solution.py:265
  13.8 0.0 collective-permute-done.2.refs_3_
  13.8 0.5 collective-permute-done.1.refs_2_
  14.2 0.7 collective-permute-done.refs_1_
  15.0 0.0 copy-done.3
  15.0 0.7 shard_map.105
  15.7 0.0 copy-start.1
  15.7 0.0 copy-start.2
  15.7 37.7 %all_to_all.15 = bf16[16,16,4480]{2,1,0:T(8,128)(2,1)S(1)} all-to-all(bf16[16,16,4480]{2,1,0:T(8,128)(2,1)S(1)} %bitcast.28), channel_id=1, replica_groups=mesh['y'=4,'xh'=2,'xl'=2,'zl'=4,'zh'=2,'c'=2] {'y','xh','xl'}, dimensions={0} | all-to-all | bytes 4587520 | tf_op jit(solution)/shard_map/all_to_all | solution.py:312
  53.4 0.0 collective-permute-start.3
  53.4 0.0 copy-done.1
  53.4 0.0 copy-done.2
  53.4 0.0 copy-start
  53.4 1.5 %shard_map.106 = (f32[320,160]{1,0:T(8,128)S(1)}, f32[320,160]{1,0:T(8,128)S(1)}) custom-call(bf16[256,4480]{1,0:T(8,128)(2,1)S(1)} %bitcast.26, bf16[160,7168]{1,0:T(8,128)(2,1)S(1)} %bitcast.21, bf16[160,7168]{1,0:T(8,128)(2,1)S(1)} %bitcast.23), custom_call_target="tpu_custom_call" | custom-call | tf_op jit(solution)/shard_map/pallas_call | solution.py:82
  54.9 2.9 %collective-permute-done.3.block = bf16[256,4480]{1,0:T(8,128)(2,1)S(1)} collective-permute-done((bf16[256,4480]{1,0:T(8,128)(2,1)S(1)}, bf16[256,4480]{1,0:T(8,128)(2,1)S(1)}, u32[]{:S(2)}, u32[]{:S(2)}) %collective-permute-start.3) | collective-permute-done | bytes 2293792 | tf_op jit(solution)/shard_map/ppermute | solution.py:315
  57.8 0.0 copy-done
  57.8 0.0 copy-start.4
  57.8 2.5 %shard_map.107 = (bf16[320,160]{1,0:T(8,128)(2,1)S(1)}, bf16[256,4480]{1,0:T(8,128)(2,1)S(1)}) custom-call(bf16[256,4480]{1,0:T(8,128)(2,1)S(1)} %collective-permute-done.3.block, bf16[160,7168]{1,0:T(8,128)(2,1)S(1)} %bitcast.22, bf16[160,7168]{1,0:T(8,128)(2,1)S(1)} %bitcast.24, bf16[160,7168]{1,0:T(8,128)(2,1)S(1)} %copy-done, ...), custom_call_target="tpu_custom_call" | custom-call | tf_op jit(solution)/shard_map/pallas_call | solution.py:82
  60.3 0.2 collective-permute-start.4
  60.5 0.0 copy-done.4
  60.5 0.5 fusion.20
  61.0 0.8 copy.12
  61.8 3.1 %collective-permute-done.4.got = bf16[256,4480]{1,0:T(8,128)(2,1)S(1)} collective-permute-done((bf16[256,4480]{1,0:T(8,128)(2,1)S(1)}, bf16[256,4480]{1,0:T(8,128)(2,1)S(1)}, u32[]{:S(2)}, u32[]{:S(2)}) %collective-permute-start.4) | collective-permute-done | bytes 2293792 | tf_op jit(solution)/shard_map/ppermute | solution.py:331
  64.8 1.2 %shard_map.108 = bf16[256,4480]{1,0:T(8,128)(2,1)S(1)} custom-call(bf16[320,160]{1,0:T(8,128)(2,1)S(1)} %get-tuple-element.28.hidden, bf16[160,7168]{1,0:T(8,128)(2,1)S(1)} %copy-done, bf16[256,4480]{1,0:T(8,128)(2,1)S(1)} %collective-permute-done.4.got), custom_call_target="tpu_custom_call" | custom-call | tf_op jit(solution)/shard_map/pallas_call | solution.py:82
  66.1 33.8 %all_to_all.16 = bf16[16,16,4480]{2,1,0:T(8,128)(2,1)S(1)} all-to-all(bf16[16,16,4480]{2,1,0:T(8,128)(2,1)S(1)} %bitcast.20), channel_id=1, replica_groups=mesh['y'=4,'xh'=2,'xl'=2,'zl'=4,'zh'=2,'c'=2] {'y','xh','xl'}, dimensions={0} | all-to-all | bytes 4587520 | tf_op jit(solution)/shard_map/all_to_all | solution.py:334
  99.9 0.8 shard_map.109
  100.7 19.0 %all_to_all.17 = bf16[8,16,1792]{2,1,0:T(8,128)(2,1)S(1)} all-to-all(bf16[8,16,1792]{2,1,0:T(8,128)(2,1)S(1)} %shard_map.109), channel_id=1, replica_groups=mesh['y'=4,'xh'=2,'xl'=2,'zl'=4,'zh'=2,'c'=2] {'zl','zh'}, dimensions={0} | all-to-all | bytes 917504 | tf_op jit(solution)/shard_map/all_to_all | solution.py:343
  119.7 0.7 reduce_sum.22
Async XLA Ops:
  2.9 10.9 %collective-permute-start.2 = (bf16[16,3712]{1,0:T(8,128)(2,1)}, bf16[16,3712]{1,0:T(8,128)(2,1)S(1)}, u32[]{:S(2)}, u32[]{:S(2)}) collective-permute-start(bf16[16,3712]{1,0:T(8,128)(2,1)} %shard_map.104.refs_0_), channel_id=1, source_target_pairs={{0,4},{4,8},{8,12},{12,2},{2,6},{6,10},{10,14},{14,0},{1,5},{5,9},... | collective-permute-start | bytes 356360 | tf_op jit(solution)/shard_map/ppermute | solution.py:38
  4.9 9.4 %collective-permute-start.1 = (bf16[16,3712]{1,0:T(8,128)(2,1)}, bf16[16,3712]{1,0:T(8,128)(2,1)S(1)}, u32[]{:S(2)}, u32[]{:S(2)}) collective-permute-start(bf16[16,3712]{1,0:T(8,128)(2,1)} %shard_map.104.refs_0_), channel_id=1, source_target_pairs={{0,10},{4,14},{8,0},{12,4},{2,8},{6,12},{10,2},{14,6},{1,9},{5,13}... | collective-permute-start | bytes 356360 | tf_op jit(solution)/shard_map/ppermute | solution.py:43
  8.4 6.5 %collective-permute-start = (bf16[16,3712]{1,0:T(8,128)(2,1)}, bf16[16,3712]{1,0:T(8,128)(2,1)S(1)}, u32[]{:S(2)}, u32[]{:S(2)}) collective-permute-start(bf16[16,3712]{1,0:T(8,128)(2,1)} %shard_map.104.refs_0_), channel_id=1, source_target_pairs={{0,14},{4,0},{8,4},{12,8},{2,12},{6,2},{10,6},{14,10},{1,15},{5,1}... | collective-permute-start | bytes 356360 | tf_op jit(solution)/shard_map/ppermute | solution.py:38
  11.1 3.8 %copy-start.3 = (bf16[16,3712]{1,0:T(8,128)(2,1)S(1)}, bf16[16,3712]{1,0:T(8,128)(2,1)}, u32[]{:S(2)}) copy-start(bf16[16,3712]{1,0:T(8,128)(2,1)} %shard_map.104.refs_0_) | copy-start | bytes 356356
  15.7 37.7 %copy-start.1 = (bf16[7168,160]{0,1:T(8,128)(2,1)S(1)}, bf16[7168,160]{0,1:T(8,128)(2,1)}, u32[]{:S(2)}) copy-start(bf16[7168,160]{0,1:T(8,128)(2,1)} %param.12) | copy-start | bytes 6881284
  15.7 37.7 %copy-start.2 = (bf16[7168,160]{0,1:T(8,128)(2,1)S(1)}, bf16[7168,160]{0,1:T(8,128)(2,1)}, u32[]{:S(2)}) copy-start(bf16[7168,160]{0,1:T(8,128)(2,1)} %param.13) | copy-start | bytes 6881284
  53.4 4.4 %collective-permute-start.3 = (bf16[256,4480]{1,0:T(8,128)(2,1)S(1)}, bf16[256,4480]{1,0:T(8,128)(2,1)S(1)}, u32[]{:S(2)}, u32[]{:S(2)}) collective-permute-start(bf16[256,4480]{1,0:T(8,128)(2,1)S(1)} %bitcast.25), channel_id=1, source_target_pairs={{0,1},{1,0},{2,3},{3,2},{4,5},{5,4},{6,7},{7,6},{8,9},{9,8},{10,11... | collective-permute-start | bytes 6881288 | tf_op jit(solution)/shard_map/ppermute | solution.py:315
  53.4 4.4 %copy-start = (bf16[160,7168]{1,0:T(8,128)(2,1)S(1)}, bf16[160,7168]{1,0:T(8,128)(2,1)}, u32[]{:S(2)}) copy-start(bf16[160,7168]{1,0:T(8,128)(2,1)} %w_down.3) | copy-start | bytes 6881284
  57.8 2.7 %copy-start.4 = (bf16[4,1024,512]{2,1,0:T(8,128)(2,1)S(1)}, bf16[4,1024,512]{2,1,0:T(8,128)(2,1)}, u32[]{:S(2)}) copy-start(bf16[4,1024,512]{2,1,0:T(8,128)(2,1)} %param.16) | copy-start | bytes 12582916
  60.3 4.5 %collective-permute-start.4 = (bf16[256,4480]{1,0:T(8,128)(2,1)S(1)}, bf16[256,4480]{1,0:T(8,128)(2,1)S(1)}, u32[]{:S(2)}, u32[]{:S(2)}) collective-permute-start(bf16[256,4480]{1,0:T(8,128)(2,1)S(1)} %get-tuple-element.29), channel_id=1, source_target_pairs={{0,1},{1,0},{2,3},{3,2},{4,5},{5,4},{6,7},{7,6},{8,9},{9,8},{10,11... | collective-permute-start | bytes 6881288 | tf_op jit(solution)/shard_map/ppermute | solution.py:331

commit v9 on v8

--- a/solution.py
+++ b/solution.py
@@ -19,7 +19,7 @@
 REACH = (0, 1, 2, -1)
 HIGH, LOW = 64, 72
 BF16, F32 = jnp.bfloat16, jnp.float32
-VMEM_BYTES = 40 * 1024 * 1024
+VMEM_BYTES = 24 * 1024 * 1024
 ALL_VMEM_BYTES = 60 * 1024 * 1024
 
 
@@ -158,67 +158,46 @@
         out[:, x, :, half:] = rest
 
 
-def experts_in(quarter, core, block, w_gate, w_up):
-    half = 2 * quarter
-    rest = dot(shuffle_table(False), block[:, half:]).astype(BF16)
-    gate, up = 0.0, 0.0
-    for f in range(2):
-        top = block[:, f * quarter : (f + 1) * quarter]
-        tail = jnp.concatenate(
-            [rest[(2 * f + i) * 64 : (2 * f + i + 1) * 64] for i in range(2)], axis=1
-        )
-        rows = jnp.concatenate([top, tail], axis=0)
-        at = pl.ds(pl.multiple_of(f * half + core * quarter, LANES), quarter)
-        gate = gate + dot_t(rows, w_gate[:, at])
-        up = up + dot_t(rows, w_up[:, at])
-    return gate, up
-
-
 def columns(quarter, core, f):
     return pl.ds(pl.multiple_of(f * 2 * quarter + core * quarter, LANES), quarter)
 
 
-def tails_out(quarter, core, hidden, w_down):
+def expert_rows(quarter, block, f):
+    rest = dot(shuffle_table(False), block[:, 2 * quarter :]).astype(BF16)
+    top = block[:, f * quarter : (f + 1) * quarter]
+    tail = [rest[(2 * f + i) * 64 : (2 * f + i + 1) * 64] for i in range(2)]
+    return jnp.concatenate([top, jnp.concatenate(tail, axis=1)], axis=0)
+
+
+def inner_kernel(quarter, block, w_gate, w_up, other_gate, other_up, mine, theirs):
+    core = lax.axis_index("c")
+    rows = [expert_rows(quarter, block, f) for f in range(2)]
+    for out, weights in ((theirs, (other_gate, other_up)), (mine, (w_gate, w_up))):
+        for i, weight in enumerate(weights):
+            out[i, :, LANES:] = jnp.zeros((out.shape[1], out.shape[2] - LANES), F32)
+            out[i, :, : weight.shape[0]] = dot_t(
+                rows[0], weight[:, columns(quarter, core, 0)]
+            ) + dot_t(rows[1], weight[:, columns(quarter, core, 1)])
+
+
+def hidden_kernel(mine, got, hidden):
+    count = hidden.shape[1]
+    gate, up = (mine[i, :, :count] + got[i, :, :count] for i in range(2))
+    hidden[...] = (gate * jax.nn.sigmoid(gate) * up).astype(BF16)
+
+
+def outer_kernel(quarter, hidden, other_hidden, w_down, other_down, out):
+    core = lax.axis_index("c")
+    main = PLANE * BLOCK
     tails = []
     for f in range(2):
-        y = dot(hidden[PLANE * BLOCK :], w_down[:, columns(quarter, core, f)])
-        tails += [y[:, : quarter // 2], y[:, quarter // 2 :]]
-    return jnp.concatenate(tails, axis=0)
-
-
-def own_kernel(quarter, block, w_gate, w_up, gate_out, up_out):
-    gate, up = experts_in(quarter, lax.axis_index("c"), block, w_gate, w_up)
-    gate_out[...] = gate
-    up_out[...] = up
-
-
-def other_kernel(
-    quarter, block, w_gate, w_up, w_down, gate_in, up_in, hidden_out, away
-):
-    there = 1 - lax.axis_index("c")
-    gate, up = experts_in(quarter, there, block, w_gate, w_up)
-    gate, up = gate + gate_in[...], up + up_in[...]
-    hidden = (gate * jax.nn.sigmoid(gate) * up).astype(BF16)
-    hidden_out[...] = hidden
-    for f in range(2):
-        main = dot(hidden[: PLANE * BLOCK], w_down[:, columns(quarter, there, f)])
-        away[:, f * quarter : (f + 1) * quarter] = main.astype(BF16)
-    rest = tails_out(quarter, there, hidden, w_down).astype(BF16)
-    away[:, 2 * quarter :] = dot(shuffle_table(True), rest).astype(BF16)
-
-
-def sum_kernel(quarter, hidden, w_down, got, out):
-    core = lax.axis_index("c")
-    for f in range(2):
-        at = slice(f * quarter, (f + 1) * quarter)
-        main = dot(hidden[: PLANE * BLOCK, :], w_down[:, columns(quarter, core, f)])
-        out[:, at] = (main + got[:, at].astype(F32)).astype(BF16)
-    rest = tails_out(quarter, core, hidden[...], w_down)
-    high = rest.astype(BF16)
-    low = (rest - high.astype(F32)).astype(BF16)
-    unshuffle = shuffle_table(True)
-    rest = dot(unshuffle, high) + dot(unshuffle, low)
-    out[:, 2 * quarter :] = (rest + got[:, 2 * quarter :].astype(F32)).astype(BF16)
+        at = columns(quarter, core, f)
+        y = dot(hidden[...], w_down[:, at]) + dot(other_hidden[...], other_down[:, at])
+        y = y.astype(BF16)
+        out[:, f * quarter : (f + 1) * quarter] = y[:main]
+        tails += [y[main:, : quarter // 2], y[main:, quarter // 2 :]]
+    tails = jnp.concatenate(tails, axis=0)
+    out[:, 2 * quarter :] = dot(shuffle_table(True), tails).astype(BF16)
 
 
 def combine_kernel(quarter, back, marks, out):
@@ -278,6 +257,7 @@
     model_width = x_rows.shape[1]
     hidden_count = w_gate.shape[1]
     w_gate, w_up = w_gate.T, w_up.T
+    other_gate, other_up, other_down = (lax.ppermute(w, "c", SWAP) for w in (w_gate, w_up, w_down))
     quarter = model_width // 4
     half, eighth = 2 * quarter, quarter // 2
     width = half + eighth
@@ -312,25 +292,24 @@
     arrived = lax.all_to_all(
         packed.reshape(PLANE, BLOCK, width), ("y", "xh", "xl"), 0, 0, tiled=True
     ).reshape(PLANE * BLOCK, width)
-    beside = lax.ppermute(arrived, "c", SWAP)
     rows = PLANE * (BLOCK + ZLO)
-    partial = jax.ShapeDtypeStruct((rows, hidden_count), F32)
-    gate, up = call(
-        functools.partial(own_kernel, quarter),
-        (partial, partial),
-        arrived, w_gate, w_up,
-    )
-    pieces = jax.ShapeDtypeStruct((PLANE * BLOCK, width), BF16)
-    hidden, away = call(
-        functools.partial(other_kernel, quarter),
-        (jax.ShapeDtypeStruct((rows, hidden_count), BF16), pieces),
-        beside, w_gate, w_up, w_down, gate, up,
-    )
-    away, weights = lax.optimization_barrier((away, weights))
+    wide = -(-hidden_count // (2 * LANES)) * 2 * LANES
+    sums = jax.ShapeDtypeStruct((2, rows, wide), F32)
+    mine, theirs = call(
+        functools.partial(inner_kernel, quarter),
+        (sums, sums),
+        arrived, w_gate, w_up, other_gate, other_up,
+    )
+    theirs, weights = lax.optimization_barrier((theirs, weights))
     attn_out = attention_mix(weights, denominator, cache)
-    got = lax.ppermute(away, "c", SWAP)
-    hidden, attn_out = lax.optimization_barrier((hidden, attn_out))
-    summed = call(functools.partial(sum_kernel, quarter), pieces, hidden, w_down, got)
+    got = lax.ppermute(theirs, "c", SWAP)
+    mine, attn_out = lax.optimization_barrier((mine, attn_out))
+    hidden = call(hidden_kernel, jax.ShapeDtypeStruct((rows, hidden_count), BF16), mine, got)
+    summed = call(
+        functools.partial(outer_kernel, quarter),
+        jax.ShapeDtypeStruct((PLANE * BLOCK, width), BF16),
+        hidden, lax.ppermute(hidden, "c", SWAP), w_down, other_down,
+    )
     returned = lax.all_to_all(
         summed.reshape(PLANE, BLOCK, width), ("y", "xh", "xl"), 0, 0, tiled=True
     ).reshape(PLANE * BLOCK, width)

time: 121 us -> 130 us (1.074)
  blocking collectives: 90.5 us -> 53.9 us
  waiting for transfers between devices: 7.17 us -> 37.5 us
  starting transfers between devices: 7.73 us -> 15.5 us
  local copies, waits for them, and re-layouts: 0.79 us -> 5.49 us
  Pallas kernels: 8.99 us -> 12.3 us
    all_to_all x1 -> x0, blocking collectives: 37.7 us -> none  [shards(): lax.all_to_all(packed.reshape(PLANE, BLOCK, width), ('y', 'xh', 'xl'), 0,...]
    all_to_all x0 -> x1, waiting for transfers between devices: none -> 34.8 us  [shards(): lax.all_to_all(packed.reshape(PLANE, BLOCK, width), ('y', 'xh', 'xl'), 0,...]
    all_to_all x0 -> x1, starting transfers between devices: none -> 7.03 us  [shards(): lax.all_to_all(packed.reshape(PLANE, BLOCK, width), ('y', 'xh', 'xl'), 0,...]
    unnamed x11 -> x13, local copies, waits for them, and re-layouts: 0.79 us -> 5.49 us
    ppermute x2 -> x5, waiting for transfers between devices: 6 us -> 2.07 us  [the longest x1 1.26 us: shards(): lax.ppermute(hidden, 'c', SWAP)]
    pallas_call x5, Pallas kernels: 6.75 us -> 10 us  [call(): pl.pallas_call(kernel, out_shape=out_shape, in_specs=[pl.BlockSpec(memory...]
  transfers between devices with their start and end apart: 5 -> 9, of which waited for: 4 -> 4; matrix products, arithmetic and copies ran while one was open for 4% -> 4% of each run, Pallas kernels for 1% -> 5%
where the time goes in v9:
time: 130 us
  blocking collectives  53.9 us (41%)
  waiting for transfers between devices  37.5 us (29%)
  starting transfers between devices  15.5 us (12%)
  Pallas kernels  12.3 us (9%)
  local copies, waits for them, and re-layouts  5.49 us (4%)
  matrix products  3.16 us (2%)
  other arithmetic  1.42 us (1%)
    all_to_all x1, waiting for transfers between devices, shards(): lax.all_to_all(packed.reshape(PLANE, BLOCK, width), ('y', 'xh', 'xl'), 0,...  34.8 us
    all_to_all x1, blocking collectives, shards(): lax.all_to_all(summed.reshape(PLANE, BLOCK, width), ('y', 'xh', 'xl'), 0,...  34.3 us
    all_to_all x1, blocking collectives, shards(): parts = lax.all_to_all(parts, ('zl', 'zh'), 0, 0, tiled=True)  19.5 us
    pallas_call x5, Pallas kernels, call(): pl.pallas_call(kernel, out_shape=out_shape, in_specs=[pl.BlockSpec(memory...  10 us
    all_to_all x1, starting transfers between devices, shards(): lax.all_to_all(packed.reshape(PLANE, BLOCK, width), ('y', 'xh', 'xl'), 0,...  7.03 us
    unnamed x13, local copies, waits for them, and re-layouts  5.49 us
    ppermute x2, starting transfers between devices, z_send(): return lax.ppermute(value, ('zl', 'zh'), z_pairs(step))  3.93 us
    ppermute x1, starting transfers between devices, z_send_apart(): return lax.ppermute(value, ('zl', 'zh', 'c'), both[0] + both[1])  3.57 us
  transfers between devices with their start and end apart: 9, of which 4 were waited for; matrix products, arithmetic and copies ran while one was open for 4% of the time, Pallas kernels for 5%

profile of v9, /device:TPU:32, one launch (start us, length us, event | category | flops | bytes accessed | tf_op | source)
XLA Modules:
  0.0 129.9 jit_solution(5083385506106815272)
XLA Ops:
  0.6 2.2 %shard_map.104.refs_0_ = bf16[16,3712]{1,0:T(8,128)(2,1)} custom-call(bf16[16,7168]{1,0:T(8,128)(2,1)} %x_far.1, s32[2,16]{1,0:T(2,128)} %bitcast.30, f32[8,7168]{1,0:T(8,128)} %bitcast.28), custom_call_target="tpu_custom_call" | custom-call | tf_op jit(solution)/shard_map/pallas_call | solution.py:266
  2.9 2.0 %collective-permute-start.2 = (bf16[16,3712]{1,0:T(8,128)(2,1)}, bf16[16,3712]{1,0:T(8,128)(2,1)S(1)}, u32[]{:S(2)}, u32[]{:S(2)}) collective-permute-start(bf16[16,3712]{1,0:T(8,128)(2,1)} %shard_map.104.refs_0_), channel_id=1, source_target_pairs={{0,4},{4,8},{8,12},{12,2},{2,6},{6,10},{10,14},{14,0},{1,5},{5,9},... | collective-permute-start | bytes 356360 | tf_op jit(solution)/shard_map/ppermute | solution.py:38
  4.9 3.6 %collective-permute-start.1 = (bf16[16,3712]{1,0:T(8,128)(2,1)}, bf16[16,3712]{1,0:T(8,128)(2,1)S(1)}, u32[]{:S(2)}, u32[]{:S(2)}) collective-permute-start(bf16[16,3712]{1,0:T(8,128)(2,1)} %shard_map.104.refs_0_), channel_id=1, source_target_pairs={{0,10},{4,14},{8,0},{12,4},{2,8},{6,12},{10,2},{14,6},{1,9},{5,13}... | collective-permute-start | bytes 356360 | tf_op jit(solution)/shard_map/ppermute | solution.py:43
  8.4 1.9 %collective-permute-start = (bf16[16,3712]{1,0:T(8,128)(2,1)}, bf16[16,3712]{1,0:T(8,128)(2,1)S(1)}, u32[]{:S(2)}, u32[]{:S(2)}) collective-permute-start(bf16[16,3712]{1,0:T(8,128)(2,1)} %shard_map.104.refs_0_), channel_id=1, source_target_pairs={{0,14},{4,0},{8,4},{12,8},{2,12},{6,2},{10,6},{14,10},{1,15},{5,1}... | collective-permute-start | bytes 356360 | tf_op jit(solution)/shard_map/ppermute | solution.py:38
  10.4 0.0 collective-permute-start.3
  10.4 0.5 collective-permute-start.4
  10.9 0.7 iota_compare_fusion
  11.6 0.0 copy-start.4
  11.6 2.7 %fusion.25 = (f32[4,64]{1,0:T(4,128)S(1)}, bf16[4,64,1024]{2,1,0:T(8,128)(2,1)S(1)}) fusion(pred[4,1024]{1,0:T(4,128)(4,1)S(1)} %iota_compare_fusion, bf16[4,1024,512]{2,1,0:T(8,128)(2,1)} %param.16, bf16[1,4,64,256]{3,1,2,0:T(4,128)(2,1)} %bitcast.31), kind=kOutput, calls=%fused_computation.16 | convolution fusion | flops 135791616 | bytes 2761728 | tf_op jit(solution)/shard_map/sub | solution.py:244
  14.3 0.0 collective-permute-done.2.refs_3_
  14.3 0.0 collective-permute-done.1.refs_2_
  14.3 0.6 collective-permute-done.refs_1_
  15.0 0.0 copy-done.4
  15.0 0.7 shard_map.105
  15.7 0.0 copy-start.1
  15.7 1.4 %copy-done.1 = bf16[8,2,16,4480]{3,2,1,0:T(8,128)(2,1)} copy-done((bf16[8,2,16,4480]{3,2,1,0:T(8,128)(2,1)}, bf16[8,2,16,4480]{3,2,1,0:T(8,128)(2,1)S(1)}, u32[]{:S(2)}) %copy-start.1) | copy-done | bytes 2293784
  17.1 7.0 %all-to-all-start = ((bf16[16,16,4480]{2,1,0:T(8,128)(2,1)}), bf16[16,16,4480]{2,1,0:T(8,128)(2,1)S(1)}, u32[]{:S(2)}, u32[]{:S(2)}) async-start(bf16[16,16,4480]{2,1,0:T(8,128)(2,1)} %bitcast.23), calls=%async_computation | async-start | bytes 4587520 | tf_op jit(solution)/shard_map/all_to_all | solution.py:292
  24.2 0.1 collective-permute-start.7
  24.3 34.8 %all-to-all-done = bf16[16,16,4480]{2,1,0:T(8,128)(2,1)S(1)} async-done(((bf16[16,16,4480]{2,1,0:T(8,128)(2,1)}), bf16[16,16,4480]{2,1,0:T(8,128)(2,1)S(1)}, u32[]{:S(2)}, u32[]{:S(2)}) %all-to-all-start) | async-done | bytes 2293792 | tf_op jit(solution)/shard_map/all_to_all | solution.py:292
  59.0 0.0 collective-permute-done.3.other_gate
  59.0 0.0 collective-permute-done.4.other_up
  59.0 0.0 copy-start.2
  59.0 1.6 %copy-done.2 = bf16[7168,160]{0,1:T(8,128)(2,1)S(1)} copy-done((bf16[7168,160]{0,1:T(8,128)(2,1)S(1)}, bf16[7168,160]{0,1:T(8,128)(2,1)}, u32[]{:S(2)}) %copy-start.2) | copy-done | bytes 2293784
  60.7 0.0 copy-start.3
  60.7 1.6 %copy-done.3 = bf16[7168,160]{0,1:T(8,128)(2,1)S(1)} copy-done((bf16[7168,160]{0,1:T(8,128)(2,1)S(1)}, bf16[7168,160]{0,1:T(8,128)(2,1)}, u32[]{:S(2)}) %copy-start.3) | copy-done | bytes 2293784
  62.3 0.0 copy-start.5
  62.3 5.1 %shard_map.106 = (f32[2,320,256]{2,1,0:T(8,128)S(1)}, f32[2,320,256]{2,1,0:T(8,128)S(1)}) custom-call(bf16[256,4480]{1,0:T(8,128)(2,1)S(1)} %bitcast.22, bf16[160,7168]{1,0:T(8,128)(2,1)S(1)} %bitcast.25, bf16[160,7168]{1,0:T(8,128)(2,1)S(1)} %bitcast.27, bf16[160,7168]{1,0:T(8,128)(2,1)} %collective-permute-done.3.other_gate, ...), custom_call_target="tpu_custom_call" | custom-call | tf_op jit(solution)/shard_map/pallas_call | solution.py:82
  67.5 0.1 collective-permute-start.5
  67.6 0.0 copy-done.5
  67.6 0.0 copy-start
  67.6 0.5 fusion.20
  68.1 0.8 copy.12
  68.8 0.8 collective-permute-done.5.got
  69.6 0.1 shard_map.107.hidden
  69.7 0.2 collective-permute-start.6
  70.0 0.0 collective-permute-done.7.other_down
  70.0 1.3 collective-permute-done.6.other_hidden
  71.2 0.0 copy-done
  71.2 3.3 %shard_map.108 = bf16[256,4480]{1,0:T(8,128)(2,1)S(1)} custom-call(bf16[320,160]{1,0:T(8,128)(2,1)S(1)} %shard_map.107.hidden, bf16[320,160]{1,0:T(8,128)(2,1)S(1)} %collective-permute-done.6.other_hidden, bf16[160,7168]{1,0:T(8,128)(2,1)S(1)} %copy-done, bf16[160,7168]{1,0:T(8,128)(2,1)} %collective-permute-done.7.other_down), custom_call_target="tpu_custom_call" | custom-call | tf_op jit(solution)/shard_map/pallas_call | solution.py:82
  74.5 34.3 %all_to_all.15 = bf16[16,16,4480]{2,1,0:T(8,128)(2,1)S(1)} all-to-all(bf16[16,16,4480]{2,1,0:T(8,128)(2,1)S(1)} %bitcast.20), channel_id=1, replica_groups=mesh['y'=4,'xh'=2,'xl'=2,'zl'=4,'zh'=2,'c'=2] {'y','xh','xl'}, dimensions={0} | all-to-all | bytes 4587520 | tf_op jit(solution)/shard_map/all_to_all | solution.py:313
  108.8 0.8 shard_map.109
  109.7 19.5 %all_to_all.16 = bf16[8,16,1792]{2,1,0:T(8,128)(2,1)S(1)} all-to-all(bf16[8,16,1792]{2,1,0:T(8,128)(2,1)S(1)} %shard_map.109), channel_id=1, replica_groups=mesh['y'=4,'xh'=2,'xl'=2,'zl'=4,'zh'=2,'c'=2] {'zl','zh'}, dimensions={0} | all-to-all | bytes 917504 | tf_op jit(solution)/shard_map/all_to_all | solution.py:322
  129.2 0.7 reduce_sum.22
Async XLA Ops:
  2.9 11.4 %collective-permute-start.2 = (bf16[16,3712]{1,0:T(8,128)(2,1)}, bf16[16,3712]{1,0:T(8,128)(2,1)S(1)}, u32[]{:S(2)}, u32[]{:S(2)}) collective-permute-start(bf16[16,3712]{1,0:T(8,128)(2,1)} %shard_map.104.refs_0_), channel_id=1, source_target_pairs={{0,4},{4,8},{8,12},{12,2},{2,6},{6,10},{10,14},{14,0},{1,5},{5,9},... | collective-permute-start | bytes 356360 | tf_op jit(solution)/shard_map/ppermute | solution.py:38
  4.9 9.4 %collective-permute-start.1 = (bf16[16,3712]{1,0:T(8,128)(2,1)}, bf16[16,3712]{1,0:T(8,128)(2,1)S(1)}, u32[]{:S(2)}, u32[]{:S(2)}) collective-permute-start(bf16[16,3712]{1,0:T(8,128)(2,1)} %shard_map.104.refs_0_), channel_id=1, source_target_pairs={{0,10},{4,14},{8,0},{12,4},{2,8},{6,12},{10,2},{14,6},{1,9},{5,13}... | collective-permute-start | bytes 356360 | tf_op jit(solution)/shard_map/ppermute | solution.py:43
  8.4 6.5 %collective-permute-start = (bf16[16,3712]{1,0:T(8,128)(2,1)}, bf16[16,3712]{1,0:T(8,128)(2,1)S(1)}, u32[]{:S(2)}, u32[]{:S(2)}) collective-permute-start(bf16[16,3712]{1,0:T(8,128)(2,1)} %shard_map.104.refs_0_), channel_id=1, source_target_pairs={{0,14},{4,0},{8,4},{12,8},{2,12},{6,2},{10,6},{14,10},{1,15},{5,1}... | collective-permute-start | bytes 356360 | tf_op jit(solution)/shard_map/ppermute | solution.py:38
  10.4 48.6 %collective-permute-start.3 = (bf16[160,7168]{1,0:T(8,128)(2,1)}, bf16[160,7168]{1,0:T(8,128)(2,1)}, u32[]{:S(2)}, u32[]{:S(2)}) collective-permute-start(bf16[160,7168]{1,0:T(8,128)(2,1)} %bitcast.24), channel_id=1, source_target_pairs={{0,1},{1,0},{2,3},{3,2},{4,5},{5,4},{6,7},{7,6},{8,9},{9,8},{10,11... | collective-permute-start | bytes 6881288 | tf_op jit(solution)/shard_map/ppermute | solution.py:260
  10.4 48.6 %collective-permute-start.4 = (bf16[160,7168]{1,0:T(8,128)(2,1)}, bf16[160,7168]{1,0:T(8,128)(2,1)}, u32[]{:S(2)}, u32[]{:S(2)}) collective-permute-start(bf16[160,7168]{1,0:T(8,128)(2,1)} %bitcast.26), channel_id=1, source_target_pairs={{0,1},{1,0},{2,3},{3,2},{4,5},{5,4},{6,7},{7,6},{8,9},{9,8},{10,11... | collective-permute-start | bytes 6881288 | tf_op jit(solution)/shard_map/ppermute | solution.py:260
  11.6 3.3 %copy-start.4 = (bf16[16,3712]{1,0:T(8,128)(2,1)S(1)}, bf16[16,3712]{1,0:T(8,128)(2,1)}, u32[]{:S(2)}) copy-start(bf16[16,3712]{1,0:T(8,128)(2,1)} %shard_map.104.refs_0_) | copy-start | bytes 356356
  15.7 1.4 %copy-start.1 = (bf16[8,2,16,4480]{3,2,1,0:T(8,128)(2,1)}, bf16[8,2,16,4480]{3,2,1,0:T(8,128)(2,1)S(1)}, u32[]{:S(2)}) copy-start(bf16[8,2,16,4480]{3,2,1,0:T(8,128)(2,1)S(1)} %get-tuple-element.18) | copy-start | bytes 6881284
  17.1 41.9 %all-to-all-start = ((bf16[16,16,4480]{2,1,0:T(8,128)(2,1)}), bf16[16,16,4480]{2,1,0:T(8,128)(2,1)S(1)}, u32[]{:S(2)}, u32[]{:S(2)}) async-start(bf16[16,16,4480]{2,1,0:T(8,128)(2,1)} %bitcast.23), calls=%async_computation | async-start | bytes 4587520 | tf_op jit(solution)/shard_map/all_to_all | solution.py:292
  24.2 45.8 %collective-permute-start.7 = (bf16[160,7168]{1,0:T(8,128)(2,1)}, bf16[160,7168]{1,0:T(8,128)(2,1)}, u32[]{:S(2)}, u32[]{:S(2)}) collective-permute-start(bf16[160,7168]{1,0:T(8,128)(2,1)} %w_down.1), channel_id=1, source_target_pairs={{0,1},{1,0},{2,3},{3,2},{4,5},{5,4},{6,7},{7,6},{8,9},{9,8},{10,11... | collective-permute-start | bytes 6881288 | tf_op jit(solution)/shard_map/ppermute | solution.py:260
  59.0 1.6 %copy-start.2 = (bf16[7168,160]{0,1:T(8,128)(2,1)S(1)}, bf16[7168,160]{0,1:T(8,128)(2,1)}, u32[]{:S(2)}) copy-start(bf16[7168,160]{0,1:T(8,128)(2,1)} %param.12) | copy-start | bytes 6881284
  60.7 1.6 %copy-start.3 = (bf16[7168,160]{0,1:T(8,128)(2,1)S(1)}, bf16[7168,160]{0,1:T(8,128)(2,1)}, u32[]{:S(2)}) copy-start(bf16[7168,160]{0,1:T(8,128)(2,1)} %param.13) | copy-start | bytes 6881284
  62.3 5.3 %copy-start.5 = (bf16[4,1024,512]{2,1,0:T(8,128)(2,1)S(1)}, bf16[4,1024,512]{2,1,0:T(8,128)(2,1)}, u32[]{:S(2)}) copy-start(bf16[4,1024,512]{2,1,0:T(8,128)(2,1)} %param.16) | copy-start | bytes 12582916
  67.5 2.2 %collective-permute-start.5 = (f32[2,320,256]{2,1,0:T(8,128)S(1)}, f32[2,320,256]{2,1,0:T(8,128)S(1)}, u32[]{:S(2)}, u32[]{:S(2)}) collective-permute-start(f32[2,320,256]{2,1,0:T(8,128)S(1)} %get-tuple-element.25), channel_id=1, source_target_pairs={{0,1},{1,0},{2,3},{3,2},{4,5},{5,4},{6,7},{7,6},{8,9},{9,8},{10,11... | collective-permute-start | bytes 1966088 | tf_op jit(solution)/shard_map/ppermute | solution.py:305
  67.6 3.6 %copy-start = (bf16[160,7168]{1,0:T(8,128)(2,1)S(1)}, bf16[160,7168]{1,0:T(8,128)(2,1)}, u32[]{:S(2)}) copy-start(bf16[160,7168]{1,0:T(8,128)(2,1)} %w_down.1) | copy-start | bytes 6881284
  69.7 1.5 %collective-permute-start.6 = (bf16[320,160]{1,0:T(8,128)(2,1)S(1)}, bf16[320,160]{1,0:T(8,128)(2,1)S(1)}, u32[]{:S(2)}, u32[]{:S(2)}) collective-permute-start(bf16[320,160]{1,0:T(8,128)(2,1)S(1)} %shard_map.107.hidden), channel_id=1, source_target_pairs={{0,1},{1,0},{2,3},{3,2},{4,5},{5,4},{6,7},{7,6},{8,9},{9,8},{10,11... | collective-permute-start | bytes 307208 | tf_op jit(solution)/shard_map/ppermute | solution.py:311

commit v10 on v8

--- a/solution.py
+++ b/solution.py
@@ -178,47 +178,44 @@
     return pl.ds(pl.multiple_of(f * 2 * quarter + core * quarter, LANES), quarter)
 
 
-def tails_out(quarter, core, hidden, w_down):
-    tails = []
-    for f in range(2):
-        y = dot(hidden[PLANE * BLOCK :], w_down[:, columns(quarter, core, f)])
-        tails += [y[:, : quarter // 2], y[:, quarter // 2 :]]
-    return jnp.concatenate(tails, axis=0)
-
-
 def own_kernel(quarter, block, w_gate, w_up, gate_out, up_out):
     gate, up = experts_in(quarter, lax.axis_index("c"), block, w_gate, w_up)
     gate_out[...] = gate
     up_out[...] = up
 
 
-def other_kernel(
-    quarter, block, w_gate, w_up, w_down, gate_in, up_in, hidden_out, away
-):
+def other_kernel(quarter, block, w_gate, w_up, gate_in, up_in, hidden):
     there = 1 - lax.axis_index("c")
     gate, up = experts_in(quarter, there, block, w_gate, w_up)
     gate, up = gate + gate_in[...], up + up_in[...]
-    hidden = (gate * jax.nn.sigmoid(gate) * up).astype(BF16)
-    hidden_out[...] = hidden
+    hidden[...] = (gate * jax.nn.sigmoid(gate) * up).astype(BF16)
+
+
+def outer_kernel(quarter, hidden, other_hidden, w_down, other_down, out, weights, arrived):
+    core = lax.axis_index("c")
+    main = PLANE * BLOCK
+    count = hidden.shape[1]
+    loads = [
+        pltpu.make_async_copy(
+            source.at[:, columns(quarter, core, f)],
+            weights.at[f, pl.ds(i * count, count)],
+            arrived.at[f, i],
+        )
+        for f in range(2)
+        for i, source in enumerate((w_down, other_down))
+    ]
+    for load in loads:
+        load.start()
+    both = jnp.concatenate([hidden[...], other_hidden[...]], axis=1)
+    tails = []
     for f in range(2):
-        main = dot(hidden[: PLANE * BLOCK], w_down[:, columns(quarter, there, f)])
-        away[:, f * quarter : (f + 1) * quarter] = main.astype(BF16)
-    rest = tails_out(quarter, there, hidden, w_down).astype(BF16)
-    away[:, 2 * quarter :] = dot(shuffle_table(True), rest).astype(BF16)
-
-
-def sum_kernel(quarter, hidden, w_down, got, out):
-    core = lax.axis_index("c")
-    for f in range(2):
-        at = slice(f * quarter, (f + 1) * quarter)
-        main = dot(hidden[: PLANE * BLOCK, :], w_down[:, columns(quarter, core, f)])
-        out[:, at] = (main + got[:, at].astype(F32)).astype(BF16)
-    rest = tails_out(quarter, core, hidden[...], w_down)
-    high = rest.astype(BF16)
-    low = (rest - high.astype(F32)).astype(BF16)
-    unshuffle = shuffle_table(True)
-    rest = dot(unshuffle, high) + dot(unshuffle, low)
-    out[:, 2 * quarter :] = (rest + got[:, 2 * quarter :].astype(F32)).astype(BF16)
+        loads[2 * f].wait()
+        loads[2 * f + 1].wait()
+        y = dot(both, weights[f]).astype(BF16)
+        out[:, f * quarter : (f + 1) * quarter] = y[:main]
+        tails += [y[main:, : quarter // 2], y[main:, quarter // 2 :]]
+    tails = jnp.concatenate(tails, axis=0)
+    out[:, 2 * quarter :] = dot(shuffle_table(True), tails).astype(BF16)
 
 
 def combine_kernel(quarter, back, marks, out):
@@ -300,7 +297,10 @@
 
     payload, queries = lax.optimization_barrier((payload, queries))
     weights, denominator = attention_weights(queries, cache, lengths)
-    blocks[0], weights, denominator = lax.optimization_barrier((payload, weights, denominator))
+    other_down = lax.ppermute(w_down, "c", SWAP)
+    blocks[0], weights, denominator, other_down = lax.optimization_barrier(
+        (payload, weights, denominator, other_down)
+    )
     packed, marks = call(
         functools.partial(pack_kernel, quarter),
         (
@@ -320,17 +320,26 @@
         (partial, partial),
         arrived, w_gate, w_up,
     )
-    pieces = jax.ShapeDtypeStruct((PLANE * BLOCK, width), BF16)
-    hidden, away = call(
+    gate, weights = lax.optimization_barrier((gate, weights))
+    attn_out = attention_mix(weights, denominator, cache)
+    gate, attn_out = lax.optimization_barrier((gate, attn_out))
+    hidden = call(
         functools.partial(other_kernel, quarter),
-        (jax.ShapeDtypeStruct((rows, hidden_count), BF16), pieces),
-        beside, w_gate, w_up, w_down, gate, up,
-    )
-    away, weights = lax.optimization_barrier((away, weights))
-    attn_out = attention_mix(weights, denominator, cache)
-    got = lax.ppermute(away, "c", SWAP)
-    hidden, attn_out = lax.optimization_barrier((hidden, attn_out))
-    summed = call(functools.partial(sum_kernel, quarter), pieces, hidden, w_down, got)
+        jax.ShapeDtypeStruct((rows, hidden_count), BF16),
+        beside, w_gate, w_up, gate, up,
+    )
+    near = pl.BlockSpec(memory_space=pltpu.VMEM)
+    summed = pl.pallas_call(
+        functools.partial(outer_kernel, quarter),
+        out_shape=jax.ShapeDtypeStruct((PLANE * BLOCK, width), BF16),
+        in_specs=[near, near, far, far],
+        out_specs=near,
+        scratch_shapes=[
+            pltpu.VMEM((2, 2 * hidden_count, quarter), BF16),
+            pltpu.SemaphoreType.DMA((2, 2)),
+        ],
+        compiler_params=pltpu.CompilerParams(vmem_limit_bytes=VMEM_BYTES),
+    )(hidden, lax.ppermute(hidden, "c", SWAP), w_down, other_down)
     returned = lax.all_to_all(
         summed.reshape(PLANE, BLOCK, width), ("y", "xh", "xl"), 0, 0, tiled=True
     ).reshape(PLANE * BLOCK, width)

time: 121 us -> 118 us (0.975)
  waiting for transfers between devices: 7.17 us -> 3.43 us
    pallas_call x0 -> x1, Pallas kernels: none -> 2.26 us  [shards(): pl.pallas_call(functools.partial(outer_kernel, quarter), out_shape=jax.Sh...]
    pallas_call x5 -> x4, Pallas kernels: 6.75 us -> 4.54 us  [call(): pl.pallas_call(kernel, out_shape=out_shape, in_specs=[pl.BlockSpec(memory...]
    ppermute x1, waiting for transfers between devices: 2.93 us -> 1.01 us  [shards(): beside = lax.ppermute(arrived, 'c', SWAP)]
    ppermute x1 -> x2, waiting for transfers between devices: 3.07 us -> 1.26 us  [the longest x1 1.26 us: shards(): lax.ppermute(hidden, 'c', SWAP)]
  transfers between devices with their start and end apart: 5 -> 6, of which waited for: 4 -> 3; matrix products, arithmetic and copies ran while one was open for 4% -> 4% of each run, Pallas kernels for 1% -> 3%
where the time goes in v10:
time: 118 us
  blocking collectives  91.1 us (77%)
  Pallas kernels  9.04 us (8%)
  starting transfers between devices  7.82 us (7%)
  waiting for transfers between devices  3.43 us (3%)
  matrix products  3.14 us (3%)
  local copies, waits for them, and re-layouts  1.48 us (1%)
  other arithmetic  1.42 us (1%)
    all_to_all x1, blocking collectives, shards(): lax.all_to_all(packed.reshape(PLANE, BLOCK, width), ('y', 'xh', 'xl'), 0,...  37.9 us
    all_to_all x1, blocking collectives, shards(): lax.all_to_all(summed.reshape(PLANE, BLOCK, width), ('y', 'xh', 'xl'), 0,...  33.8 us
    all_to_all x1, blocking collectives, shards(): parts = lax.all_to_all(parts, ('zl', 'zh'), 0, 0, tiled=True)  19.4 us
    pallas_call x4, Pallas kernels, call(): pl.pallas_call(kernel, out_shape=out_shape, in_specs=[pl.BlockSpec(memory...  4.54 us
    ppermute x2, starting transfers between devices, z_send(): return lax.ppermute(value, ('zl', 'zh'), z_pairs(step))  3.93 us
    ppermute x1, starting transfers between devices, z_send_apart(): return lax.ppermute(value, ('zl', 'zh', 'c'), both[0] + both[1])  3.57 us
    sub x1, matrix products, attention_weights(): weights = jnp.where(live[:, None, :], jnp.exp(scores - largest), 0.0)  2.68 us
  transfers between devices with their start and end apart: 6, of which 3 were waited for; matrix products, arithmetic and copies ran while one was open for 4% of the time, Pallas kernels for 3%

profile of v10, /device:TPU:32, one launch (start us, length us, event | category | flops | bytes accessed | tf_op | source)
XLA Modules:
  0.0 118.1 jit_solution(13142936481345728473)
XLA Ops:
  0.6 0.1 collective-permute-start
  0.7 2.2 %shard_map.104.refs_0_ = bf16[16,3712]{1,0:T(8,128)(2,1)} custom-call(bf16[16,7168]{1,0:T(8,128)(2,1)} %x_far.1, s32[2,16]{1,0:T(2,128)} %bitcast.31, f32[8,7168]{1,0:T(8,128)} %bitcast.29), custom_call_target="tpu_custom_call" | custom-call | tf_op jit(solution)/shard_map/pallas_call | solution.py:283
  3.0 2.0 %collective-permute-start.3 = (bf16[16,3712]{1,0:T(8,128)(2,1)}, bf16[16,3712]{1,0:T(8,128)(2,1)S(1)}, u32[]{:S(2)}, u32[]{:S(2)}) collective-permute-start(bf16[16,3712]{1,0:T(8,128)(2,1)} %shard_map.104.refs_0_), channel_id=1, source_target_pairs={{0,4},{4,8},{8,12},{12,2},{2,6},{6,10},{10,14},{14,0},{1,5},{5,9},... | collective-permute-start | bytes 356360 | tf_op jit(solution)/shard_map/ppermute | solution.py:38
  5.0 3.6 %collective-permute-start.2 = (bf16[16,3712]{1,0:T(8,128)(2,1)}, bf16[16,3712]{1,0:T(8,128)(2,1)S(1)}, u32[]{:S(2)}, u32[]{:S(2)}) collective-permute-start(bf16[16,3712]{1,0:T(8,128)(2,1)} %shard_map.104.refs_0_), channel_id=1, source_target_pairs={{0,10},{4,14},{8,0},{12,4},{2,8},{6,12},{10,2},{14,6},{1,9},{5,13}... | collective-permute-start | bytes 356360 | tf_op jit(solution)/shard_map/ppermute | solution.py:43
  8.6 1.9 %collective-permute-start.1 = (bf16[16,3712]{1,0:T(8,128)(2,1)}, bf16[16,3712]{1,0:T(8,128)(2,1)S(1)}, u32[]{:S(2)}, u32[]{:S(2)}) collective-permute-start(bf16[16,3712]{1,0:T(8,128)(2,1)} %shard_map.104.refs_0_), channel_id=1, source_target_pairs={{0,14},{4,0},{8,4},{12,8},{2,12},{6,2},{10,6},{14,10},{1,15},{5,1}... | collective-permute-start | bytes 356360 | tf_op jit(solution)/shard_map/ppermute | solution.py:38
  10.5 0.7 iota_compare_fusion
  11.2 0.0 copy-start.3
  11.2 2.7 %fusion.17 = (f32[4,64]{1,0:T(4,128)S(1)}, bf16[4,64,1024]{2,1,0:T(8,128)(2,1)S(1)}) fusion(pred[4,1024]{1,0:T(4,128)(4,1)S(1)} %iota_compare_fusion, bf16[4,1024,512]{2,1,0:T(8,128)(2,1)} %param.16, bf16[1,4,64,256]{3,1,2,0:T(4,128)(2,1)} %bitcast.32), kind=kOutput, calls=%fused_computation.15 | convolution fusion | flops 135791616 | bytes 2761728 | tf_op jit(solution)/shard_map/sub | solution.py:262
  13.9 0.0 collective-permute-done.other_down
  13.9 0.0 collective-permute-done.3.refs_3_
  13.9 0.0 collective-permute-done.2.refs_2_
  13.9 1.1 collective-permute-done.1.refs_1_
  15.1 0.0 copy-done.3
  15.1 0.7 shard_map.105
  15.8 0.0 copy-start
  15.8 0.0 copy-start.1
  15.8 37.9 %all_to_all.15 = bf16[16,16,4480]{2,1,0:T(8,128)(2,1)S(1)} all-to-all(bf16[16,16,4480]{2,1,0:T(8,128)(2,1)S(1)} %bitcast.28), channel_id=1, replica_groups=mesh['y'=4,'xh'=2,'xl'=2,'zl'=4,'zh'=2,'c'=2] {'y','xh','xl'}, dimensions={0} | all-to-all | bytes 4587520 | tf_op jit(solution)/shard_map/all_to_all | solution.py:312
  53.7 0.0 collective-permute-start.4
  53.7 0.0 copy-done
  53.7 0.0 copy-done.1
  53.7 0.0 copy-start.4
  53.7 1.5 %shard_map.106 = (f32[320,160]{1,0:T(8,128)S(1)}, f32[320,160]{1,0:T(8,128)S(1)}) custom-call(bf16[256,4480]{1,0:T(8,128)(2,1)S(1)} %bitcast.22, bf16[160,7168]{1,0:T(8,128)(2,1)S(1)} %bitcast.24, bf16[160,7168]{1,0:T(8,128)(2,1)S(1)} %bitcast.26), custom_call_target="tpu_custom_call" | custom-call | tf_op jit(solution)/shard_map/pallas_call | solution.py:82
  55.2 0.7 copy-done.4
  55.9 0.5 fusion.16
  56.3 0.8 copy.12
  57.1 1.0 collective-permute-done.4.block
  58.1 0.0 copy-start.2
  58.1 1.5 %shard_map.107.hidden = bf16[320,160]{1,0:T(8,128)(2,1)S(1)} custom-call(bf16[256,4480]{1,0:T(8,128)(2,1)S(1)} %collective-permute-done.4.block, bf16[160,7168]{1,0:T(8,128)(2,1)S(1)} %bitcast.25, bf16[160,7168]{1,0:T(8,128)(2,1)S(1)} %bitcast.27, f32[320,160]{1,0:T(8,128)S(1)} %get-tuple-element.25.gate_in, f32[320,160]{1,0:T(8,128)S(1)} %get-tuple-element.26.up_in), custom_call_target="tpu_custom_call" | custom-call | tf_op jit(solution)/shard_map/pallas_call | solution.py:82
  59.6 0.2 collective-permute-start.5
  59.8 1.3 %collective-permute-done.5.other_hidden = bf16[320,160]{1,0:T(8,128)(2,1)S(1)} collective-permute-done((bf16[320,160]{1,0:T(8,128)(2,1)S(1)}, bf16[320,160]{1,0:T(8,128)(2,1)S(1)}, u32[]{:S(2)}, u32[]{:S(2)}) %collective-permute-start.5) | collective-permute-done | bytes 102432 | tf_op jit(solution)/shard_map/ppermute | solution.py:342
  61.1 0.0 copy-done.2
  61.1 2.3 %shard_map.108 = bf16[256,4480]{1,0:T(8,128)(2,1)S(1)} custom-call(bf16[320,160]{1,0:T(8,128)(2,1)S(1)} %shard_map.107.hidden, bf16[320,160]{1,0:T(8,128)(2,1)S(1)} %collective-permute-done.5.other_hidden, bf16[160,7168]{1,0:T(8,128)(2,1)S(1)} %copy-done.2, bf16[160,7168]{1,0:T(8,128)(2,1)S(1)} %collective-permute-done.other_down), custom_call_target="tpu_custom_call" | custom-call | tf_op jit(solution)/shard_map/pallas_call | solution.py:332
  63.4 33.8 %all_to_all.16 = bf16[16,16,4480]{2,1,0:T(8,128)(2,1)S(1)} all-to-all(bf16[16,16,4480]{2,1,0:T(8,128)(2,1)S(1)} %bitcast.20), channel_id=1, replica_groups=mesh['y'=4,'xh'=2,'xl'=2,'zl'=4,'zh'=2,'c'=2] {'y','xh','xl'}, dimensions={0} | all-to-all | bytes 4587520 | tf_op jit(solution)/shard_map/all_to_all | solution.py:343
  97.2 0.9 shard_map.109
  98.0 19.4 %all_to_all.17 = bf16[8,16,1792]{2,1,0:T(8,128)(2,1)S(1)} all-to-all(bf16[8,16,1792]{2,1,0:T(8,128)(2,1)S(1)} %shard_map.109), channel_id=1, replica_groups=mesh['y'=4,'xh'=2,'xl'=2,'zl'=4,'zh'=2,'c'=2] {'zl','zh'}, dimensions={0} | all-to-all | bytes 917504 | tf_op jit(solution)/shard_map/all_to_all | solution.py:352
  117.4 0.7 reduce_sum.22
Async XLA Ops:
  0.6 13.3 %collective-permute-start = (bf16[160,7168]{1,0:T(8,128)(2,1)}, bf16[160,7168]{1,0:T(8,128)(2,1)S(1)}, u32[]{:S(2)}, u32[]{:S(2)}) collective-permute-start(bf16[160,7168]{1,0:T(8,128)(2,1)} %w_down.1), channel_id=1, source_target_pairs={{0,1},{1,0},{2,3},{3,2},{4,5},{5,4},{6,7},{7,6},{8,9},{9,8},{10,11... | collective-permute-start | bytes 6881288 | tf_op jit(solution)/shard_map/ppermute | solution.py:300
  3.0 10.9 %collective-permute-start.3 = (bf16[16,3712]{1,0:T(8,128)(2,1)}, bf16[16,3712]{1,0:T(8,128)(2,1)S(1)}, u32[]{:S(2)}, u32[]{:S(2)}) collective-permute-start(bf16[16,3712]{1,0:T(8,128)(2,1)} %shard_map.104.refs_0_), channel_id=1, source_target_pairs={{0,4},{4,8},{8,12},{12,2},{2,6},{6,10},{10,14},{14,0},{1,5},{5,9},... | collective-permute-start | bytes 356360 | tf_op jit(solution)/shard_map/ppermute | solution.py:38
  5.0 9.0 %collective-permute-start.2 = (bf16[16,3712]{1,0:T(8,128)(2,1)}, bf16[16,3712]{1,0:T(8,128)(2,1)S(1)}, u32[]{:S(2)}, u32[]{:S(2)}) collective-permute-start(bf16[16,3712]{1,0:T(8,128)(2,1)} %shard_map.104.refs_0_), channel_id=1, source_target_pairs={{0,10},{4,14},{8,0},{12,4},{2,8},{6,12},{10,2},{14,6},{1,9},{5,13}... | collective-permute-start | bytes 356360 | tf_op jit(solution)/shard_map/ppermute | solution.py:43
  8.6 6.5 %collective-permute-start.1 = (bf16[16,3712]{1,0:T(8,128)(2,1)}, bf16[16,3712]{1,0:T(8,128)(2,1)S(1)}, u32[]{:S(2)}, u32[]{:S(2)}) collective-permute-start(bf16[16,3712]{1,0:T(8,128)(2,1)} %shard_map.104.refs_0_), channel_id=1, source_target_pairs={{0,14},{4,0},{8,4},{12,8},{2,12},{6,2},{10,6},{14,10},{1,15},{5,1}... | collective-permute-start | bytes 356360 | tf_op jit(solution)/shard_map/ppermute | solution.py:38
  11.2 3.8 %copy-start.3 = (bf16[16,3712]{1,0:T(8,128)(2,1)S(1)}, bf16[16,3712]{1,0:T(8,128)(2,1)}, u32[]{:S(2)}) copy-start(bf16[16,3712]{1,0:T(8,128)(2,1)} %shard_map.104.refs_0_) | copy-start | bytes 356356
  15.8 37.9 %copy-start = (bf16[7168,160]{0,1:T(8,128)(2,1)S(1)}, bf16[7168,160]{0,1:T(8,128)(2,1)}, u32[]{:S(2)}) copy-start(bf16[7168,160]{0,1:T(8,128)(2,1)} %param.12) | copy-start | bytes 6881284
  15.8 37.9 %copy-start.1 = (bf16[7168,160]{0,1:T(8,128)(2,1)S(1)}, bf16[7168,160]{0,1:T(8,128)(2,1)}, u32[]{:S(2)}) copy-start(bf16[7168,160]{0,1:T(8,128)(2,1)} %param.13) | copy-start | bytes 6881284
  53.7 4.4 %collective-permute-start.4 = (bf16[256,4480]{1,0:T(8,128)(2,1)S(1)}, bf16[256,4480]{1,0:T(8,128)(2,1)S(1)}, u32[]{:S(2)}, u32[]{:S(2)}) collective-permute-start(bf16[256,4480]{1,0:T(8,128)(2,1)S(1)} %bitcast.21), channel_id=1, source_target_pairs={{0,1},{1,0},{2,3},{3,2},{4,5},{5,4},{6,7},{7,6},{8,9},{9,8},{10,11... | collective-permute-start | bytes 6881288 | tf_op jit(solution)/shard_map/ppermute | solution.py:315
  53.7 2.2 %copy-start.4 = (bf16[4,1024,512]{2,1,0:T(8,128)(2,1)S(1)}, bf16[4,1024,512]{2,1,0:T(8,128)(2,1)}, u32[]{:S(2)}) copy-start(bf16[4,1024,512]{2,1,0:T(8,128)(2,1)} %param.16) | copy-start | bytes 12582916
  58.1 3.0 %copy-start.2 = (bf16[160,7168]{1,0:T(8,128)(2,1)S(1)}, bf16[160,7168]{1,0:T(8,128)(2,1)}, u32[]{:S(2)}) copy-start(bf16[160,7168]{1,0:T(8,128)(2,1)} %w_down.1) | copy-start | bytes 6881284
  59.6 1.5 %collective-permute-start.5 = (bf16[320,160]{1,0:T(8,128)(2,1)S(1)}, bf16[320,160]{1,0:T(8,128)(2,1)S(1)}, u32[]{:S(2)}, u32[]{:S(2)}) collective-permute-start(bf16[320,160]{1,0:T(8,128)(2,1)S(1)} %shard_map.107.hidden), channel_id=1, source_target_pairs={{0,1},{1,0},{2,3},{3,2},{4,5},{5,4},{6,7},{7,6},{8,9},{9,8},{10,11... | collective-permute-start | bytes 307208 | tf_op jit(solution)/shard_map/ppermute | solution.py:342

commit v11 on v10

--- a/solution.py
+++ b/solution.py
@@ -100,7 +100,11 @@
         load.start()
     for load in loads:
         load.wait()
-    values = x_rows[...].astype(F32)
+    parts = [jnp.zeros((BLOCK, LANES), F32)] * EXPERTS
+    for at in range(0, x_rows.shape[1], LANES):
+        values = x_rows[:, at : at + LANES].astype(F32)
+        for e in range(EXPERTS):
+            parts[e] = parts[e] + values * router[e : e + 1, at : at + LANES]
     row, lane = grid(BLOCK, LANES)
     first, second = jnp.zeros_like(row), jnp.zeros_like(row)
     for r in range(BLOCK):
@@ -108,7 +112,7 @@
         second = jnp.where(row == r, ids[1, r], second)
     squashed, total = [], 0.0
     for e in range(EXPERTS):
-        logit = jnp.sum(values * router[e : e + 1, :], axis=1, keepdims=True)
+        logit = jnp.sum(parts[e], axis=1, keepdims=True)
         kept = jnp.where((first == e) | (second == e), jax.nn.sigmoid(logit), 0.0)
         squashed.append(kept)
         total = total + kept
@@ -184,16 +188,10 @@
     up_out[...] = up
 
 
-def other_kernel(quarter, block, w_gate, w_up, gate_in, up_in, hidden):
-    there = 1 - lax.axis_index("c")
-    gate, up = experts_in(quarter, there, block, w_gate, w_up)
-    gate, up = gate + gate_in[...], up + up_in[...]
-    hidden[...] = (gate * jax.nn.sigmoid(gate) * up).astype(BF16)
-
-
-def outer_kernel(quarter, hidden, other_hidden, w_down, other_down, out, weights, arrived):
+def other_kernel(
+    quarter, block, w_gate, w_up, gate_in, up_in, w_down, other_down, hidden, weights, arrived
+):
     core = lax.axis_index("c")
-    main = PLANE * BLOCK
     count = hidden.shape[1]
     loads = [
         pltpu.make_async_copy(
@@ -206,11 +204,18 @@
     ]
     for load in loads:
         load.start()
+    gate, up = experts_in(quarter, 1 - core, block, w_gate, w_up)
+    gate, up = gate + gate_in[...], up + up_in[...]
+    hidden[...] = (gate * jax.nn.sigmoid(gate) * up).astype(BF16)
+    for load in loads:
+        load.wait()
+
+
+def outer_kernel(quarter, hidden, other_hidden, weights, out):
+    main = PLANE * BLOCK
     both = jnp.concatenate([hidden[...], other_hidden[...]], axis=1)
     tails = []
     for f in range(2):
-        loads[2 * f].wait()
-        loads[2 * f + 1].wait()
         y = dot(both, weights[f]).astype(BF16)
         out[:, f * quarter : (f + 1) * quarter] = y[:main]
         tails += [y[main:, : quarter // 2], y[main:, quarter // 2 :]]
@@ -297,7 +302,7 @@
 
     payload, queries = lax.optimization_barrier((payload, queries))
     weights, denominator = attention_weights(queries, cache, lengths)
-    other_down = lax.ppermute(w_down, "c", SWAP)
+    other_down = lax.ppermute(lax.optimization_barrier((payload, w_down))[1], "c", SWAP)
     blocks[0], weights, denominator, other_down = lax.optimization_barrier(
         (payload, weights, denominator, other_down)
     )
@@ -323,23 +328,23 @@
     gate, weights = lax.optimization_barrier((gate, weights))
     attn_out = attention_mix(weights, denominator, cache)
     gate, attn_out = lax.optimization_barrier((gate, attn_out))
-    hidden = call(
+    near = pl.BlockSpec(memory_space=pltpu.VMEM)
+    hidden, down = pl.pallas_call(
         functools.partial(other_kernel, quarter),
-        jax.ShapeDtypeStruct((rows, hidden_count), BF16),
-        beside, w_gate, w_up, gate, up,
-    )
-    near = pl.BlockSpec(memory_space=pltpu.VMEM)
-    summed = pl.pallas_call(
+        out_shape=(
+            jax.ShapeDtypeStruct((rows, hidden_count), BF16),
+            jax.ShapeDtypeStruct((2, 2 * hidden_count, quarter), BF16),
+        ),
+        in_specs=[near] * 5 + [far] * 2,
+        out_specs=(near, near),
+        scratch_shapes=[pltpu.SemaphoreType.DMA((2, 2))],
+        compiler_params=pltpu.CompilerParams(vmem_limit_bytes=VMEM_BYTES),
+    )(beside, w_gate, w_up, gate, up, w_down, other_down)
+    summed = call(
         functools.partial(outer_kernel, quarter),
-        out_shape=jax.ShapeDtypeStruct((PLANE * BLOCK, width), BF16),
-        in_specs=[near, near, far, far],
-        out_specs=near,
-        scratch_shapes=[
-            pltpu.VMEM((2, 2 * hidden_count, quarter), BF16),
-            pltpu.SemaphoreType.DMA((2, 2)),
-        ],
-        compiler_params=pltpu.CompilerParams(vmem_limit_bytes=VMEM_BYTES),
-    )(hidden, lax.ppermute(hidden, "c", SWAP), w_down, other_down)
+        jax.ShapeDtypeStruct((PLANE * BLOCK, width), BF16),
+        hidden, lax.ppermute(hidden, "c", SWAP), down,
+    )
     returned = lax.all_to_all(
         summed.reshape(PLANE, BLOCK, width), ("y", "xh", "xl"), 0, 0, tiled=True
     ).reshape(PLANE * BLOCK, width)

time: 118 us -> 118 us (level)
  transfers between devices with their start and end apart: 6 -> 6, of which waited for: 3 -> 3; matrix products, arithmetic and copies ran while one was open for 4% -> 4% of each run, Pallas kernels for 3% -> 1%
where the time goes in v11:
time: 118 us
  blocking collectives  91.2 us (77%)
  Pallas kernels  8.59 us (7%)
  starting transfers between devices  7.82 us (7%)
  waiting for transfers between devices  3.43 us (3%)
  matrix products  3.14 us (3%)
  local copies, waits for them, and re-layouts  1.47 us (1%)
  other arithmetic  1.42 us (1%)
    all_to_all x1, blocking collectives, shards(): lax.all_to_all(packed.reshape(PLANE, BLOCK, width), ('y', 'xh', 'xl'), 0,...  37.8 us
    all_to_all x1, blocking collectives, shards(): lax.all_to_all(summed.reshape(PLANE, BLOCK, width), ('y', 'xh', 'xl'), 0,...  33.8 us
    all_to_all x1, blocking collectives, shards(): parts = lax.all_to_all(parts, ('zl', 'zh'), 0, 0, tiled=True)  19.6 us
    pallas_call x4, Pallas kernels, call(): pl.pallas_call(kernel, out_shape=out_shape, in_specs=[pl.BlockSpec(memory...  4.69 us
    ppermute x2, starting transfers between devices, z_send(): return lax.ppermute(value, ('zl', 'zh'), z_pairs(step))  3.93 us
    ppermute x1, starting transfers between devices, z_send_apart(): return lax.ppermute(value, ('zl', 'zh', 'c'), both[0] + both[1])  3.57 us
    sub x1, matrix products, attention_weights(): weights = jnp.where(live[:, None, :], jnp.exp(scores - largest), 0.0)  2.67 us
  transfers between devices with their start and end apart: 6, of which 3 were waited for; matrix products, arithmetic and copies ran while one was open for 4% of the time, Pallas kernels for 1%

profile of v11, /device:TPU:32, one launch (start us, length us, event | category | flops | bytes accessed | tf_op | source)
XLA Modules:
  0.0 117.8 jit_solution(1403584837321087295)
XLA Ops:
  0.6 2.1 %shard_map.104.refs_0_ = bf16[16,3712]{1,0:T(8,128)(2,1)} custom-call(bf16[16,7168]{1,0:T(8,128)(2,1)} %x_far.1, s32[2,16]{1,0:T(2,128)} %bitcast.31, f32[8,7168]{1,0:T(8,128)} %bitcast.29), custom_call_target="tpu_custom_call" | custom-call | tf_op jit(solution)/shard_map/pallas_call | solution.py:288
  2.8 0.1 collective-permute-start
  2.9 2.0 %collective-permute-start.3 = (bf16[16,3712]{1,0:T(8,128)(2,1)}, bf16[16,3712]{1,0:T(8,128)(2,1)S(1)}, u32[]{:S(2)}, u32[]{:S(2)}) collective-permute-start(bf16[16,3712]{1,0:T(8,128)(2,1)} %shard_map.104.refs_0_), channel_id=1, source_target_pairs={{0,4},{4,8},{8,12},{12,2},{2,6},{6,10},{10,14},{14,0},{1,5},{5,9},... | collective-permute-start | bytes 356360 | tf_op jit(solution)/shard_map/ppermute | solution.py:38
  4.9 3.6 %collective-permute-start.2 = (bf16[16,3712]{1,0:T(8,128)(2,1)}, bf16[16,3712]{1,0:T(8,128)(2,1)S(1)}, u32[]{:S(2)}, u32[]{:S(2)}) collective-permute-start(bf16[16,3712]{1,0:T(8,128)(2,1)} %shard_map.104.refs_0_), channel_id=1, source_target_pairs={{0,10},{4,14},{8,0},{12,4},{2,8},{6,12},{10,2},{14,6},{1,9},{5,13}... | collective-permute-start | bytes 356360 | tf_op jit(solution)/shard_map/ppermute | solution.py:43
  8.4 1.9 %collective-permute-start.1 = (bf16[16,3712]{1,0:T(8,128)(2,1)}, bf16[16,3712]{1,0:T(8,128)(2,1)S(1)}, u32[]{:S(2)}, u32[]{:S(2)}) collective-permute-start(bf16[16,3712]{1,0:T(8,128)(2,1)} %shard_map.104.refs_0_), channel_id=1, source_target_pairs={{0,14},{4,0},{8,4},{12,8},{2,12},{6,2},{10,6},{14,10},{1,15},{5,1}... | collective-permute-start | bytes 356360 | tf_op jit(solution)/shard_map/ppermute | solution.py:38
  10.4 0.7 iota_compare_fusion
  11.1 0.0 copy-start.3
  11.1 2.7 %fusion.17 = (f32[4,64]{1,0:T(4,128)S(1)}, bf16[4,64,1024]{2,1,0:T(8,128)(2,1)S(1)}) fusion(pred[4,1024]{1,0:T(4,128)(4,1)S(1)} %iota_compare_fusion, bf16[4,1024,512]{2,1,0:T(8,128)(2,1)} %param.16, bf16[1,4,64,256]{3,1,2,0:T(4,128)(2,1)} %bitcast.32), kind=kOutput, calls=%fused_computation.15 | convolution fusion | flops 135791616 | bytes 2761728 | tf_op jit(solution)/shard_map/sub | solution.py:267
  13.8 0.0 collective-permute-done.other_down
  13.8 0.0 collective-permute-done.3.refs_3_
  13.8 0.0 collective-permute-done.2.refs_2_
  13.8 1.1 collective-permute-done.1.refs_1_
  15.0 0.0 copy-done.3
  15.0 0.7 shard_map.105
  15.7 0.0 copy-start
  15.7 0.0 copy-start.1
  15.7 37.8 %all_to_all.15 = bf16[16,16,4480]{2,1,0:T(8,128)(2,1)S(1)} all-to-all(bf16[16,16,4480]{2,1,0:T(8,128)(2,1)S(1)} %bitcast.28), channel_id=1, replica_groups=mesh['y'=4,'xh'=2,'xl'=2,'zl'=4,'zh'=2,'c'=2] {'y','xh','xl'}, dimensions={0} | all-to-all | bytes 4587520 | tf_op jit(solution)/shard_map/all_to_all | solution.py:317
  53.6 0.0 collective-permute-start.4
  53.6 0.0 copy-done
  53.6 0.0 copy-done.1
  53.6 0.0 copy-start.4
  53.6 1.5 %shard_map.106 = (f32[320,160]{1,0:T(8,128)S(1)}, f32[320,160]{1,0:T(8,128)S(1)}) custom-call(bf16[256,4480]{1,0:T(8,128)(2,1)S(1)} %bitcast.21, bf16[160,7168]{1,0:T(8,128)(2,1)S(1)} %bitcast.24, bf16[160,7168]{1,0:T(8,128)(2,1)S(1)} %bitcast.26), custom_call_target="tpu_custom_call" | custom-call | tf_op jit(solution)/shard_map/pallas_call | solution.py:82
  55.1 0.0 copy-start.2
  55.1 0.7 copy-done.4
  55.8 0.5 fusion.16
  56.2 0.8 copy.12
  57.0 1.0 collective-permute-done.4.block
  58.0 0.0 copy-done.2
  58.0 1.8 %shard_map.107 = (bf16[320,160]{1,0:T(8,128)(2,1)S(1)}, bf16[2,320,1792]{2,1,0:T(8,128)(2,1)S(1)}) custom-call(bf16[256,4480]{1,0:T(8,128)(2,1)S(1)} %collective-permute-done.4.block, bf16[160,7168]{1,0:T(8,128)(2,1)S(1)} %bitcast.25, bf16[160,7168]{1,0:T(8,128)(2,1)S(1)} %bitcast.27, f32[320,160]{1,0:T(8,128)S(1)} %get-tuple-element.29.gate_in, ...), custom_call_target="tpu_custom_call" | custom-call | tf_op jit(solution)/shard_map/pallas_call | solution.py:332
  59.8 0.2 collective-permute-start.5
  60.0 1.3 %collective-permute-done.5.other_hidden = bf16[320,160]{1,0:T(8,128)(2,1)S(1)} collective-permute-done((bf16[320,160]{1,0:T(8,128)(2,1)S(1)}, bf16[320,160]{1,0:T(8,128)(2,1)S(1)}, u32[]{:S(2)}, u32[]{:S(2)}) %collective-permute-start.5) | collective-permute-done | bytes 102432 | tf_op jit(solution)/shard_map/ppermute | solution.py:346
  61.3 1.6 %shard_map.108 = bf16[256,4480]{1,0:T(8,128)(2,1)S(1)} custom-call(bf16[320,160]{1,0:T(8,128)(2,1)S(1)} %get-tuple-element.32.hidden, bf16[320,160]{1,0:T(8,128)(2,1)S(1)} %collective-permute-done.5.other_hidden, bf16[2,320,1792]{2,1,0:T(8,128)(2,1)S(1)} %get-tuple-element.33.weights), custom_call_target="tpu_custom_call" | custom-call | tf_op jit(solution)/shard_map/pallas_call | solution.py:82
  62.9 33.8 %all_to_all.16 = bf16[16,16,4480]{2,1,0:T(8,128)(2,1)S(1)} all-to-all(bf16[16,16,4480]{2,1,0:T(8,128)(2,1)S(1)} %bitcast.22), channel_id=1, replica_groups=mesh['y'=4,'xh'=2,'xl'=2,'zl'=4,'zh'=2,'c'=2] {'y','xh','xl'}, dimensions={0} | all-to-all | bytes 4587520 | tf_op jit(solution)/shard_map/all_to_all | solution.py:348
  96.7 0.8 shard_map.109
  97.5 19.6 %all_to_all.17 = bf16[8,16,1792]{2,1,0:T(8,128)(2,1)S(1)} all-to-all(bf16[8,16,1792]{2,1,0:T(8,128)(2,1)S(1)} %shard_map.109), channel_id=1, replica_groups=mesh['y'=4,'xh'=2,'xl'=2,'zl'=4,'zh'=2,'c'=2] {'zl','zh'}, dimensions={0} | all-to-all | bytes 917504 | tf_op jit(solution)/shard_map/all_to_all | solution.py:357
  117.1 0.7 reduce_sum.22
Async XLA Ops:
  2.8 11.0 %collective-permute-start = (bf16[160,7168]{1,0:T(8,128)(2,1)}, bf16[160,7168]{1,0:T(8,128)(2,1)S(1)}, u32[]{:S(2)}, u32[]{:S(2)}) collective-permute-start(bf16[160,7168]{1,0:T(8,128)(2,1)} %w_down.1), channel_id=1, source_target_pairs={{0,1},{1,0},{2,3},{3,2},{4,5},{5,4},{6,7},{7,6},{8,9},{9,8},{10,11... | collective-permute-start | bytes 6881288 | tf_op jit(solution)/shard_map/ppermute | solution.py:305
  2.9 10.9 %collective-permute-start.3 = (bf16[16,3712]{1,0:T(8,128)(2,1)}, bf16[16,3712]{1,0:T(8,128)(2,1)S(1)}, u32[]{:S(2)}, u32[]{:S(2)}) collective-permute-start(bf16[16,3712]{1,0:T(8,128)(2,1)} %shard_map.104.refs_0_), channel_id=1, source_target_pairs={{0,4},{4,8},{8,12},{12,2},{2,6},{6,10},{10,14},{14,0},{1,5},{5,9},... | collective-permute-start | bytes 356360 | tf_op jit(solution)/shard_map/ppermute | solution.py:38
  4.9 9.0 %collective-permute-start.2 = (bf16[16,3712]{1,0:T(8,128)(2,1)}, bf16[16,3712]{1,0:T(8,128)(2,1)S(1)}, u32[]{:S(2)}, u32[]{:S(2)}) collective-permute-start(bf16[16,3712]{1,0:T(8,128)(2,1)} %shard_map.104.refs_0_), channel_id=1, source_target_pairs={{0,10},{4,14},{8,0},{12,4},{2,8},{6,12},{10,2},{14,6},{1,9},{5,13}... | collective-permute-start | bytes 356360 | tf_op jit(solution)/shard_map/ppermute | solution.py:43
  8.4 6.5 %collective-permute-start.1 = (bf16[16,3712]{1,0:T(8,128)(2,1)}, bf16[16,3712]{1,0:T(8,128)(2,1)S(1)}, u32[]{:S(2)}, u32[]{:S(2)}) collective-permute-start(bf16[16,3712]{1,0:T(8,128)(2,1)} %shard_map.104.refs_0_), channel_id=1, source_target_pairs={{0,14},{4,0},{8,4},{12,8},{2,12},{6,2},{10,6},{14,10},{1,15},{5,1}... | collective-permute-start | bytes 356360 | tf_op jit(solution)/shard_map/ppermute | solution.py:38
  11.1 3.8 %copy-start.3 = (bf16[16,3712]{1,0:T(8,128)(2,1)S(1)}, bf16[16,3712]{1,0:T(8,128)(2,1)}, u32[]{:S(2)}) copy-start(bf16[16,3712]{1,0:T(8,128)(2,1)} %shard_map.104.refs_0_) | copy-start | bytes 356356
  15.7 37.9 %copy-start = (bf16[7168,160]{0,1:T(8,128)(2,1)S(1)}, bf16[7168,160]{0,1:T(8,128)(2,1)}, u32[]{:S(2)}) copy-start(bf16[7168,160]{0,1:T(8,128)(2,1)} %param.12) | copy-start | bytes 6881284
  15.7 37.9 %copy-start.1 = (bf16[7168,160]{0,1:T(8,128)(2,1)S(1)}, bf16[7168,160]{0,1:T(8,128)(2,1)}, u32[]{:S(2)}) copy-start(bf16[7168,160]{0,1:T(8,128)(2,1)} %param.13) | copy-start | bytes 6881284
  53.6 4.4 %collective-permute-start.4 = (bf16[256,4480]{1,0:T(8,128)(2,1)S(1)}, bf16[256,4480]{1,0:T(8,128)(2,1)S(1)}, u32[]{:S(2)}, u32[]{:S(2)}) collective-permute-start(bf16[256,4480]{1,0:T(8,128)(2,1)S(1)} %bitcast.20), channel_id=1, source_target_pairs={{0,1},{1,0},{2,3},{3,2},{4,5},{5,4},{6,7},{7,6},{8,9},{9,8},{10,11... | collective-permute-start | bytes 6881288 | tf_op jit(solution)/shard_map/ppermute | solution.py:320
  53.6 2.2 %copy-start.4 = (bf16[4,1024,512]{2,1,0:T(8,128)(2,1)S(1)}, bf16[4,1024,512]{2,1,0:T(8,128)(2,1)}, u32[]{:S(2)}) copy-start(bf16[4,1024,512]{2,1,0:T(8,128)(2,1)} %param.16) | copy-start | bytes 12582916
  55.1 2.9 %copy-start.2 = (bf16[160,7168]{1,0:T(8,128)(2,1)S(1)}, bf16[160,7168]{1,0:T(8,128)(2,1)}, u32[]{:S(2)}) copy-start(bf16[160,7168]{1,0:T(8,128)(2,1)} %w_down.1) | copy-start | bytes 6881284
  59.8 1.5 %collective-permute-start.5 = (bf16[320,160]{1,0:T(8,128)(2,1)S(1)}, bf16[320,160]{1,0:T(8,128)(2,1)S(1)}, u32[]{:S(2)}, u32[]{:S(2)}) collective-permute-start(bf16[320,160]{1,0:T(8,128)(2,1)S(1)} %get-tuple-element.32.hidden), channel_id=1, source_target_pairs={{0,1},{1,0},{2,3},{3,2},{4,5},{5,4},{6,7},{7,6},{8,9},{9,8},{10,11... | collective-permute-start | bytes 307208 | tf_op jit(solution)/shard_map/ppermute | solution.py:346

commit v12 on v11

--- a/solution.py
+++ b/solution.py
@@ -15,6 +15,7 @@
 EXPERTS = 8
 BLOCK = 16
 PLANE = 16
+PLANE_AXES = ("y", "xl", "xh")
 LANES = 128
 REACH = (0, 1, 2, -1)
 HIGH, LOW = 64, 72
@@ -150,16 +151,16 @@
     slot, row = grid(EXPERTS * BLOCK, ZLO * BLOCK)
     mask = ones(fifth(slot & 15) == row >> 4)
     main = dot((dot_t(pick_main, chosen) * mask).astype(BF16), rows)
-    main = main.astype(BF16).reshape(EXPERTS, BLOCK, half)
+    main = main.astype(BF16).reshape(EXPERTS // 2, 2, BLOCK, half)
     chosen4 = jnp.concatenate([chosen] * 4, axis=0)
     rows4 = jnp.concatenate([rows[:, i * eighth : (i + 1) * eighth] for i in range(4)], axis=0)
     slot, row = grid(EXPERTS * BLOCK, 4 * ZLO * BLOCK)
     mask = ones(((slot >> 2) & 3 == row >> 6) & ((row >> 4) & 3 == 3))
     rest = dot((dot_t(pick_rest, chosen4) * mask).astype(BF16), rows4)
-    rest = rest.astype(BF16).reshape(EXPERTS, BLOCK, eighth)
+    rest = rest.astype(BF16).reshape(EXPERTS // 2, 2, BLOCK, eighth)
     for x in range(2):
-        out[:, x, :, :half] = main
-        out[:, x, :, half:] = rest
+        out[:, x, :, :, :half] = main
+        out[:, x, :, :, half:] = rest
 
 
 def experts_in(quarter, core, block, w_gate, w_up):
@@ -227,7 +228,7 @@
     half = 2 * quarter
     chosen = marks[...]
     lane, slot = grid(LANES, PLANE * BLOCK)
-    expert = slot >> 5
+    expert = ((slot >> 6) << 1) + ((slot >> 4) & 1)
     same = fifth(lane) == expert
     back_main = ones(same & (fifth_rest(lane) == fifth_rest(slot & 15))).astype(BF16)
     back_rest = ones(same & (fifth_rest(lane) == 1 + (slot & 3))).astype(BF16)
@@ -251,7 +252,7 @@
         owner = (lax.axis_index("zl") + (REACH[k] % ZLO)) & (ZLO - 1)
         for f in range(2):
             piece = total[k * BLOCK : (k + 1) * BLOCK, f * quarter : (f + 1) * quarter]
-            out[owner * 2 + f] = piece.astype(BF16)
+            out[f * ZLO + owner] = piece.astype(BF16)
 
 
 def attention_weights(queries, cache, lengths):
@@ -309,13 +310,13 @@
     packed, marks = call(
         functools.partial(pack_kernel, quarter),
         (
-            jax.ShapeDtypeStruct((EXPERTS, 2, BLOCK, width), BF16),
+            jax.ShapeDtypeStruct((EXPERTS // 2, 2, 2, BLOCK, width), BF16),
             jax.ShapeDtypeStruct((ZLO * BLOCK, LANES), BF16),
         ),
         *blocks,
     )
     arrived = lax.all_to_all(
-        packed.reshape(PLANE, BLOCK, width), ("y", "xh", "xl"), 0, 0, tiled=True
+        packed.reshape(PLANE, BLOCK, width), PLANE_AXES, 0, 0, tiled=True
     ).reshape(PLANE * BLOCK, width)
     beside = lax.ppermute(arrived, "c", SWAP)
     rows = PLANE * (BLOCK + ZLO)
@@ -346,7 +347,7 @@
         hidden, lax.ppermute(hidden, "c", SWAP), down,
     )
     returned = lax.all_to_all(
-        summed.reshape(PLANE, BLOCK, width), ("y", "xh", "xl"), 0, 0, tiled=True
+        summed.reshape(PLANE, BLOCK, width), PLANE_AXES, 0, 0, tiled=True
     ).reshape(PLANE * BLOCK, width)
 
     parts = call(
@@ -354,7 +355,7 @@
         jax.ShapeDtypeStruct((ZALL, BLOCK, quarter), BF16),
         returned, marks,
     )
-    parts = lax.all_to_all(parts, ("zl", "zh"), 0, 0, tiled=True)
+    parts = lax.all_to_all(parts, ("zh", "zl"), 0, 0, tiled=True)
     moe_out = jnp.sum(parts.astype(F32), axis=0)
     return (moe_out.astype(BF16), attn_out)
 

time: 118 us -> 118 us (level)
  no operation moved by 1% of the time
where the time goes in v12:
time: 118 us; the launch traced here: 117 us
  blocking collectives  90.6 us (77%)
  Pallas kernels  8.6 us (7%)
  starting transfers between devices  7.82 us (7%)
  waiting for transfers between devices  3.43 us (3%)
  matrix products  3.14 us (3%)
  local copies, waits for them, and re-layouts  1.47 us (1%)
  other arithmetic  1.42 us (1%)
    all_to_all x1, blocking collectives, shards(): lax.all_to_all(packed.reshape(PLANE, BLOCK, width), PLANE_AXES, 0, 0, til...  37.7 us
    all_to_all x1, blocking collectives, shards(): lax.all_to_all(summed.reshape(PLANE, BLOCK, width), PLANE_AXES, 0, 0, til...  33.9 us
    all_to_all x1, blocking collectives, shards(): parts = lax.all_to_all(parts, ('zh', 'zl'), 0, 0, tiled=True)  19 us
    pallas_call x4, Pallas kernels, call(): pl.pallas_call(kernel, out_shape=out_shape, in_specs=[pl.BlockSpec(memory...  4.7 us
    ppermute x2, starting transfers between devices, z_send(): return lax.ppermute(value, ('zl', 'zh'), z_pairs(step))  3.93 us
    ppermute x1, starting transfers between devices, z_send_apart(): return lax.ppermute(value, ('zl', 'zh', 'c'), both[0] + both[1])  3.57 us
    sub x1, matrix products, attention_weights(): weights = jnp.where(live[:, None, :], jnp.exp(scores - largest), 0.0)  2.67 us
  transfers between devices with their start and end apart: 6, of which 3 were waited for; matrix products, arithmetic and copies ran while one was open for 4% of the time, Pallas kernels for 1%

profile of v12, /device:TPU:32, one launch (start us, length us, event | category | flops | bytes accessed | tf_op | source)
XLA Modules:
  0.0 117.2 jit_solution(4151933302115374329)
XLA Ops:
  0.6 2.1 %shard_map.104.refs_0_ = bf16[16,3712]{1,0:T(8,128)(2,1)} custom-call(bf16[16,7168]{1,0:T(8,128)(2,1)} %x_far.1, s32[2,16]{1,0:T(2,128)} %bitcast.31, f32[8,7168]{1,0:T(8,128)} %bitcast.29), custom_call_target="tpu_custom_call" | custom-call | tf_op jit(solution)/shard_map/pallas_call | solution.py:289
  2.8 0.1 collective-permute-start
  2.9 2.0 %collective-permute-start.3 = (bf16[16,3712]{1,0:T(8,128)(2,1)}, bf16[16,3712]{1,0:T(8,128)(2,1)S(1)}, u32[]{:S(2)}, u32[]{:S(2)}) collective-permute-start(bf16[16,3712]{1,0:T(8,128)(2,1)} %shard_map.104.refs_0_), channel_id=1, source_target_pairs={{0,4},{4,8},{8,12},{12,2},{2,6},{6,10},{10,14},{14,0},{1,5},{5,9},... | collective-permute-start | bytes 356360 | tf_op jit(solution)/shard_map/ppermute | solution.py:39
  4.9 3.6 %collective-permute-start.2 = (bf16[16,3712]{1,0:T(8,128)(2,1)}, bf16[16,3712]{1,0:T(8,128)(2,1)S(1)}, u32[]{:S(2)}, u32[]{:S(2)}) collective-permute-start(bf16[16,3712]{1,0:T(8,128)(2,1)} %shard_map.104.refs_0_), channel_id=1, source_target_pairs={{0,10},{4,14},{8,0},{12,4},{2,8},{6,12},{10,2},{14,6},{1,9},{5,13}... | collective-permute-start | bytes 356360 | tf_op jit(solution)/shard_map/ppermute | solution.py:44
  8.4 1.9 %collective-permute-start.1 = (bf16[16,3712]{1,0:T(8,128)(2,1)}, bf16[16,3712]{1,0:T(8,128)(2,1)S(1)}, u32[]{:S(2)}, u32[]{:S(2)}) collective-permute-start(bf16[16,3712]{1,0:T(8,128)(2,1)} %shard_map.104.refs_0_), channel_id=1, source_target_pairs={{0,14},{4,0},{8,4},{12,8},{2,12},{6,2},{10,6},{14,10},{1,15},{5,1}... | collective-permute-start | bytes 356360 | tf_op jit(solution)/shard_map/ppermute | solution.py:39
  10.4 0.7 iota_compare_fusion
  11.1 0.0 copy-start.3
  11.1 2.7 %fusion.17 = (f32[4,64]{1,0:T(4,128)S(1)}, bf16[4,64,1024]{2,1,0:T(8,128)(2,1)S(1)}) fusion(pred[4,1024]{1,0:T(4,128)(4,1)S(1)} %iota_compare_fusion, bf16[4,1024,512]{2,1,0:T(8,128)(2,1)} %param.16, bf16[1,4,64,256]{3,1,2,0:T(4,128)(2,1)} %bitcast.32), kind=kOutput, calls=%fused_computation.15 | convolution fusion | flops 135791616 | bytes 2761728 | tf_op jit(solution)/shard_map/sub | solution.py:268
  13.8 0.0 collective-permute-done.other_down
  13.8 0.0 collective-permute-done.3.refs_3_
  13.8 0.0 collective-permute-done.2.refs_2_
  13.8 1.1 collective-permute-done.1.refs_1_
  15.0 0.0 copy-done.3
  15.0 0.7 shard_map.105
  15.7 0.0 copy-start
  15.7 0.0 copy-start.1
  15.7 37.7 %all_to_all.15 = bf16[16,16,4480]{2,1,0:T(8,128)(2,1)S(1)} all-to-all(bf16[16,16,4480]{2,1,0:T(8,128)(2,1)S(1)} %bitcast.28), channel_id=1, replica_groups=mesh['y'=4,'xh'=2,'xl'=2,'zl'=4,'zh'=2,'c'=2] {'y','xl','xh'}, dimensions={0} | all-to-all | bytes 4587520 | tf_op jit(solution)/shard_map/all_to_all | solution.py:318
  53.4 0.0 collective-permute-start.4
  53.4 0.0 copy-done
  53.4 0.0 copy-done.1
  53.4 0.0 copy-start.4
  53.4 1.5 %shard_map.106 = (f32[320,160]{1,0:T(8,128)S(1)}, f32[320,160]{1,0:T(8,128)S(1)}) custom-call(bf16[256,4480]{1,0:T(8,128)(2,1)S(1)} %bitcast.21, bf16[160,7168]{1,0:T(8,128)(2,1)S(1)} %bitcast.24, bf16[160,7168]{1,0:T(8,128)(2,1)S(1)} %bitcast.26), custom_call_target="tpu_custom_call" | custom-call | tf_op jit(solution)/shard_map/pallas_call | solution.py:83
  54.9 0.0 copy-start.2
  54.9 0.7 copy-done.4
  55.6 0.5 fusion.16
  56.1 0.8 copy.12
  56.8 1.0 collective-permute-done.4.block
  57.8 0.0 copy-done.2
  57.9 1.8 %shard_map.107 = (bf16[320,160]{1,0:T(8,128)(2,1)S(1)}, bf16[2,320,1792]{2,1,0:T(8,128)(2,1)S(1)}) custom-call(bf16[256,4480]{1,0:T(8,128)(2,1)S(1)} %collective-permute-done.4.block, bf16[160,7168]{1,0:T(8,128)(2,1)S(1)} %bitcast.25, bf16[160,7168]{1,0:T(8,128)(2,1)S(1)} %bitcast.27, f32[320,160]{1,0:T(8,128)S(1)} %get-tuple-element.29.gate_in, ...), custom_call_target="tpu_custom_call" | custom-call | tf_op jit(solution)/shard_map/pallas_call | solution.py:333
  59.6 0.2 collective-permute-start.5
  59.8 1.3 %collective-permute-done.5.other_hidden = bf16[320,160]{1,0:T(8,128)(2,1)S(1)} collective-permute-done((bf16[320,160]{1,0:T(8,128)(2,1)S(1)}, bf16[320,160]{1,0:T(8,128)(2,1)S(1)}, u32[]{:S(2)}, u32[]{:S(2)}) %collective-permute-start.5) | collective-permute-done | bytes 102432 | tf_op jit(solution)/shard_map/ppermute | solution.py:347
  61.1 1.6 %shard_map.108 = bf16[256,4480]{1,0:T(8,128)(2,1)S(1)} custom-call(bf16[320,160]{1,0:T(8,128)(2,1)S(1)} %get-tuple-element.32.hidden, bf16[320,160]{1,0:T(8,128)(2,1)S(1)} %collective-permute-done.5.other_hidden, bf16[2,320,1792]{2,1,0:T(8,128)(2,1)S(1)} %get-tuple-element.33.weights), custom_call_target="tpu_custom_call" | custom-call | tf_op jit(solution)/shard_map/pallas_call | solution.py:83
  62.7 33.9 %all_to_all.16 = bf16[16,16,4480]{2,1,0:T(8,128)(2,1)S(1)} all-to-all(bf16[16,16,4480]{2,1,0:T(8,128)(2,1)S(1)} %bitcast.22), channel_id=1, replica_groups=mesh['y'=4,'xh'=2,'xl'=2,'zl'=4,'zh'=2,'c'=2] {'y','xl','xh'}, dimensions={0} | all-to-all | bytes 4587520 | tf_op jit(solution)/shard_map/all_to_all | solution.py:349
  96.6 0.9 shard_map.109
  97.5 19.0 %all_to_all.17 = bf16[8,16,1792]{2,1,0:T(8,128)(2,1)S(1)} all-to-all(bf16[8,16,1792]{2,1,0:T(8,128)(2,1)S(1)} %shard_map.109), channel_id=1, replica_groups=mesh['y'=4,'xh'=2,'xl'=2,'zl'=4,'zh'=2,'c'=2] {'zh','zl'}, dimensions={0} | all-to-all | bytes 917504 | tf_op jit(solution)/shard_map/all_to_all | solution.py:358
  116.5 0.7 reduce_sum.22
Async XLA Ops:
  2.8 11.0 %collective-permute-start = (bf16[160,7168]{1,0:T(8,128)(2,1)}, bf16[160,7168]{1,0:T(8,128)(2,1)S(1)}, u32[]{:S(2)}, u32[]{:S(2)}) collective-permute-start(bf16[160,7168]{1,0:T(8,128)(2,1)} %w_down.1), channel_id=1, source_target_pairs={{0,1},{1,0},{2,3},{3,2},{4,5},{5,4},{6,7},{7,6},{8,9},{9,8},{10,11... | collective-permute-start | bytes 6881288 | tf_op jit(solution)/shard_map/ppermute | solution.py:306
  2.9 10.9 %collective-permute-start.3 = (bf16[16,3712]{1,0:T(8,128)(2,1)}, bf16[16,3712]{1,0:T(8,128)(2,1)S(1)}, u32[]{:S(2)}, u32[]{:S(2)}) collective-permute-start(bf16[16,3712]{1,0:T(8,128)(2,1)} %shard_map.104.refs_0_), channel_id=1, source_target_pairs={{0,4},{4,8},{8,12},{12,2},{2,6},{6,10},{10,14},{14,0},{1,5},{5,9},... | collective-permute-start | bytes 356360 | tf_op jit(solution)/shard_map/ppermute | solution.py:39
  4.9 9.0 %collective-permute-start.2 = (bf16[16,3712]{1,0:T(8,128)(2,1)}, bf16[16,3712]{1,0:T(8,128)(2,1)S(1)}, u32[]{:S(2)}, u32[]{:S(2)}) collective-permute-start(bf16[16,3712]{1,0:T(8,128)(2,1)} %shard_map.104.refs_0_), channel_id=1, source_target_pairs={{0,10},{4,14},{8,0},{12,4},{2,8},{6,12},{10,2},{14,6},{1,9},{5,13}... | collective-permute-start | bytes 356360 | tf_op jit(solution)/shard_map/ppermute | solution.py:44
  8.4 6.5 %collective-permute-start.1 = (bf16[16,3712]{1,0:T(8,128)(2,1)}, bf16[16,3712]{1,0:T(8,128)(2,1)S(1)}, u32[]{:S(2)}, u32[]{:S(2)}) collective-permute-start(bf16[16,3712]{1,0:T(8,128)(2,1)} %shard_map.104.refs_0_), channel_id=1, source_target_pairs={{0,14},{4,0},{8,4},{12,8},{2,12},{6,2},{10,6},{14,10},{1,15},{5,1}... | collective-permute-start | bytes 356360 | tf_op jit(solution)/shard_map/ppermute | solution.py:39
  11.1 3.8 %copy-start.3 = (bf16[16,3712]{1,0:T(8,128)(2,1)S(1)}, bf16[16,3712]{1,0:T(8,128)(2,1)}, u32[]{:S(2)}) copy-start(bf16[16,3712]{1,0:T(8,128)(2,1)} %shard_map.104.refs_0_) | copy-start | bytes 356356
  15.7 37.7 %copy-start = (bf16[7168,160]{0,1:T(8,128)(2,1)S(1)}, bf16[7168,160]{0,1:T(8,128)(2,1)}, u32[]{:S(2)}) copy-start(bf16[7168,160]{0,1:T(8,128)(2,1)} %param.12) | copy-start | bytes 6881284
  15.7 37.7 %copy-start.1 = (bf16[7168,160]{0,1:T(8,128)(2,1)S(1)}, bf16[7168,160]{0,1:T(8,128)(2,1)}, u32[]{:S(2)}) copy-start(bf16[7168,160]{0,1:T(8,128)(2,1)} %param.13) | copy-start | bytes 6881284
  53.4 4.4 %collective-permute-start.4 = (bf16[256,4480]{1,0:T(8,128)(2,1)S(1)}, bf16[256,4480]{1,0:T(8,128)(2,1)S(1)}, u32[]{:S(2)}, u32[]{:S(2)}) collective-permute-start(bf16[256,4480]{1,0:T(8,128)(2,1)S(1)} %bitcast.20), channel_id=1, source_target_pairs={{0,1},{1,0},{2,3},{3,2},{4,5},{5,4},{6,7},{7,6},{8,9},{9,8},{10,11... | collective-permute-start | bytes 6881288 | tf_op jit(solution)/shard_map/ppermute | solution.py:321
  53.4 2.2 %copy-start.4 = (bf16[4,1024,512]{2,1,0:T(8,128)(2,1)S(1)}, bf16[4,1024,512]{2,1,0:T(8,128)(2,1)}, u32[]{:S(2)}) copy-start(bf16[4,1024,512]{2,1,0:T(8,128)(2,1)} %param.16) | copy-start | bytes 12582916
  54.9 2.9 %copy-start.2 = (bf16[160,7168]{1,0:T(8,128)(2,1)S(1)}, bf16[160,7168]{1,0:T(8,128)(2,1)}, u32[]{:S(2)}) copy-start(bf16[160,7168]{1,0:T(8,128)(2,1)} %w_down.1) | copy-start | bytes 6881284
  59.6 1.5 %collective-permute-start.5 = (bf16[320,160]{1,0:T(8,128)(2,1)S(1)}, bf16[320,160]{1,0:T(8,128)(2,1)S(1)}, u32[]{:S(2)}, u32[]{:S(2)}) collective-permute-start(bf16[320,160]{1,0:T(8,128)(2,1)S(1)} %get-tuple-element.32.hidden), channel_id=1, source_target_pairs={{0,1},{1,0},{2,3},{3,2},{4,5},{5,4},{6,7},{7,6},{8,9},{9,8},{10,11... | collective-permute-start | bytes 307208 | tf_op jit(solution)/shard_map/ppermute | solution.py:347

commit v13 on v12

--- a/solution.py
+++ b/solution.py
@@ -303,7 +303,7 @@
 
     payload, queries = lax.optimization_barrier((payload, queries))
     weights, denominator = attention_weights(queries, cache, lengths)
-    other_down = lax.ppermute(lax.optimization_barrier((payload, w_down))[1], "c", SWAP)
+    other_down = lax.ppermute(w_down, "c", SWAP)
     blocks[0], weights, denominator, other_down = lax.optimization_barrier(
         (payload, weights, denominator, other_down)
     )

time: 118 us -> 118 us (level)
  transfers between devices with their start and end apart: 6 -> 6, of which waited for: 3 -> 3; matrix products, arithmetic and copies ran while one was open for 4% -> 4% of each run, Pallas kernels for 1% -> 3%
where the time goes in v13:
time: 118 us; the launch traced here: 117 us
  blocking collectives  90.5 us (77%)
  Pallas kernels  8.59 us (7%)
  starting transfers between devices  7.82 us (7%)
  waiting for transfers between devices  3.43 us (3%)
  matrix products  3.14 us (3%)
  local copies, waits for them, and re-layouts  1.47 us (1%)
  other arithmetic  1.42 us (1%)
    all_to_all x1, blocking collectives, shards(): lax.all_to_all(packed.reshape(PLANE, BLOCK, width), PLANE_AXES, 0, 0, til...  37.7 us
    all_to_all x1, blocking collectives, shards(): lax.all_to_all(summed.reshape(PLANE, BLOCK, width), PLANE_AXES, 0, 0, til...  33.9 us
    all_to_all x1, blocking collectives, shards(): parts = lax.all_to_all(parts, ('zh', 'zl'), 0, 0, tiled=True)  18.9 us
    pallas_call x4, Pallas kernels, call(): pl.pallas_call(kernel, out_shape=out_shape, in_specs=[pl.BlockSpec(memory...  4.69 us
    ppermute x2, starting transfers between devices, z_send(): return lax.ppermute(value, ('zl', 'zh'), z_pairs(step))  3.93 us
    ppermute x1, starting transfers between devices, z_send_apart(): return lax.ppermute(value, ('zl', 'zh', 'c'), both[0] + both[1])  3.57 us
    sub x1, matrix products, attention_weights(): weights = jnp.where(live[:, None, :], jnp.exp(scores - largest), 0.0)  2.67 us
  transfers between devices with their start and end apart: 6, of which 3 were waited for; matrix products, arithmetic and copies ran while one was open for 4% of the time, Pallas kernels for 3%

profile of v13, /device:TPU:32, one launch (start us, length us, event | category | flops | bytes accessed | tf_op | source)
XLA Modules:
  0.0 117.1 jit_solution(6559102466424790457)
XLA Ops:
  0.6 0.1 collective-permute-start
  0.7 2.1 %shard_map.104.refs_0_ = bf16[16,3712]{1,0:T(8,128)(2,1)} custom-call(bf16[16,7168]{1,0:T(8,128)(2,1)} %x_far.1, s32[2,16]{1,0:T(2,128)} %bitcast.31, f32[8,7168]{1,0:T(8,128)} %bitcast.29), custom_call_target="tpu_custom_call" | custom-call | tf_op jit(solution)/shard_map/pallas_call | solution.py:289
  2.9 2.0 %collective-permute-start.3 = (bf16[16,3712]{1,0:T(8,128)(2,1)}, bf16[16,3712]{1,0:T(8,128)(2,1)S(1)}, u32[]{:S(2)}, u32[]{:S(2)}) collective-permute-start(bf16[16,3712]{1,0:T(8,128)(2,1)} %shard_map.104.refs_0_), channel_id=1, source_target_pairs={{0,4},{4,8},{8,12},{12,2},{2,6},{6,10},{10,14},{14,0},{1,5},{5,9},... | collective-permute-start | bytes 356360 | tf_op jit(solution)/shard_map/ppermute | solution.py:39
  4.9 3.6 %collective-permute-start.2 = (bf16[16,3712]{1,0:T(8,128)(2,1)}, bf16[16,3712]{1,0:T(8,128)(2,1)S(1)}, u32[]{:S(2)}, u32[]{:S(2)}) collective-permute-start(bf16[16,3712]{1,0:T(8,128)(2,1)} %shard_map.104.refs_0_), channel_id=1, source_target_pairs={{0,10},{4,14},{8,0},{12,4},{2,8},{6,12},{10,2},{14,6},{1,9},{5,13}... | collective-permute-start | bytes 356360 | tf_op jit(solution)/shard_map/ppermute | solution.py:44
  8.4 1.9 %collective-permute-start.1 = (bf16[16,3712]{1,0:T(8,128)(2,1)}, bf16[16,3712]{1,0:T(8,128)(2,1)S(1)}, u32[]{:S(2)}, u32[]{:S(2)}) collective-permute-start(bf16[16,3712]{1,0:T(8,128)(2,1)} %shard_map.104.refs_0_), channel_id=1, source_target_pairs={{0,14},{4,0},{8,4},{12,8},{2,12},{6,2},{10,6},{14,10},{1,15},{5,1}... | collective-permute-start | bytes 356360 | tf_op jit(solution)/shard_map/ppermute | solution.py:39
  10.4 0.7 iota_compare_fusion
  11.1 0.0 copy-start.3
  11.1 2.7 %fusion.17 = (f32[4,64]{1,0:T(4,128)S(1)}, bf16[4,64,1024]{2,1,0:T(8,128)(2,1)S(1)}) fusion(pred[4,1024]{1,0:T(4,128)(4,1)S(1)} %iota_compare_fusion, bf16[4,1024,512]{2,1,0:T(8,128)(2,1)} %param.16, bf16[1,4,64,256]{3,1,2,0:T(4,128)(2,1)} %bitcast.32), kind=kOutput, calls=%fused_computation.15 | convolution fusion | flops 135791616 | bytes 2761728 | tf_op jit(solution)/shard_map/sub | solution.py:268
  13.8 0.0 collective-permute-done.other_down
  13.8 0.0 collective-permute-done.3.refs_3_
  13.8 0.0 collective-permute-done.2.refs_2_
  13.8 1.1 collective-permute-done.1.refs_1_
  15.0 0.0 copy-done.3
  15.0 0.7 shard_map.105
  15.7 0.0 copy-start
  15.7 0.0 copy-start.1
  15.7 37.7 %all_to_all.15 = bf16[16,16,4480]{2,1,0:T(8,128)(2,1)S(1)} all-to-all(bf16[16,16,4480]{2,1,0:T(8,128)(2,1)S(1)} %bitcast.28), channel_id=1, replica_groups=mesh['y'=4,'xh'=2,'xl'=2,'zl'=4,'zh'=2,'c'=2] {'y','xl','xh'}, dimensions={0} | all-to-all | bytes 4587520 | tf_op jit(solution)/shard_map/all_to_all | solution.py:318
  53.4 0.0 collective-permute-start.4
  53.4 0.0 copy-done
  53.4 0.0 copy-done.1
  53.4 0.0 copy-start.4
  53.4 1.5 %shard_map.106 = (f32[320,160]{1,0:T(8,128)S(1)}, f32[320,160]{1,0:T(8,128)S(1)}) custom-call(bf16[256,4480]{1,0:T(8,128)(2,1)S(1)} %bitcast.21, bf16[160,7168]{1,0:T(8,128)(2,1)S(1)} %bitcast.24, bf16[160,7168]{1,0:T(8,128)(2,1)S(1)} %bitcast.26), custom_call_target="tpu_custom_call" | custom-call | tf_op jit(solution)/shard_map/pallas_call | solution.py:83
  54.9 0.0 copy-start.2
  54.9 0.7 copy-done.4
  55.6 0.5 fusion.16
  56.1 0.8 copy.12
  56.8 1.0 collective-permute-done.4.block
  57.8 0.0 copy-done.2
  57.9 1.8 %shard_map.107 = (bf16[320,160]{1,0:T(8,128)(2,1)S(1)}, bf16[2,320,1792]{2,1,0:T(8,128)(2,1)S(1)}) custom-call(bf16[256,4480]{1,0:T(8,128)(2,1)S(1)} %collective-permute-done.4.block, bf16[160,7168]{1,0:T(8,128)(2,1)S(1)} %bitcast.25, bf16[160,7168]{1,0:T(8,128)(2,1)S(1)} %bitcast.27, f32[320,160]{1,0:T(8,128)S(1)} %get-tuple-element.27.gate_in, ...), custom_call_target="tpu_custom_call" | custom-call | tf_op jit(solution)/shard_map/pallas_call | solution.py:333
  59.6 0.2 collective-permute-start.5
  59.8 1.3 %collective-permute-done.5.other_hidden = bf16[320,160]{1,0:T(8,128)(2,1)S(1)} collective-permute-done((bf16[320,160]{1,0:T(8,128)(2,1)S(1)}, bf16[320,160]{1,0:T(8,128)(2,1)S(1)}, u32[]{:S(2)}, u32[]{:S(2)}) %collective-permute-start.5) | collective-permute-done | bytes 102432 | tf_op jit(solution)/shard_map/ppermute | solution.py:347
  61.1 1.6 %shard_map.108 = bf16[256,4480]{1,0:T(8,128)(2,1)S(1)} custom-call(bf16[320,160]{1,0:T(8,128)(2,1)S(1)} %get-tuple-element.30.hidden, bf16[320,160]{1,0:T(8,128)(2,1)S(1)} %collective-permute-done.5.other_hidden, bf16[2,320,1792]{2,1,0:T(8,128)(2,1)S(1)} %get-tuple-element.31.weights), custom_call_target="tpu_custom_call" | custom-call | tf_op jit(solution)/shard_map/pallas_call | solution.py:83
  62.7 33.9 %all_to_all.16 = bf16[16,16,4480]{2,1,0:T(8,128)(2,1)S(1)} all-to-all(bf16[16,16,4480]{2,1,0:T(8,128)(2,1)S(1)} %bitcast.22), channel_id=1, replica_groups=mesh['y'=4,'xh'=2,'xl'=2,'zl'=4,'zh'=2,'c'=2] {'y','xl','xh'}, dimensions={0} | all-to-all | bytes 4587520 | tf_op jit(solution)/shard_map/all_to_all | solution.py:349
  96.6 0.9 shard_map.109
  97.5 18.9 %all_to_all.17 = bf16[8,16,1792]{2,1,0:T(8,128)(2,1)S(1)} all-to-all(bf16[8,16,1792]{2,1,0:T(8,128)(2,1)S(1)} %shard_map.109), channel_id=1, replica_groups=mesh['y'=4,'xh'=2,'xl'=2,'zl'=4,'zh'=2,'c'=2] {'zh','zl'}, dimensions={0} | all-to-all | bytes 917504 | tf_op jit(solution)/shard_map/all_to_all | solution.py:358
  116.4 0.7 reduce_sum.22
Async XLA Ops:
  0.6 13.2 %collective-permute-start = (bf16[160,7168]{1,0:T(8,128)(2,1)}, bf16[160,7168]{1,0:T(8,128)(2,1)S(1)}, u32[]{:S(2)}, u32[]{:S(2)}) collective-permute-start(bf16[160,7168]{1,0:T(8,128)(2,1)} %w_down.1), channel_id=1, source_target_pairs={{0,1},{1,0},{2,3},{3,2},{4,5},{5,4},{6,7},{7,6},{8,9},{9,8},{10,11... | collective-permute-start | bytes 6881288 | tf_op jit(solution)/shard_map/ppermute | solution.py:306
  2.9 10.9 %collective-permute-start.3 = (bf16[16,3712]{1,0:T(8,128)(2,1)}, bf16[16,3712]{1,0:T(8,128)(2,1)S(1)}, u32[]{:S(2)}, u32[]{:S(2)}) collective-permute-start(bf16[16,3712]{1,0:T(8,128)(2,1)} %shard_map.104.refs_0_), channel_id=1, source_target_pairs={{0,4},{4,8},{8,12},{12,2},{2,6},{6,10},{10,14},{14,0},{1,5},{5,9},... | collective-permute-start | bytes 356360 | tf_op jit(solution)/shard_map/ppermute | solution.py:39
  4.9 9.0 %collective-permute-start.2 = (bf16[16,3712]{1,0:T(8,128)(2,1)}, bf16[16,3712]{1,0:T(8,128)(2,1)S(1)}, u32[]{:S(2)}, u32[]{:S(2)}) collective-permute-start(bf16[16,3712]{1,0:T(8,128)(2,1)} %shard_map.104.refs_0_), channel_id=1, source_target_pairs={{0,10},{4,14},{8,0},{12,4},{2,8},{6,12},{10,2},{14,6},{1,9},{5,13}... | collective-permute-start | bytes 356360 | tf_op jit(solution)/shard_map/ppermute | solution.py:44
  8.4 6.5 %collective-permute-start.1 = (bf16[16,3712]{1,0:T(8,128)(2,1)}, bf16[16,3712]{1,0:T(8,128)(2,1)S(1)}, u32[]{:S(2)}, u32[]{:S(2)}) collective-permute-start(bf16[16,3712]{1,0:T(8,128)(2,1)} %shard_map.104.refs_0_), channel_id=1, source_target_pairs={{0,14},{4,0},{8,4},{12,8},{2,12},{6,2},{10,6},{14,10},{1,15},{5,1}... | collective-permute-start | bytes 356360 | tf_op jit(solution)/shard_map/ppermute | solution.py:39
  11.1 3.8 %copy-start.3 = (bf16[16,3712]{1,0:T(8,128)(2,1)S(1)}, bf16[16,3712]{1,0:T(8,128)(2,1)}, u32[]{:S(2)}) copy-start(bf16[16,3712]{1,0:T(8,128)(2,1)} %shard_map.104.refs_0_) | copy-start | bytes 356356
  15.7 37.7 %copy-start = (bf16[7168,160]{0,1:T(8,128)(2,1)S(1)}, bf16[7168,160]{0,1:T(8,128)(2,1)}, u32[]{:S(2)}) copy-start(bf16[7168,160]{0,1:T(8,128)(2,1)} %param.12) | copy-start | bytes 6881284
  15.7 37.7 %copy-start.1 = (bf16[7168,160]{0,1:T(8,128)(2,1)S(1)}, bf16[7168,160]{0,1:T(8,128)(2,1)}, u32[]{:S(2)}) copy-start(bf16[7168,160]{0,1:T(8,128)(2,1)} %param.13) | copy-start | bytes 6881284
  53.4 4.4 %collective-permute-start.4 = (bf16[256,4480]{1,0:T(8,128)(2,1)S(1)}, bf16[256,4480]{1,0:T(8,128)(2,1)S(1)}, u32[]{:S(2)}, u32[]{:S(2)}) collective-permute-start(bf16[256,4480]{1,0:T(8,128)(2,1)S(1)} %bitcast.20), channel_id=1, source_target_pairs={{0,1},{1,0},{2,3},{3,2},{4,5},{5,4},{6,7},{7,6},{8,9},{9,8},{10,11... | collective-permute-start | bytes 6881288 | tf_op jit(solution)/shard_map/ppermute | solution.py:321
  53.4 2.2 %copy-start.4 = (bf16[4,1024,512]{2,1,0:T(8,128)(2,1)S(1)}, bf16[4,1024,512]{2,1,0:T(8,128)(2,1)}, u32[]{:S(2)}) copy-start(bf16[4,1024,512]{2,1,0:T(8,128)(2,1)} %param.16) | copy-start | bytes 12582916
  54.9 2.9 %copy-start.2 = (bf16[160,7168]{1,0:T(8,128)(2,1)S(1)}, bf16[160,7168]{1,0:T(8,128)(2,1)}, u32[]{:S(2)}) copy-start(bf16[160,7168]{1,0:T(8,128)(2,1)} %w_down.1) | copy-start | bytes 6881284
  59.6 1.5 %collective-permute-start.5 = (bf16[320,160]{1,0:T(8,128)(2,1)S(1)}, bf16[320,160]{1,0:T(8,128)(2,1)S(1)}, u32[]{:S(2)}, u32[]{:S(2)}) collective-permute-start(bf16[320,160]{1,0:T(8,128)(2,1)S(1)} %get-tuple-element.30.hidden), channel_id=1, source_target_pairs={{0,1},{1,0},{2,3},{3,2},{4,5},{5,4},{6,7},{7,6},{8,9},{9,8},{10,11... | collective-permute-start | bytes 307208 | tf_op jit(solution)/shard_map/ppermute | solution.py:347
